TPU v7x, 512 devices: a whole 4x4x16 slice. The times are simulated.
512 devices in a mesh: dp: 16 (over z_hi, x, core), seq: 32 (over y, z_lo).
Axes of the slice: x: 4, y: 4, z: 16 (z_hi: 2, z_lo: 8; z = z_hi * 8 + z_lo), core: 2. Of those that a mesh axis runs over, the one named last changes fastest.
Arguments:
- ssm_input: bfloat16 [65536, 1024], P(('dp', 'seq')), may hold values from -6 to 6
- gate_input: bfloat16 [65536, 1024], P(('dp', 'seq')), may hold values from -6 to 6
- b_proj: bfloat16 [65536, 128], P(('dp', 'seq')), may hold values from -6 to 6
- c_proj: bfloat16 [65536, 128], P(('dp', 'seq')), may hold values from -0.5 to 0.5
- dt_raw: float32 [65536, 16], P(('dp', 'seq')), may hold values from -5 to 5
- cotangent: bfloat16 [65536, 1024], P(('dp', 'seq')), may hold values from -6 to 6
- a_log: float32 [16], replicated, may hold values from -11 to -3
- dt_bias: float32 [16], replicated, may hold values from -2.5 to 2.5
- d_skip: float32 [16], replicated, may hold values from -3 to 3
- norm_gain: float32 [1024], replicated, may hold values from 0.5 to 1.5
- probe_a: float32 [16], replicated, may hold values from -3 to 3
- probe_dt: float32 [16], replicated, may hold values from -3 to 3
- probe_skip: float32 [16], replicated, may hold values from -3 to 3
- probe_gain: float32 [1024], replicated, may hold values from -3 to 3
Outputs:
- hvp_input: float32 [65536, 1024], P(('dp', 'seq'))
- hvp_a: float32 [16], replicated
- hvp_dt: float32 [16], replicated
- hvp_skip: float32 [16], replicated
- hvp_gain: float32 [1024], replicated
All inputs are finite; a program needn't handle non-finite values.
Results may differ from a plain program's by a relative error of at most 0.0004.
Values sent between devices are 32-bit elements; how exact they have to be, the bound alone decides.
No kernel may reach another device: no remote copies, remote signals or barrier semaphores. Data moves between devices by JAX's collectives and lax.ppermute only.
A program may use at most 128 MiB of HBM per device.

v0:
```python
import math

import jax
import jax.numpy as jnp
from jax import lax
from jax.sharding import PartitionSpec as P

PRECISE = lax.Precision.HIGHEST
EPS = 1e-05


def entering(x, axis, combine, identity, reverse):
    count, place = (lax.axis_size(axis), lax.axis_index(axis))
    everything = jax.tree.map(lambda part: lax.all_gather(part, axis), x)
    start = jax.tree.map(
        lambda part, zero: jnp.broadcast_to(jnp.asarray(zero, part.dtype), part.shape), x, identity
    )

    def lap(k, before):
        at = count - 1 - k if reverse else k
        reached = at > place if reverse else at < place
        new = combine(before, jax.tree.map(lambda part: part[at], everything))
        return jax.tree.map(lambda a, b: jnp.where(reached, a, b), new, before)

    return lax.fori_loop(0, count, lap, start)


def block_state(params, x_vals, b_vals, dt_vals):
    a_log, dt_bias = (params[0], params[1])
    steps_dt = jax.nn.softplus(dt_vals + dt_bias[None, :])
    rates = -jnp.exp(a_log)[None, :] * steps_dt
    cum_decay = jnp.cumsum(rates, axis=0)
    totals = cum_decay[-1]
    tail_weight = jnp.exp(totals[None, :] - cum_decay) * steps_dt
    n_heads = a_log.shape[0]
    x_heads = x_vals.reshape(x_vals.shape[0], n_heads, -1)
    states = jnp.einsum("sh,shp,sn->hpn", tail_weight, x_heads, b_vals, precision=PRECISE)
    return (totals, states, steps_dt, cum_decay)


def block_out(params, x_vals, z_vals, b_vals, c_vals, dt_vals, h_in):
    a_log, dt_bias, d_skip, norm_gain = params
    totals, states, steps_dt, cum_decay = block_state(params, x_vals, b_vals, dt_vals)
    n_rows = x_vals.shape[0]
    n_heads = a_log.shape[0]
    x_heads = x_vals.reshape(n_rows, n_heads, -1)
    scores = jnp.dot(c_vals, b_vals.T, precision=PRECISE)
    cum_heads = cum_decay.T
    gap_decay = cum_heads[:, :, None] - cum_heads[:, None, :]
    causal = (jnp.arange(n_rows)[:, None] >= jnp.arange(n_rows)[None, :])[None]
    decays = jnp.where(causal, jnp.exp(jnp.where(causal, gap_decay, 0.0)), 0.0)
    weights = decays * scores[None] * steps_dt.T[:, None, :]
    mixed_y = jnp.einsum("hts,shp->thp", weights, x_heads, precision=PRECISE)
    mixed_y = mixed_y + jnp.exp(cum_decay)[:, :, None] * jnp.einsum(
        "tn,hpn->thp", c_vals, h_in, precision=PRECISE
    )
    mixed_y = mixed_y + d_skip[None, :, None] * x_heads
    gated_y = mixed_y.reshape(n_rows, -1) * jax.nn.silu(z_vals)
    inv_rms = lax.rsqrt(jnp.mean(gated_y * gated_y, axis=1, keepdims=True) + EPS)
    normed = gated_y * inv_rms * norm_gain[None, :]
    h_out = jnp.exp(totals)[:, None, None] * h_in + states
    return (normed, h_out)


def joint_combine(earlier, later):
    g_early, s_early, dg_early, ds_early = earlier
    g_late, s_late, dg_late, ds_late = later
    growth = jnp.exp(g_late)[:, None, None]
    return (
        g_early + g_late,
        growth * s_early + s_late,
        dg_early + dg_late,
        growth * (ds_early + dg_late[:, None, None] * s_early) + ds_late,
    )


def per_device(
    ssm_input,
    gate_input,
    b_proj,
    c_proj,
    dt_raw,
    cotangent,
    a_log,
    dt_bias,
    d_skip,
    norm_gain,
    probe_a,
    probe_dt,
    probe_skip,
    probe_gain,
):
    params = (a_log, dt_bias, d_skip, norm_gain)
    probe = (probe_a, probe_dt, probe_skip, probe_gain)
    x_vals = ssm_input.astype(jnp.float32)
    z_vals = gate_input.astype(jnp.float32)
    b_vals = b_proj.astype(jnp.float32)
    c_vals = c_proj.astype(jnp.float32)
    cot_vals = cotangent.astype(jnp.float32)
    n_heads = a_log.shape[0]
    zero_g = jnp.zeros((n_heads,), jnp.float32)
    zero_h = jnp.zeros((n_heads, x_vals.shape[1] // n_heads, b_vals.shape[1]), jnp.float32)

    def state_fn(prm):
        totals, states, steps_dt, cum_decay = block_state(prm, x_vals, b_vals, dt_raw)
        return (totals, states)

    (totals, states), (d_totals, d_states) = jax.jvp(state_fn, (params,), (probe,))

    def local_loss(prm, x_arg, h_in):
        normed, h_out = block_out(prm, x_arg, z_vals, b_vals, c_vals, dt_raw, h_in)
        return jnp.sum(normed * cot_vals)

    def seed_fn(prm, h_in):
        return jax.grad(local_loss, argnums=2)(prm, x_vals, h_in)

    carried = entering(
        (totals, states, d_totals, d_states),
        "seq",
        joint_combine,
        (zero_g, zero_h, zero_g, zero_h),
        False,
    )
    h_in, d_h_in = (carried[1], carried[3])
    seeds, d_seeds = jax.jvp(seed_fn, (params, h_in), (probe, d_h_in))
    returned = entering(
        (totals, seeds, d_totals, d_seeds),
        "seq",
        joint_combine,
        (zero_g, zero_h, zero_g, zero_h),
        True,
    )
    adjoint, d_adjoint = (returned[1], returned[3])

    def full_loss(prm, x_arg, h_in_arg, adjoint_arg):
        normed, h_out = block_out(prm, x_arg, z_vals, b_vals, c_vals, dt_raw, h_in_arg)
        return jnp.sum(normed * cot_vals) + jnp.sum(adjoint_arg * h_out)

    def grad_fn(prm, h_in_arg, adjoint_arg):
        return jax.grad(full_loss, argnums=(0, 1))(prm, x_vals, h_in_arg, adjoint_arg)

    primal, tangent = jax.jvp(grad_fn, (params, h_in, adjoint), (probe, d_h_in, d_adjoint))
    param_tan, input_tan = tangent
    summed = lax.psum((param_tan[0], param_tan[1], param_tan[2], param_tan[3]), ("dp", "seq"))
    factor = 1.0 / math.sqrt(x_vals.shape[0] * lax.axis_size("dp") * lax.axis_size("seq"))
    return (
        input_tan,
        summed[0] * factor,
        summed[1] * factor,
        summed[2] * factor,
        summed[3] * factor,
    )


def solution(mesh):
    placed = (
        P(("dp", "seq"), None),
        P(("dp", "seq"), None),
        P(("dp", "seq"), None),
        P(("dp", "seq"), None),
        P(("dp", "seq"), None),
        P(("dp", "seq"), None),
        P(),
        P(),
        P(),
        P(),
        P(),
        P(),
        P(),
        P(),
    )
    return jax.shard_map(
        per_device,
        mesh=mesh,
        in_specs=placed,
        out_specs=(P(("dp", "seq"), None), P(), P(), P(), P()),
        check_vma=False,
    )
```

profile of v0, /device:TPU:1, one launch (start us, length us, event | category | flops | bytes accessed | tf_op | source)
XLA Modules:
  0.0 1792.9 jit_solution(13869056227657222695)
XLA Ops:
  15.8 113.2 %all-gather.5 = f32[32,1,16]{2,1,0:T(1,128)S(1)} all-gather(f32[1,1,16]{2,1,0:T(1,128)S(1)} %get-tuple-element.535), channel_id=1, replica_groups=mesh['dp'=16,'seq'=32] {'seq'}, dimensions={0}, use_global_device_ids=true | all-gather | bytes 2112 | tf_op jit(solution)/shard_map/all_gather | solution.py:14
  129.0 99.9 %all-gather.4 = f32[32,1,16]{2,1,0:T(1,128)S(1)} all-gather(f32[1,1,16]{2,1,0:T(1,128)S(1)} %get-tuple-element.537), channel_id=1, replica_groups=mesh['dp'=16,'seq'=32] {'seq'}, dimensions={0}, use_global_device_ids=true | all-gather | bytes 2112 | tf_op jit(solution)/shard_map/all_gather | solution.py:14
  230.5 2.5 convolution_bitcast_fusion.3
  233.0 166.8 %all-gather.13.cloned.1.call-done = f32[512,64,128]{2,1,0:T(8,128)} async-done(((f32[16,64,128]{2,1,0:T(8,128)}), f32[512,64,128]{2,1,0:T(8,128)}) %all-gather.13.cloned.1.call-update) | async-done | bytes 16777232 | tf_op jit(solution)/shard_map/all_gather | solution.py:14
  399.8 376.3 %all-gather.11.cloned.1.call-done = f32[512,64,128]{2,1,0:T(8,128)} async-done(((f32[16,64,128]{2,1,0:T(8,128)}), f32[512,64,128]{2,1,0:T(8,128)}) %all-gather.11.cloned.1.call-update) | async-done | bytes 16777232 | tf_op jit(solution)/shard_map/all_gather | solution.py:14
  776.1 51.6 %while.34 = (s32[]{:T(128)}, f32[16,64,128]{2,1,0:T(8,128)S(1)}, f32[16,64,128]{2,1,0:T(8,128)S(1)}, s32[]{:T(128)}, f32[32,16]{1,0:T(8,128)S(1)}, /*index=5*/f3...) while((s32[]{:T(128)}, f32[16,64,128]{2,1,0:T(8,128)S(1)}, ...), condition=%wide.region_4.6_spmd.clone, body=%wide.region_3.5_spmd.clone.sunk | while | flops 1310724 | bytes 3146241 | solution.py:25
  803.6 1.6 fusion.159
  829.0 3.7 add_add_fusion.5
  832.6 2.0 copy.227
  837.7 2.3 multiply_reduce_fusion.1
  840.1 3.6 multiply_reduce_fusion.3
  855.2 3.8 add_reduce_fusion
  859.9 2.0 add_reduce_fusion.2
  861.9 2.9 fusion.14
  864.8 356.5 %all-gather.17.cloned.1.call-done = f32[512,64,128]{2,1,0:T(8,128)} async-done(((f32[16,64,128]{2,1,0:T(8,128)}), f32[512,64,128]{2,1,0:T(8,128)}) %all-gather.17.cloned.1.call-update) | async-done | bytes 16777232 | tf_op jit(solution)/shard_map/all_gather | solution.py:14
  1221.3 375.7 %all-gather.15.cloned.1.call-done = f32[512,64,128]{2,1,0:T(8,128)} async-done(((f32[16,64,128]{2,1,0:T(8,128)}), f32[512,64,128]{2,1,0:T(8,128)}) %all-gather.15.cloned.1.call-update) | async-done | bytes 16777232 | tf_op jit(solution)/shard_map/all_gather | solution.py:14
  1597.0 73.3 %while.35 = (s32[]{:T(128)}, f32[16,64,128]{2,1,0:T(8,128)S(1)}, f32[16,64,128]{2,1,0:T(8,128)S(1)}, s32[]{:T(128)}, f32[32,16]{1,0:T(8,128)}, /*index=5*/f32[32...) while((s32[]{:T(128)}, f32[16,64,128]{2,1,0:T(8,128)S(1)}, ...), condition=%wide.region_15.17_spmd.clone, body=%wide.region_14.16_spmd.clone.sunk | while | flops 1310728 | bytes 3146303 | solution.py:25
  1606.8 1.6 fusion.161
  1609.0 1.6 fusion.161
  1611.3 1.6 fusion.161
  1613.6 1.6 fusion.161
  1629.7 1.6 fusion.161
  1677.8 102.5 %all-reduce.2 = (f32[16]{0:T(128)S(1)}, f32[16]{0:T(128)S(1)}, f32[16]{0:T(128)S(1)}, f32[1024]{0:T(1024)S(1)}) all-reduce(f32[16]{0:T(128)S(1)} %multiply_add_fusion.9, f32[16]{0:T(128)S(1)} %get-tuple-element.462, f32[16]{0:T(128)} %reduce_sum.286, f32[1024]{0:T(1024)} %get-tuple-element.457), channel_id=1, replica_groups=mesh['dp'=16,'seq'=32] {'dp','seq'}, use_global_device_ids=true, to_apply=%region_30.32 | all-reduce | flops 1072 | bytes 8576 | tf_op jit(solution)/shard_map/psum | solution.py:144
  1782.4 2.9 fusion.12
  (244 shorter events, 150.5 us)
Async XLA Ops:
  7.2 4.7 copy-start
  7.2 820.6 %copy-start.6 = (bf16[128,128]{1,0:T(8,128)(2,1)S(1)}, bf16[128,128]{1,0:T(8,128)(2,1)}, u32[]{:S(2)}) copy-start(bf16[128,128]{1,0:T(8,128)(2,1)} %param.23) | copy-start | bytes 98308
  7.2 392.6 %all-gather.13.cloned.1.call-start = ((), (), s32[]{:S(2)}) async-start(), calls=%async_computation.1 | async-start | bytes 17301504 | tf_op jit(solution)/shard_map/all_gather | solution.py:14
  7.9 1.5 copy-start.20
  7.9 1.5 copy-start.21
  11.9 764.2 %copy-start.16 = (f32[16,128]{1,0:T(8,128)}, f32[16,128]{1,0:T(8,128)S(1)}, u32[]{:S(2)}) copy-start(f32[16,128]{1,0:T(8,128)S(1)} %get-tuple-element.549) | copy-start | bytes 24580
  11.9 822.9 %copy-start.17 = (f32[16,128]{1,0:T(8,128)}, f32[16,128]{1,0:T(8,128)S(1)}, u32[]{:S(2)}) copy-start(f32[16,128]{1,0:T(8,128)S(1)} %get-tuple-element.552) | copy-start | bytes 24580
  13.1 763.0 %all-gather.11.cloned.1.call-start = ((), (), s32[]{:S(2)}) async-start(), calls=%async_computation | async-start | bytes 17301504 | tf_op jit(solution)/shard_map/all_gather | solution.py:14
  14.4 821.9 %copy-start.1 = (bf16[128,1024]{1,0:T(8,128)(2,1)S(1)}, bf16[128,1024]{1,0:T(8,128)(2,1)}, u32[]{:S(2)}) copy-start(bf16[128,1024]{1,0:T(8,128)(2,1)} %param.21) | copy-start | bytes 786436
  14.4 1206.9 %all-gather.17.cloned.1.call-start = ((), (), s32[]{:S(2)}) async-start(), calls=%async_computation.3 | async-start | bytes 17301504 | tf_op jit(solution)/shard_map/all_gather | solution.py:14
  15.6 822.1 %copy-start.18 = (f32[16,128]{1,0:T(8,128)}, f32[16,128]{1,0:T(8,128)S(1)}, u32[]{:S(2)}) copy-start(f32[16,128]{1,0:T(8,128)S(1)} %copy.218) | copy-start | bytes 24580
  15.7 812.9 %copy-start.19 = (f32[16,128]{1,0:T(8,128)}, f32[16,128]{1,0:T(8,128)S(1)}, u32[]{:S(2)}) copy-start(f32[16,128]{1,0:T(8,128)S(1)} %copy.230) | copy-start | bytes 24580
  229.0 608.7 %copy-start.14 = (pred[128,128]{1,0:T(8,128)(4,1)}, pred[128,128]{1,0:T(8,128)(4,1)S(1)}, u32[]{:S(2)}) copy-start(pred[128,128]{1,0:T(8,128)(4,1)S(1)} %iota_compare_fusion) | copy-start | bytes 49156
  230.5 607.2 %copy-start.12 = (f32[1024]{0:T(1024)S(1)}, f32[1024]{0:T(1024)}, u32[]{:S(2)}) copy-start(f32[1024]{0:T(1024)} %param.33) | copy-start | bytes 12292
  230.5 607.2 %copy-start.13 = (f32[1024]{0:T(1024)S(1)}, f32[1024]{0:T(1024)}, u32[]{:S(2)}) copy-start(f32[1024]{0:T(1024)} %param.29) | copy-start | bytes 12292
  233.0 607.1 %copy-start.2 = (bf16[128,1024]{1,0:T(8,128)(2,1)S(1)}, bf16[128,1024]{1,0:T(8,128)(2,1)}, u32[]{:S(2)}) copy-start(bf16[128,1024]{1,0:T(8,128)(2,1)} %param.20) | copy-start | bytes 786436
  827.7 0.8 copy-start.10
  827.8 0.8 copy-start.11
  828.5 4.1 copy-start.5
  847.4 749.5 %all-gather.15.cloned.1.call-start = ((), (), s32[]{:S(2)}) async-start(), calls=%async_computation.2 | async-start | bytes 17301504 | tf_op jit(solution)/shard_map/all_gather | solution.py:14
  848.9 13.1 copy-start.9
  848.9 13.1 copy-start.15
  852.8 817.5 %copy-start.3 = (f32[128,1024]{0,1:T(8,128)}, f32[128,1024]{0,1:T(8,128)S(1)}, u32[]{:S(2)}) copy-start(f32[128,1024]{0,1:T(8,128)S(1)} %copy.234) | copy-start | bytes 1572868
  855.2 816.3 %copy-start.7 = (f32[128,16]{0,1:T(8,128)S(1)}, f32[128,16]{0,1:T(8,128)}, u32[]{:S(2)}) copy-start(f32[128,16]{0,1:T(8,128)} %param.24) | copy-start | bytes 24580
  (2 other events, 1.5 us)
Sparse Core Ops, SparseCore 0:
  13.2 386.5 all-gather.12
  402.5 373.6 all-gather.10
  847.6 373.6 all-gather.16
  1223.2 373.6 all-gather.14
where the time goes:
time: 1800 us; the launch traced here: 1790 us
  waiting for transfers between devices  1280 us (71%)
  blocking collectives  316 us (18%)
  other arithmetic  123 us (7%)
  local copies, waits for them, and re-layouts  38.8 us (2%)
  matrix products  24 us (1%)
    all_gather x4, waiting for transfers between devices, entering(): everything = jax.tree.map(lambda part: lax.all_gather(part, axis), x)  1280 us
    all_gather x2, blocking collectives, entering(): everything = jax.tree.map(lambda part: lax.all_gather(part, axis), x)  213 us
    psum x1, blocking collectives, per_device(): lax.psum((param_tan[0], param_tan[1], param_tan[2], param_tan[3]), ('dp',...  102 us
    select_n x64, other arithmetic, lap(): return jax.tree.map(lambda a, b: jnp.where(reached, a, b), new, before)  100 us
  transfers between devices with their start and end apart: 4, of which 4 were waited for; matrix products, arithmetic and copies ran while one was open for 1% of the time, Pallas kernels for 0%

commit v1 on v0

v1 whole, which is shorter than its diff:
```python
import functools
import math

import jax
import jax.numpy as jnp
from jax import lax
from jax.experimental import pallas as pl
from jax.experimental.pallas import tpu as pltpu
from jax.sharding import Mesh, PartitionSpec as P

F32, BF16 = jnp.float32, jnp.bfloat16
EPS = 1e-05
T = 128
N = 128
HD = 64
HEADS = 16
CH = 1024
BLK = 4
HPD = HEADS // BLK
CPD = HPD * HD
ROWS = BLK * HPD
SEGS = 8
CPS = CPD // SEGS
PARAMS = 6
X_ROWS = CPD + N + HPD + PARAMS * HPD + 4
G_ROWS = 2 * CPD + T + 8
M_ROWS = 2 * CPS + 8
VMEM = 48 * 1024 * 1024

(K_C, K_DC, K_DT, K_DDT, K_W, K_DW, K_TAIL, K_SG, K_DSG, K_F0, K_F1, K_G, K_DG, K_F0T, K_F1T, K_D, K_DD) = range(17)
TABLE = 17


def split(a):
    hi = a.astype(BF16)
    return hi, (a - hi.astype(F32)).astype(BF16)


def mm(a, b):
    return lax.dot_general(a, b, (((1,), (0,)), ((), ())), preferred_element_type=F32)


def mmt(a, b):
    return lax.dot_general(a, b, (((1,), (1,)), ((), ())), preferred_element_type=F32)


def heads_rows(table, k, b):
    return jnp.concatenate(
        [jnp.broadcast_to(table[k, b * HPD + h : b * HPD + h + 1, :], (HD, T)) for h in range(HPD)], axis=0
    )


def pack_x_kernel(x_ref, b_ref, dt_ref, *rest):
    prm, o_ref = rest[:PARAMS], rest[PARAMS]
    for j in range(BLK):
        for i in range(CPD // 128):
            lo = j * CPD + i * 128
            o_ref[j, i * 128 : (i + 1) * 128, :] = x_ref[:, lo : lo + 128].astype(F32).T
        o_ref[j, CPD : CPD + N, :] = b_ref[...].astype(F32)
        at = CPD + N
        o_ref[j, at : at + HPD, :] = dt_ref[j * HPD : (j + 1) * HPD, :]
        at += HPD
        for k in range(PARAMS):
            for h in range(HPD):
                o_ref[j, at : at + 1, :] = jnp.full((1, T), prm[k][j * HPD + h], F32)
                at += 1
        o_ref[j, at : at + 4, :] = jnp.zeros((4, T), F32)


def pack_g_kernel(z_ref, cot_ref, c_ref, gain_ref, dgain_ref, o_ref):
    halves = CPD // 128
    for j in range(BLK):
        for n, ref in enumerate((z_ref, cot_ref)):
            for i in range(halves):
                lo = j * CPD + i * 128
                at = n * CPD + i * 128
                o_ref[j, at : at + 128, :] = ref[:, lo : lo + 128].astype(F32).T
        o_ref[j, 2 * CPD : 2 * CPD + T, :] = c_ref[...].astype(F32)
        at = 2 * CPD + T
        o_ref[j, at : at + halves, :] = gain_ref[j * halves : (j + 1) * halves, :]
        o_ref[j, at + halves : at + 2 * halves, :] = dgain_ref[j * halves : (j + 1) * halves, :]
        o_ref[j, at + 2 * halves : at + 8, :] = jnp.zeros((8 - 2 * halves, 128), F32)


def write_message(msg_ref, total, d_total, table):
    for j in range(SEGS):
        h = j * CPS // HD
        msg_ref[j, 0:CPS, :] = total[j * CPS : (j + 1) * CPS]
        msg_ref[j, CPS : 2 * CPS, :] = d_total[j * CPS : (j + 1) * CPS]
        g, dg = None, None
        for b in range(BLK):
            r = b * HPD + h
            g_b, dg_b = table[K_G, r : r + 1, :], table[K_DG, r : r + 1, :]
            g, dg = (g_b, dg_b) if g is None else (g + g_b, dg + dg_b)
        msg_ref[j, 2 * CPS : 2 * CPS + 1, :] = g
        msg_ref[j, 2 * CPS + 1 : 2 * CPS + 2, :] = dg
        msg_ref[j, 2 * CPS + 2 : M_ROWS, :] = jnp.zeros((M_ROWS - 2 * CPS - 2, T), F32)


def state_kernel(r_ref, table_ref, cols_ref, s_ref, msg_ref):
    at = CPD + N

    def gather(lo):
        return jnp.concatenate([r_ref[b, lo : lo + HPD, :] for b in range(BLK)], axis=0)

    raw = gather(at)
    a_log, dt_bias, d_skip, p_a, p_dt, p_skip = [gather(at + HPD * (1 + k)) for k in range(PARAMS)]
    pre = raw + dt_bias
    dt = jnp.maximum(pre, 0.0) + jnp.log1p(jnp.exp(-jnp.abs(pre)))
    sg = 1.0 / (1.0 + jnp.exp(-pre))
    dsg = sg * (1.0 - sg) * p_dt
    ddt = sg * p_dt
    a = -jnp.exp(a_log)
    da = a * p_a
    before = lax.broadcasted_iota(jnp.int32, (T, T), 0) <= lax.broadcasted_iota(jnp.int32, (T, T), 1)
    sums = lax.dot_general(
        jnp.concatenate([dt, sg, dsg], axis=0),
        jnp.where(before, 1.0, 0.0).astype(F32),
        (((1,), (0,)), ((), ())),
        precision=lax.Precision.HIGHEST,
        preferred_element_type=F32,
    )
    cum_dt, cum_sg, cum_dsg = sums[:ROWS], sums[ROWS : 2 * ROWS], sums[2 * ROWS :]
    c = a * cum_dt
    dc = da * cum_dt + a * p_dt * cum_sg
    f0 = a * cum_sg
    f1 = da * cum_sg + a * cum_dsg

    def last(v):
        return jnp.broadcast_to(v[:, T - 1 : T], (ROWS, T))

    g, dg = last(c), last(dc)
    tail = jnp.exp(g - c)
    w = tail * dt
    dw = tail * ((dg - dc) * dt + ddt)
    for k, v in (
        (K_C, c), (K_DC, dc), (K_DT, dt), (K_DDT, ddt), (K_W, w), (K_DW, dw), (K_TAIL, tail), (K_SG, sg),
        (K_DSG, dsg), (K_F0, f0), (K_F1, f1), (K_G, g), (K_DG, dg), (K_F0T, last(f0)), (K_F1T, last(f1)),
        (K_D, d_skip), (K_DD, p_skip),
    ):
        table_ref[k] = v
    cols_ref[...] = jnp.concatenate(
        [c, dc, dt, ddt, jnp.zeros((T - 4 * ROWS, T), F32)], axis=0
    ).T
    total = jnp.zeros((CPD, N), F32)
    d_total = jnp.zeros((CPD, N), F32)
    for b in range(BLK):
        xt = r_ref[b, 0:CPD, :]
        bmat = r_ref[b, CPD : CPD + N, :].astype(BF16)
        parts = split(xt * heads_rows(table_ref, K_W, b)) + split(xt * heads_rows(table_ref, K_DW, b))
        got = mm(jnp.concatenate(parts, axis=0), bmat)
        s = got[0:CPD] + got[CPD : 2 * CPD]
        ds = got[2 * CPD : 3 * CPD] + got[3 * CPD :]
        s_ref[b, 0] = s
        s_ref[b, 1] = ds
        eg = jnp.exp(heads_rows(table_ref, K_G, b))
        d_total = eg * (d_total + heads_rows(table_ref, K_DG, b) * total) + ds
        total = eg * total + s
    write_message(msg_ref, total, d_total, table_ref)


def scan_kernel(reverse, m_ref, o_ref):
    total = jnp.zeros((CPS, N), F32)
    d_total = jnp.zeros((CPS, N), F32)
    for i in range(SEGS - 1, -1, -1) if reverse else range(SEGS):
        o_ref[i, 0:CPS, :] = total
        o_ref[i, CPS : 2 * CPS, :] = d_total
        eg = jnp.exp(m_ref[i, 2 * CPS : 2 * CPS + 1, :])
        dg = m_ref[i, 2 * CPS + 1 : 2 * CPS + 2, :]
        d_total = eg * (d_total + dg * total) + m_ref[i, CPS : 2 * CPS, :]
        total = eg * total + m_ref[i, 0:CPS, :]


def gains(g_ref):
    at = 2 * CPD + T
    halves = CPD // 128
    out = []
    for n in range(2):
        rows = [g_ref[0, at + n * halves + i : at + n * halves + i + 1, :] for i in range(halves)]
        out.append(jnp.concatenate([jnp.broadcast_to(v, (T, 128)).T for v in rows], axis=0))
    return out


def silu(z):
    return z / (1.0 + jnp.exp(-z))


def decays(table, cols, r, scores, causal):
    gap = table[K_C, r : r + 1, :] - cols[:, r : r + 1]
    d_gap = table[K_DC, r : r + 1, :] - cols[:, ROWS + r : ROWS + r + 1]
    return jnp.where(causal, scores * jnp.exp(jnp.where(causal, gap, 0.0)), 0.0), d_gap


def causal_mask():
    return lax.broadcasted_iota(jnp.int32, (T, T), 0) <= lax.broadcasted_iota(jnp.int32, (T, T), 1)


def out_kernel(r_ref, g_ref, h_ref, table_ref, cols_ref, s_ref, y_ref, hb_ref, msg_ref):
    causal = causal_mask()
    gain, dgain = gains(g_ref)
    h = h_ref[:, 0:CPS, :].reshape(CPD, N)
    dh = h_ref[:, CPS : 2 * CPS, :].reshape(CPD, N)
    for b in range(BLK):
        xt = r_ref[b, 0:CPD, :]
        xb = xt.astype(BF16)
        bmat = r_ref[b, CPD : CPD + N, :].astype(BF16)
        cmat = g_ref[b, 2 * CPD : 2 * CPD + T, :].astype(BF16)
        hb_ref[b, 0] = h
        hb_ref[b, 1] = dh
        got = mmt(jnp.concatenate(split(h) + split(dh), axis=0), cmat)
        ch = got[0:CPD] + got[CPD : 2 * CPD]
        dch = got[2 * CPD : 3 * CPD] + got[3 * CPD :]
        scores = mmt(bmat, cmat)
        y_parts, dy_parts = [], []
        for i in range(HPD):
            r = b * HPD + i
            mat, d_gap = decays(table_ref, cols_ref, r, scores, causal)
            dt = cols_ref[:, 2 * ROWS + r : 2 * ROWS + r + 1]
            ddt = cols_ref[:, 3 * ROWS + r : 3 * ROWS + r + 1]
            w = mat * dt
            dw = mat * (d_gap * dt + ddt)
            w_hi, w_lo = split(jnp.concatenate([w, dw], axis=1))
            x_i = xb[i * HD : (i + 1) * HD]
            inner = mm(x_i, w_hi) + mm(x_i, w_lo)
            ec = jnp.exp(table_ref[K_C, r : r + 1, :])
            dc = table_ref[K_DC, r : r + 1, :]
            ch_i, dch_i = ch[i * HD : (i + 1) * HD], dch[i * HD : (i + 1) * HD]
            y_parts.append(inner[:, :T] + ec * ch_i)
            dy_parts.append(inner[:, T:] + ec * (dc * ch_i + dch_i))
        y_nd = jnp.concatenate(y_parts, axis=0)
        dy_nd = jnp.concatenate(dy_parts, axis=0)
        y_ref[0, b] = y_nd
        y_ref[1, b] = dy_nd
        s = silu(g_ref[b, 0:CPD, :])
        cot = g_ref[b, CPD : 2 * CPD, :]
        u = (y_nd + heads_rows(table_ref, K_D, b) * xt) * s
        du = (dy_nd + heads_rows(table_ref, K_DD, b) * xt) * s
        q, dq = gain * cot, dgain * cot
        for n, v in enumerate((u * u, u * q, u * du, du * q + u * dq)):
            row = jnp.sum(v, axis=0, keepdims=True)
            for j in range(BLK):
                msg_ref[j, n * BLK + b : n * BLK + b + 1, :] = row
        eg = jnp.exp(heads_rows(table_ref, K_G, b))
        dh = eg * (dh + heads_rows(table_ref, K_DG, b) * h) + s_ref[b, 1]
        h = eg * h + s_ref[b, 0]


def seed_kernel(r_ref, g_ref, n_ref, table_ref, y_ref, yb_ref, seed_ref, gain_ref, msg_ref):
    gain, dgain = gains(g_ref)
    sums = n_ref[0] + n_ref[1] + n_ref[2] + n_ref[3]
    acc = jnp.zeros((CPD, T), F32)
    adj = jnp.zeros((CPD, N), F32)
    d_adj = jnp.zeros((CPD, N), F32)
    for b in range(BLK - 1, -1, -1):
        xt = r_ref[b, 0:CPD, :]
        cmat = g_ref[b, 2 * CPD : 2 * CPD + T, :].astype(BF16)
        s = silu(g_ref[b, 0:CPD, :])
        cot = g_ref[b, CPD : 2 * CPD, :]
        u = (y_ref[0, b] + heads_rows(table_ref, K_D, b) * xt) * s
        du = (y_ref[1, b] + heads_rows(table_ref, K_DD, b) * xt) * s
        square, m, p, dm = [sums[n * BLK + b : n * BLK + b + 1, :] for n in range(4)]
        mean = square * (1.0 / CH) + EPS
        inv = lax.rsqrt(mean)
        inv = inv * (1.5 - 0.5 * mean * inv * inv)
        cube = inv * inv * inv
        dinv = -cube * p * (1.0 / CH)
        k2 = cube * m * (1.0 / CH)
        k3 = (3.0 * inv * inv * dinv * m + cube * dm) * (1.0 / CH)
        q, dq = gain * cot, dgain * cot
        yb = s * (inv * q - k2 * u)
        dyb = s * (dinv * q + inv * dq - k3 * u - k2 * du)
        yb_ref[0, b] = yb
        yb_ref[1, b] = dyb
        acc = acc + cot * (du * inv + u * dinv)
        ec = jnp.exp(heads_rows(table_ref, K_C, b))
        e0 = ec * yb
        e1 = ec * (heads_rows(table_ref, K_DC, b) * yb + dyb)
        got = mm(jnp.concatenate(split(e0) + split(e1), axis=0), cmat)
        seed = got[0:CPD] + got[CPD : 2 * CPD]
        d_seed = got[2 * CPD : 3 * CPD] + got[3 * CPD :]
        seed_ref[b, 0] = seed
        seed_ref[b, 1] = d_seed
        eg = jnp.exp(heads_rows(table_ref, K_G, b))
        d_adj = eg * (d_adj + heads_rows(table_ref, K_DG, b) * adj) + d_seed
        adj = eg * adj + seed
    for i in range(CPD // 128):
        gain_ref[i : i + 1, :] = jnp.sum(acc[i * 128 : (i + 1) * 128].T, axis=0, keepdims=True)
    write_message(msg_ref, adj, d_adj, table_ref)


def head_sum(v):
    return jnp.sum(v, axis=0, keepdims=True)


def input_kernel(r_ref, g_ref, l_ref, table_ref, cols_ref, y_ref, yb_ref, hb_ref, seed_ref, gain_ref, o_ref, part_ref):
    causal = causal_mask()
    adj = l_ref[:, 0:CPS, :].reshape(CPD, N)
    d_adj = l_ref[:, CPS : 2 * CPS, :].reshape(CPD, N)
    acc_a = [jnp.zeros((1, T), F32) for _ in range(HPD)]
    acc_dt = [jnp.zeros((1, T), F32) for _ in range(HPD)]
    acc_skip = [jnp.zeros((1, T), F32) for _ in range(HPD)]
    for b in range(BLK - 1, -1, -1):
        bmat = r_ref[b, CPD : CPD + N, :].astype(BF16)
        cmat = g_ref[b, 0:T, :].astype(BF16)
        got = mmt(jnp.concatenate(split(adj) + split(d_adj), axis=0), bmat)
        bl = got[0:CPD] + got[CPD : 2 * CPD]
        dbl = got[2 * CPD : 3 * CPD] + got[3 * CPD :]
        scores = mmt(bmat, cmat)
        out_parts = []
        for i in range(HPD):
            r = b * HPD + i
            rows = slice(i * HD, (i + 1) * HD)

            def row(k):
                return table_ref[k, r : r + 1, :]

            mat, d_gap = decays(table_ref, cols_ref, r, scores, causal)
            l_hi, l_lo = split(mat)
            n_hi, n_lo = split(mat * d_gap)
            yb, dyb = yb_ref[0, b, rows, :], yb_ref[1, b, rows, :]
            y_hi, y_lo = split(yb)
            dy_hi, dy_lo = split(dyb)
            got = mmt(jnp.concatenate([y_hi, dy_hi, y_lo, dy_lo], axis=0), l_hi)
            low = mmt(jnp.concatenate([y_hi, dy_hi], axis=0), l_lo)
            both = got[: 2 * HD] + got[2 * HD :] + low
            gap_part = mmt(jnp.concatenate([y_hi, y_lo], axis=0), n_hi)
            gap_part = gap_part[:HD] + gap_part[HD:] + mmt(y_hi, n_lo)
            xt = r_ref[b, rows, :]
            bl_i, dbl_i = bl[rows], dbl[rows]
            tail, dt, ddt, dc, dg = row(K_TAIL), row(K_DT), row(K_DDT), row(K_DC), row(K_DG)
            k = both[:HD] + tail * bl_i
            dk = both[HD:] + gap_part + tail * ((dg - dc) * bl_i + dbl_i)
            out_parts.append(ddt * k + dt * dk + row(K_DD) * yb + row(K_D) * dyb)
            y_nd, dy_nd = y_ref[0, b, rows, :], y_ref[1, b, rows, :]
            xk, dxk = head_sum(xt * k), head_sum(xt * dk)
            e0 = head_sum(yb * y_nd) - dt * xk
            e1 = head_sum(dyb * y_nd + yb * dy_nd) - ddt * xk - dt * dxk
            xbl, dxbl = head_sum(xt * bl_i), head_sum(xt * dbl_i)
            h, dh = hb_ref[b, 0, rows, :], hb_ref[b, 1, rows, :]
            lam, d_lam = adj[rows], d_adj[rows]
            eg = jnp.exp(row(K_G))
            hl = eg * head_sum(lam * h)
            dhl = eg * head_sum(d_lam * h + lam * dh)
            g0 = hl + row(K_W) * xbl
            g1 = dg * hl + dhl + row(K_DW) * xbl + row(K_W) * dxbl
            acc_a[i] = acc_a[i] + dc * e0 + row(K_C) * e1 + dg * g0 + row(K_G) * g1
            acc_dt[i] = (
                acc_dt[i] + row(K_DSG) * xk + row(K_SG) * dxk + row(K_F1) * e0 + row(K_F0) * e1
                + row(K_F1T) * g0 + row(K_F0T) * g1
            )
            acc_skip[i] = acc_skip[i] + head_sum(xt * dyb)
        out = jnp.concatenate(out_parts, axis=0)
        for i in range(CPD // 128):
            o_ref[b, i * 128 : (i + 1) * 128, :] = out[i * 128 : (i + 1) * 128].T
        if b:
            eg = jnp.exp(heads_rows(table_ref, K_G, b))
            d_adj = eg * (d_adj + heads_rows(table_ref, K_DG, b) * adj) + seed_ref[b, 1]
            adj = eg * adj + seed_ref[b, 0]
    for i in range(HPD):
        part_ref[i : i + 1, :] = acc_a[i]
        part_ref[HPD + i : HPD + i + 1, :] = acc_dt[i]
        part_ref[2 * HPD + i : 2 * HPD + i + 1, :] = acc_skip[i]
    part_ref[3 * HPD : 3 * HPD + 2, :] = gain_ref[...]
    part_ref[3 * HPD + 2 :, :] = jnp.zeros((2, T), F32)


def call(kernel, name, outs, in_specs=None):
    def shape(dims):
        return jax.ShapeDtypeStruct(dims, F32)

    many = isinstance(outs, list)
    spec = pl.BlockSpec(memory_space=pltpu.VMEM)

    def run(*args):
        return pl.pallas_call(
            kernel,
            name=name,
            out_shape=[shape(o) for o in outs] if many else shape(outs),
            out_specs=[spec] * len(outs) if many else spec,
            in_specs=in_specs or [spec] * len(args),
            compiler_params=pltpu.CompilerParams(vmem_limit_bytes=VMEM),
        )(*args)

    return run


def per_device(
    ssm_input,
    gate_input,
    b_proj,
    c_proj,
    dt_raw,
    cotangent,
    a_log,
    dt_bias,
    d_skip,
    norm_gain,
    probe_a,
    probe_dt,
    probe_skip,
    probe_gain,
):
    vm, sm = pl.BlockSpec(memory_space=pltpu.VMEM), pl.BlockSpec(memory_space=pltpu.SMEM)

    def exchange(v, axes):
        return lax.all_to_all(v, axes, 0, 0)

    group, segs = "zl", ("y", "zh")
    packed = call(pack_x_kernel, "pack_x", (BLK, X_ROWS, T), [vm] * 3 + [sm] * PARAMS)(
        ssm_input, b_proj, dt_raw.T, a_log, dt_bias, d_skip, probe_a, probe_dt, probe_skip
    )
    r = exchange(packed, group)
    packed_g = call(pack_g_kernel, "pack_g", (BLK, G_ROWS, T))(
        gate_input, cotangent, c_proj, norm_gain.reshape(8, 128), probe_gain.reshape(8, 128)
    )
    g = exchange(packed_g, group)
    table, cols, s, msg = call(
        state_kernel,
        "state",
        [(TABLE, ROWS, T), (T, T), (BLK, 2, CPD, N), (SEGS, M_ROWS, N)],
    )(r)
    before = call(functools.partial(scan_kernel, False), "scan_up", (SEGS, 2 * CPS, N))(exchange(msg, segs))
    h_in = exchange(before, segs)
    y, h_blocks, norms = call(
        out_kernel, "mix", [(2, BLK, CPD, T), (BLK, 2, CPD, N), (BLK, 4 * BLK, T)]
    )(r, g, h_in, table, cols, s)
    norms = exchange(norms, group)
    y_bar, seeds, d_gain, msg = call(
        seed_kernel,
        "seeds",
        [(2, BLK, CPD, T), (BLK, 2, CPD, N), (2, 128), (SEGS, M_ROWS, N)],
    )(r, g, norms, table, y)
    after = call(functools.partial(scan_kernel, True), "scan_down", (SEGS, 2 * CPS, N))(exchange(msg, segs))
    adj = exchange(after, segs)
    c_all = g[:, 2 * CPD : 2 * CPD + T, :]
    out, part = call(input_kernel, "input_grad", [(BLK, CPD, 128), (4 * HPD, T)])(
        r, c_all, adj, table, cols, y, y_bar, h_blocks, seeds, d_gain
    )
    out = exchange(out, group).reshape(CH // 128, T, 128)
    hvp_input = jnp.transpose(out, (1, 0, 2)).reshape(T, CH)

    devices = lax.axis_size("dp")
    part = jnp.sum(exchange(jnp.broadcast_to(part[None], (devices,) + part.shape), "dp"), axis=0)
    whole = SEGS * BLK
    part = exchange(jnp.broadcast_to(part[None], (whole,) + part.shape), ("y", "zh", "zl"))
    part = jnp.sum(part.reshape(SEGS, BLK, 4 * HPD, T), axis=0)
    factor = 1.0 / math.sqrt(T * devices * whole)
    heads = jnp.sum(part[:, : 3 * HPD, :], axis=2).reshape(BLK, 3, HPD) * factor
    hvp_gain = part[:, 3 * HPD : 3 * HPD + 2, :].reshape(CH) * factor
    return (
        hvp_input,
        heads[:, 0].reshape(HEADS),
        heads[:, 1].reshape(HEADS),
        heads[:, 2].reshape(HEADS),
        hvp_gain,
    )


def solution(mesh):
    fine = Mesh(mesh.devices.reshape(mesh.devices.shape[0], 4, 2, 4), ("dp", "y", "zh", "zl"))
    tokens = P(("dp", "y", "zh", "zl"), None)
    return jax.shard_map(
        per_device,
        mesh=fine,
        in_specs=(tokens,) * 6 + (P(),) * 8,
        out_specs=(tokens, P(), P(), P(), P()),
        check_vma=False,
    )
```

time: 1800 us -> 257 us (0.14)
  waiting for transfers between devices: 1280 us -> 77.1 us
  blocking collectives: 316 us -> 125 us
  other arithmetic: 123 us -> 0.73 us
  matrix products: 24 us -> 0 us
  starting transfers between devices: 0.35 us -> 22.6 us
  local copies, waits for them, and re-layouts: 38.8 us -> 18.1 us
    all_gather x4 -> x0, waiting for transfers between devices: 1280 us -> none  [entering(): everything = jax.tree.map(lambda part: lax.all_gather(part, axis), x)]
    all_gather x2 -> x0, blocking collectives: 213 us -> none  [entering(): everything = jax.tree.map(lambda part: lax.all_gather(part, axis), x)]
    all_to_all x0 -> x6, blocking collectives: none -> 125 us  [exchange(): return lax.all_to_all(v, axes, 0, 0)]
    psum x1 -> x0, blocking collectives: 102 us -> none  [per_device(): lax.psum((param_tan[0], param_tan[1], param_tan[2], param_tan[3]), ('dp',...]
    select_n x64 -> x0, other arithmetic: 100 us -> none  [lap(): return jax.tree.map(lambda a, b: jnp.where(reached, a, b), new, before)]
    all_to_all x0 -> x4, waiting for transfers between devices: none -> 77.1 us  [exchange(): return lax.all_to_all(v, axes, 0, 0)]
    dot_general x15 -> x0, matrix products: 24 us -> none  [the longest x6 16.8 us: block_out(): mixed_y = jnp.einsum('hts,shp->thp', weights, x_heads, precision=PRECISE)]
    exp x65 -> x0, local copies, waits for them, and re-layouts: 22.6 us -> none  [the longest x64 22.5 us: joint_combine(): growth = jnp.exp(g_late)[:, None, None]]
  transfers between devices with their start and end apart: 4 -> 4, of which waited for: 4 -> 4; matrix products, arithmetic and copies ran while one was open for 1% -> 1% of each run, Pallas kernels for 0% -> 1%
where the time goes in v1:
time: 257 us; the launch traced here: 255 us
  blocking collectives  125 us (49%)
  waiting for transfers between devices  77.1 us (30%)
  starting transfers between devices  22.6 us (9%)
  local copies, waits for them, and re-layouts  18.1 us (7%)
  Pallas kernels  11.3 us (4%)
    all_to_all x6, blocking collectives, exchange(): return lax.all_to_all(v, axes, 0, 0)  125 us
    all_to_all x4, waiting for transfers between devices, exchange(): return lax.all_to_all(v, axes, 0, 0)  77.1 us
    all_to_all x4, starting transfers between devices, exchange(): return lax.all_to_all(v, axes, 0, 0)  22.6 us
    unnamed x46, local copies, waits for them, and re-layouts  14.6 us
    pallas_call x8, Pallas kernels, run(): pl.pallas_call(kernel, name=name, out_shape=[shape(o) for o in outs] if m...  11.3 us
  transfers between devices with their start and end apart: 4, of which 4 were waited for; matrix products, arithmetic and copies ran while one was open for 1% of the time, Pallas kernels for 1%

profile of v1, /device:TPU:1, one launch (start us, length us, event | category | flops | bytes accessed | tf_op | source)
XLA Modules:
  0.0 255.5 jit_solution(6509151954015940446)
XLA Ops:
  7.8 26.6 %all_to_all.50.r_ref = f32[4,416,128]{2,1,0:T(8,128)S(1)} all-to-all(f32[4,416,128]{2,1,0:T(8,128)S(1)} %pack_x.1), channel_id=1, replica_groups=mesh['dp'=16,'y'=4,'zh'=2,'zl'=4] {'zl'}, dimensions={0} | all-to-all | bytes 1703936 | tf_op jit(solution)/shard_map/all_to_all | solution.py:406
  34.4 1.5 state.1
  36.9 11.5 %all-to-all-start.2 = ((f32[8,72,128]{2,1,0:T(8,128)}), f32[8,72,128]{2,1,0:T(8,128)S(1)}, u32[]{:S(2)}, u32[]{:S(2)}) async-start(f32[8,72,128]{2,1,0:T(8,128)} %get-tuple-element.18), calls=%async_computation.2 | async-start | bytes 589824 | tf_op jit(solution)/shard_map/all_to_all | solution.py:406
  48.4 1.3 pack_g.1
  49.7 19.5 %all-to-all-done.2.m_ref = f32[8,72,128]{2,1,0:T(8,128)S(1)} async-done(((f32[8,72,128]{2,1,0:T(8,128)}), f32[8,72,128]{2,1,0:T(8,128)S(1)}, u32[]{:S(2)}, u32[]{:S(2)}) %all-to-all-start.2) | async-done | bytes 294944 | tf_op jit(solution)/shard_map/all_to_all | solution.py:406
  69.3 3.5 %all-to-all-start.1 = ((f32[4,648,128]{2,1,0:T(8,128)}), f32[4,648,128]{2,1,0:T(8,128)S(1)}, u32[]{:S(2)}, u32[]{:S(2)}) async-start(f32[4,648,128]{2,1,0:T(8,128)} %pack_g.1), calls=%async_computation.1 | async-start | bytes 2654208 | tf_op jit(solution)/shard_map/all_to_all | solution.py:406
  72.9 31.2 %all-to-all-done.1.g_ref = f32[4,648,128]{2,1,0:T(8,128)S(1)} async-done(((f32[4,648,128]{2,1,0:T(8,128)}), f32[4,648,128]{2,1,0:T(8,128)S(1)}, u32[]{:S(2)}, u32[]{:S(2)}) %all-to-all-start.1) | async-done | bytes 1327136 | tf_op jit(solution)/shard_map/all_to_all | solution.py:406
  104.1 20.6 %all_to_all.51.h_ref = f32[8,64,128]{2,1,0:T(8,128)S(1)} all-to-all(f32[8,64,128]{2,1,0:T(8,128)S(1)} %scan_up.1), channel_id=1, replica_groups=mesh['dp'=16,'y'=4,'zh'=2,'zl'=4] {'y','zh'}, dimensions={0} | all-to-all | bytes 524288 | tf_op jit(solution)/shard_map/all_to_all | solution.py:406
  124.8 1.2 copy-done.3
  126.0 2.0 mix.1
  128.0 6.9 %all_to_all.52.n_ref = f32[4,16,128]{2,1,0:T(8,128)S(1)} all-to-all(f32[4,16,128]{2,1,0:T(8,128)S(1)} %get-tuple-element.22), channel_id=1, replica_groups=mesh['dp'=16,'y'=4,'zh'=2,'zl'=4] {'zl'}, dimensions={0} | all-to-all | bytes 65536 | tf_op jit(solution)/shard_map/all_to_all | solution.py:406
  134.8 1.1 seeds.1
  136.0 1.0 copy-done.4
  137.0 1.0 copy-done.6
  137.9 23.7 %all_to_all.53.m_ref = f32[8,72,128]{2,1,0:T(8,128)S(1)} all-to-all(f32[8,72,128]{2,1,0:T(8,128)S(1)} %get-tuple-element.24), channel_id=1, replica_groups=mesh['dp'=16,'y'=4,'zh'=2,'zl'=4] {'y','zh'}, dimensions={0} | all-to-all | bytes 589824 | tf_op jit(solution)/shard_map/all_to_all | solution.py:406
  162.4 4.0 %all-to-all-start.6 = ((f32[8,64,128]{2,1,0:T(8,128)}), f32[8,64,128]{2,1,0:T(8,128)}, u32[]{:S(2)}, u32[]{:S(2)}) async-start(f32[8,64,128]{2,1,0:T(8,128)} %copy-done.8), calls=%async_computation.6 | async-start | bytes 524288 | tf_op jit(solution)/shard_map/all_to_all | solution.py:406
  167.2 15.0 %all-to-all-done.6.l_ref = f32[8,64,128]{2,1,0:T(8,128)} async-done(((f32[8,64,128]{2,1,0:T(8,128)}), f32[8,64,128]{2,1,0:T(8,128)}, u32[]{:S(2)}, u32[]{:S(2)}) %all-to-all-start.6) | async-done | bytes 262176 | tf_op jit(solution)/shard_map/all_to_all | solution.py:406
  182.2 1.2 copy-done.1
  183.4 1.2 copy-done.5
  185.6 4.6 %input_grad.1 = (f32[4,256,128]{2,1,0:T(8,128)}, f32[16,128]{1,0:T(8,128)S(1)}) custom-call(f32[4,416,128]{2,1,0:T(8,128)S(1)} %all_to_all.50.r_ref, f32[4,128,128]{2,1,0:T(8,128)S(1)} %copy-done.7, f32[8,64,128]{2,1,0:T(8,128)} %all-to-all-done.6.l_ref, f32[17,16,128]{2,1,0:T(8,128)S(1)} %get-tuple-element.19.table_ref, ...), custom_call_target="tpu_custom_call" | custom-call | tf_op jit(solution)/shard_map/input_grad/pallas_call | solution.py:375
  190.2 25.2 %all_to_all.54 = f32[16,16,128]{2,1,0:T(8,128)S(1)} all-to-all(f32[16,16,128]{2,1,0:T(8,128)S(1)} %broadcast_in_dim.4), channel_id=1, replica_groups=mesh['dp'=16,'y'=4,'zh'=2,'zl'=4] {'dp'}, dimensions={0} | all-to-all | bytes 262144 | tf_op jit(solution)/shard_map/all_to_all | solution.py:406
  215.5 21.7 %all_to_all.55 = f32[32,16,128]{2,1,0:T(8,128)S(1)} all-to-all(f32[32,16,128]{2,1,0:T(8,128)S(1)} %broadcast_in_dim.5), channel_id=1, replica_groups=mesh['dp'=16,'y'=4,'zh'=2,'zl'=4] {'y','zh','zl'}, dimensions={0} | all-to-all | bytes 524288 | tf_op jit(solution)/shard_map/all_to_all | solution.py:406
  237.2 3.5 %all-to-all-start.7 = ((f32[4,256,128]{2,1,0:T(8,128)}), f32[4,256,128]{2,1,0:T(8,128)S(1)}, u32[]{:S(2)}, u32[]{:S(2)}) async-start(f32[4,256,128]{2,1,0:T(8,128)} %get-tuple-element.29), calls=%async_computation.7 | async-start | bytes 1048576 | tf_op jit(solution)/shard_map/all_to_all | solution.py:406
  243.3 11.3 %all-to-all-done.7 = f32[4,256,128]{2,1,0:T(8,128)S(1)} async-done(((f32[4,256,128]{2,1,0:T(8,128)}), f32[4,256,128]{2,1,0:T(8,128)S(1)}, u32[]{:S(2)}, u32[]{:S(2)}) %all-to-all-start.7) | async-done | bytes 524320 | tf_op jit(solution)/shard_map/all_to_all | solution.py:406
  (58 shorter events, 14.0 us)
Async XLA Ops:
  0.6 1.0 copy-start.9
  1.6 0.8 copy-start.12
  2.3 0.7 copy-start.14
  3.0 0.7 copy-start.17
  3.7 0.7 copy-start.18
  4.4 0.7 copy-start.19
  7.7 40.7 %copy-start.10 = (bf16[128,1024]{1,0:T(8,128)(2,1)S(1)}, bf16[128,1024]{1,0:T(8,128)(2,1)}, u32[]{:S(2)}) copy-start(bf16[128,1024]{1,0:T(8,128)(2,1)} %z_ref.1) | copy-start | bytes 786436
  7.7 40.7 %copy-start.11 = (bf16[128,1024]{1,0:T(8,128)(2,1)S(1)}, bf16[128,1024]{1,0:T(8,128)(2,1)}, u32[]{:S(2)}) copy-start(bf16[128,1024]{1,0:T(8,128)(2,1)} %cot_ref.1) | copy-start | bytes 786436
  7.7 40.7 %copy-start.13 = (bf16[128,128]{1,0:T(8,128)(2,1)S(1)}, bf16[128,128]{1,0:T(8,128)(2,1)}, u32[]{:S(2)}) copy-start(bf16[128,128]{1,0:T(8,128)(2,1)} %c_ref.1) | copy-start | bytes 98308
  7.7 40.7 %copy-start.15 = (f32[1024]{0:T(1024)S(1)}, f32[1024]{0:T(1024)}, u32[]{:S(2)}) copy-start(f32[1024]{0:T(1024)} %param.23) | copy-start | bytes 12292
  7.7 40.7 %copy-start.16 = (f32[1024]{0:T(1024)S(1)}, f32[1024]{0:T(1024)}, u32[]{:S(2)}) copy-start(f32[1024]{0:T(1024)} %param.27) | copy-start | bytes 12292
  35.9 1.0 copy-start.2
  36.9 32.4 %all-to-all-start.2 = ((f32[8,72,128]{2,1,0:T(8,128)}), f32[8,72,128]{2,1,0:T(8,128)S(1)}, u32[]{:S(2)}, u32[]{:S(2)}) async-start(f32[8,72,128]{2,1,0:T(8,128)} %get-tuple-element.18), calls=%async_computation.2 | async-start | bytes 589824 | tf_op jit(solution)/shard_map/all_to_all | solution.py:406
  69.3 34.8 %all-to-all-start.1 = ((f32[4,648,128]{2,1,0:T(8,128)}), f32[4,648,128]{2,1,0:T(8,128)S(1)}, u32[]{:S(2)}, u32[]{:S(2)}) async-start(f32[4,648,128]{2,1,0:T(8,128)} %pack_g.1), calls=%async_computation.1 | async-start | bytes 2654208 | tf_op jit(solution)/shard_map/all_to_all | solution.py:406
  124.7 1.2 copy-start.3
  128.0 8.0 %copy-start = (f32[4,2,256,128]{3,2,1,0:T(8,128)}, f32[4,2,256,128]{3,2,1,0:T(8,128)S(1)}, u32[]{:S(2)}) copy-start(f32[4,2,256,128]{3,2,1,0:T(8,128)S(1)} %get-tuple-element.26.hb_ref) | copy-start | bytes 3145732
  136.0 1.0 copy-start.4
  137.0 1.0 copy-start.6
  161.7 0.7 copy-start.8
  162.4 19.8 %all-to-all-start.6 = ((f32[8,64,128]{2,1,0:T(8,128)}), f32[8,64,128]{2,1,0:T(8,128)}, u32[]{:S(2)}, u32[]{:S(2)}) async-start(f32[8,64,128]{2,1,0:T(8,128)} %copy-done.8), calls=%async_computation.6 | async-start | bytes 524288 | tf_op jit(solution)/shard_map/all_to_all | solution.py:406
  182.2 1.2 copy-start.1
  183.4 1.2 copy-start.5
  184.6 0.9 copy-start.7
  237.2 17.4 %all-to-all-start.7 = ((f32[4,256,128]{2,1,0:T(8,128)}), f32[4,256,128]{2,1,0:T(8,128)S(1)}, u32[]{:S(2)}, u32[]{:S(2)}) async-start(f32[4,256,128]{2,1,0:T(8,128)} %get-tuple-element.29), calls=%async_computation.7 | async-start | bytes 1048576 | tf_op jit(solution)/shard_map/all_to_all | solution.py:406
  (3 other events, 2.0 us)

commit v2 on v1

--- a/solution.py
+++ b/solution.py
@@ -22,10 +22,14 @@
 SEGS = 8
 CPS = CPD // SEGS
 PARAMS = 6
-X_ROWS = CPD + N + HPD + PARAMS * HPD + 4
+NEAR = 32
+FAR = 16
+FIRST = (1,)
+EARLY = (2, 3)
+X_ROWS = CPD + N + HPD + 4
 G_ROWS = 2 * CPD + T + 8
 M_ROWS = 2 * CPS + 8
-VMEM = 48 * 1024 * 1024
+VMEM = 16 * 1024 * 1024
 
 (K_C, K_DC, K_DT, K_DDT, K_W, K_DW, K_TAIL, K_SG, K_DSG, K_F0, K_F1, K_G, K_DG, K_F0T, K_F1T, K_D, K_DD) = range(17)
 TABLE = 17
@@ -50,8 +54,7 @@
     )
 
 
-def pack_x_kernel(x_ref, b_ref, dt_ref, *rest):
-    prm, o_ref = rest[:PARAMS], rest[PARAMS]
+def pack_x_kernel(x_ref, b_ref, dt_ref, o_ref):
     for j in range(BLK):
         for i in range(CPD // 128):
             lo = j * CPD + i * 128
@@ -60,33 +63,36 @@
         at = CPD + N
         o_ref[j, at : at + HPD, :] = dt_ref[j * HPD : (j + 1) * HPD, :]
         at += HPD
-        for k in range(PARAMS):
-            for h in range(HPD):
-                o_ref[j, at : at + 1, :] = jnp.full((1, T), prm[k][j * HPD + h], F32)
-                at += 1
-        o_ref[j, at : at + 4, :] = jnp.zeros((4, T), F32)
-
-
-def pack_g_kernel(z_ref, cot_ref, c_ref, gain_ref, dgain_ref, o_ref):
+        o_ref[j, at:X_ROWS, :] = jnp.zeros((X_ROWS - at, T), F32)
+
+
+def pack_g_kernel(zl_ref, z_ref, cot_ref, c_ref, gain_ref, dgain_ref, after_ref, *o_refs):
+    del after_ref
     halves = CPD // 128
-    for j in range(BLK):
+    for d, o_ref in enumerate(o_refs):
+        j = lax.rem(zl_ref[0] + d, BLK)
         for n, ref in enumerate((z_ref, cot_ref)):
             for i in range(halves):
-                lo = j * CPD + i * 128
+                lo = pl.multiple_of(j * CPD + i * 128, 128)
                 at = n * CPD + i * 128
-                o_ref[j, at : at + 128, :] = ref[:, lo : lo + 128].astype(F32).T
-        o_ref[j, 2 * CPD : 2 * CPD + T, :] = c_ref[...].astype(F32)
+                o_ref[at : at + 128, :] = ref[:, pl.ds(lo, 128)].astype(F32).T
+        o_ref[2 * CPD : 2 * CPD + T, :] = c_ref[...].astype(F32)
         at = 2 * CPD + T
-        o_ref[j, at : at + halves, :] = gain_ref[j * halves : (j + 1) * halves, :]
-        o_ref[j, at + halves : at + 2 * halves, :] = dgain_ref[j * halves : (j + 1) * halves, :]
-        o_ref[j, at + 2 * halves : at + 8, :] = jnp.zeros((8 - 2 * halves, 128), F32)
-
-
-def write_message(msg_ref, total, d_total, table):
+        for i in range(halves):
+            o_ref[at + i : at + i + 1, :] = gain_ref[pl.ds(j * halves + i, 1), :]
+            o_ref[at + halves + i : at + halves + i + 1, :] = dgain_ref[pl.ds(j * halves + i, 1), :]
+        o_ref[at + 2 * halves : at + 8, :] = jnp.zeros((8 - 2 * halves, 128), F32)
+
+
+def write_message(msg_ref, total, d_total):
+    for j in range(SEGS):
+        msg_ref[j, 0:CPS, :] = total[j * CPS : (j + 1) * CPS]
+        msg_ref[j, CPS : 2 * CPS, :] = d_total[j * CPS : (j + 1) * CPS]
+
+
+def write_decay(msg_ref, table):
     for j in range(SEGS):
         h = j * CPS // HD
-        msg_ref[j, 0:CPS, :] = total[j * CPS : (j + 1) * CPS]
-        msg_ref[j, CPS : 2 * CPS, :] = d_total[j * CPS : (j + 1) * CPS]
         g, dg = None, None
         for b in range(BLK):
             r = b * HPD + h
@@ -97,14 +103,16 @@
         msg_ref[j, 2 * CPS + 2 : M_ROWS, :] = jnp.zeros((M_ROWS - 2 * CPS - 2, T), F32)
 
 
-def state_kernel(r_ref, table_ref, cols_ref, s_ref, msg_ref):
+def state_kernel(zl_ref, *rest):
+    prm, r_ref = rest[:PARAMS], rest[PARAMS]
+    table_ref, cols_ref, s_ref, msg_ref = rest[-4:]
     at = CPD + N
-
-    def gather(lo):
-        return jnp.concatenate([r_ref[b, lo : lo + HPD, :] for b in range(BLK)], axis=0)
-
-    raw = gather(at)
-    a_log, dt_bias, d_skip, p_a, p_dt, p_skip = [gather(at + HPD * (1 + k)) for k in range(PARAMS)]
+    raw = jnp.concatenate([r_ref[b, at : at + HPD, :] for b in range(BLK)], axis=0)
+
+    def head_values(ref):
+        return jnp.concatenate([jnp.full((1, T), ref[zl_ref[0] * HPD + h], F32) for h in range(HPD)] * BLK, axis=0)
+
+    a_log, dt_bias, d_skip, p_a, p_dt, p_skip = [head_values(ref) for ref in prm]
     pre = raw + dt_bias
     dt = jnp.maximum(pre, 0.0) + jnp.log1p(jnp.exp(-jnp.abs(pre)))
     sg = 1.0 / (1.0 + jnp.exp(-pre))
@@ -156,19 +164,24 @@
         eg = jnp.exp(heads_rows(table_ref, K_G, b))
         d_total = eg * (d_total + heads_rows(table_ref, K_DG, b) * total) + ds
         total = eg * total + s
-    write_message(msg_ref, total, d_total, table_ref)
-
-
-def scan_kernel(reverse, m_ref, o_ref):
+    write_message(msg_ref, total, d_total)
+    write_decay(msg_ref, table_ref)
+
+
+def scan_kernel(reverse, decay_ref, m_ref, o_ref):
     total = jnp.zeros((CPS, N), F32)
     d_total = jnp.zeros((CPS, N), F32)
     for i in range(SEGS - 1, -1, -1) if reverse else range(SEGS):
         o_ref[i, 0:CPS, :] = total
         o_ref[i, CPS : 2 * CPS, :] = d_total
-        eg = jnp.exp(m_ref[i, 2 * CPS : 2 * CPS + 1, :])
-        dg = m_ref[i, 2 * CPS + 1 : 2 * CPS + 2, :]
+        eg = jnp.exp(decay_ref[i, 2 * CPS : 2 * CPS + 1, :])
+        dg = decay_ref[i, 2 * CPS + 1 : 2 * CPS + 2, :]
         d_total = eg * (d_total + dg * total) + m_ref[i, CPS : 2 * CPS, :]
         total = eg * total + m_ref[i, 0:CPS, :]
+
+
+def scan_up_kernel(m_ref, *rest):
+    scan_kernel(False, m_ref, m_ref, rest[-1])
 
 
 def gains(g_ref):
@@ -195,7 +208,16 @@
     return lax.broadcasted_iota(jnp.int32, (T, T), 0) <= lax.broadcasted_iota(jnp.int32, (T, T), 1)
 
 
-def out_kernel(r_ref, g_ref, h_ref, table_ref, cols_ref, s_ref, y_ref, hb_ref, msg_ref):
+def out_kernel(
+    zl_ref, r_ref, g0, g1, g2, g3, h_ref, table_ref, cols_ref, s_ref, g_ref, y_ref, hb_ref, msg_ref, sems
+):
+    copies = []
+    for d, src in enumerate((g0, g1, g2, g3)):
+        b = lax.rem(zl_ref[0] + BLK - d, BLK)
+        copies.append(pltpu.make_async_copy(src, g_ref.at[b], sems.at[d]))
+        copies[-1].start()
+    for copy in copies:
+        copy.wait()
     causal = causal_mask()
     gain, dgain = gains(g_ref)
     h = h_ref[:, 0:CPS, :].reshape(CPD, N)
@@ -285,14 +307,17 @@
         adj = eg * adj + seed
     for i in range(CPD // 128):
         gain_ref[i : i + 1, :] = jnp.sum(acc[i * 128 : (i + 1) * 128].T, axis=0, keepdims=True)
-    write_message(msg_ref, adj, d_adj, table_ref)
+    write_message(msg_ref, adj, d_adj)
 
 
 def head_sum(v):
     return jnp.sum(v, axis=0, keepdims=True)
 
 
-def input_kernel(r_ref, g_ref, l_ref, table_ref, cols_ref, y_ref, yb_ref, hb_ref, seed_ref, gain_ref, o_ref, part_ref):
+def input_kernel(
+    zl_ref, r_ref, g_ref, l_ref, table_ref, cols_ref, y_ref, yb_ref, hb_ref, seed_ref, gain_ref, *rest
+):
+    o_refs, part_ref, o_ref, sems = rest[:BLK], rest[BLK], rest[BLK + 1], rest[BLK + 2]
     causal = causal_mask()
     adj = l_ref[:, 0:CPS, :].reshape(CPD, N)
     d_adj = l_ref[:, CPS : 2 * CPS, :].reshape(CPD, N)
@@ -301,7 +326,7 @@
     acc_skip = [jnp.zeros((1, T), F32) for _ in range(HPD)]
     for b in range(BLK - 1, -1, -1):
         bmat = r_ref[b, CPD : CPD + N, :].astype(BF16)
-        cmat = g_ref[b, 0:T, :].astype(BF16)
+        cmat = g_ref[b, 2 * CPD : 2 * CPD + T, :].astype(BF16)
         got = mmt(jnp.concatenate(split(adj) + split(d_adj), axis=0), bmat)
         bl = got[0:CPD] + got[CPD : 2 * CPD]
         dbl = got[2 * CPD : 3 * CPD] + got[3 * CPD :]
@@ -356,15 +381,57 @@
             eg = jnp.exp(heads_rows(table_ref, K_G, b))
             d_adj = eg * (d_adj + heads_rows(table_ref, K_DG, b) * adj) + seed_ref[b, 1]
             adj = eg * adj + seed_ref[b, 0]
-    for i in range(HPD):
-        part_ref[i : i + 1, :] = acc_a[i]
-        part_ref[HPD + i : HPD + i + 1, :] = acc_dt[i]
-        part_ref[2 * HPD + i : 2 * HPD + i + 1, :] = acc_skip[i]
-    part_ref[3 * HPD : 3 * HPD + 2, :] = gain_ref[...]
-    part_ref[3 * HPD + 2 :, :] = jnp.zeros((2, T), F32)
-
-
-def call(kernel, name, outs, in_specs=None):
+    part = jnp.concatenate(acc_a + acc_dt + acc_skip + [gain_ref[...], jnp.zeros((2, T), F32)], axis=0)
+    copies = []
+    for d in range(BLK):
+        copies.append(pltpu.make_async_copy(o_ref.at[lax.rem(zl_ref[0] + d, BLK)], o_refs[d], sems.at[d]))
+        copies[-1].start()
+    for i in range(NEAR):
+        part_ref[i] = part
+    for copy in copies:
+        copy.wait()
+
+
+def place_kernel(zl_ref, i0, i1, i2, i3, o_ref, sems):
+    copies = []
+    for d, src in enumerate((i0, i1, i2, i3)):
+        j = lax.rem(zl_ref[0] + BLK - d, BLK)
+        for i in range(CPD // 128):
+            lo = pl.multiple_of(j * CPD + i * 128, 128)
+            copies.append(
+                pltpu.make_async_copy(
+                    src.at[pl.ds(i * 128, 128), :], o_ref.at[:, pl.ds(lo, 128)], sems.at[len(copies)]
+                )
+            )
+            copies[-1].start()
+    for copy in copies:
+        copy.wait()
+
+
+def sum_kernel(m_ref, o_ref):
+    total = m_ref[0]
+    for i in range(1, NEAR):
+        total = total + m_ref[i]
+    for i in range(FAR):
+        o_ref[i] = total
+
+
+def finish_kernel(factor, m_ref, a_ref, dt_ref, skip_ref, gain_ref):
+    outs = (a_ref, dt_ref, skip_ref)
+    rows = [[] for _ in outs]
+    for j in range(BLK):
+        total = m_ref[j]
+        for i in range(1, FAR // BLK):
+            total = total + m_ref[i * BLK + j]
+        total = total * factor
+        for n in range(len(outs)):
+            rows[n].append(total[n * HPD : (n + 1) * HPD, :])
+        gain_ref[2 * j : 2 * j + 2, :] = total[3 * HPD : 3 * HPD + 2, :]
+    for n, ref in enumerate(outs):
+        ref[...] = jnp.sum(jnp.concatenate(rows[n], axis=0).T, axis=0, keepdims=True)
+
+
+def call(kernel, name, outs, in_specs=None, scratch=(), out_specs=None):
     def shape(dims):
         return jax.ShapeDtypeStruct(dims, F32)
 
@@ -376,8 +443,9 @@
             kernel,
             name=name,
             out_shape=[shape(o) for o in outs] if many else shape(outs),
-            out_specs=[spec] * len(outs) if many else spec,
+            out_specs=out_specs or ([spec] * len(outs) if many else spec),
             in_specs=in_specs or [spec] * len(args),
+            scratch_shapes=list(scratch),
             compiler_params=pltpu.CompilerParams(vmem_limit_bytes=VMEM),
         )(*args)
 
@@ -400,65 +468,85 @@
     probe_skip,
     probe_gain,
 ):
-    vm, sm = pl.BlockSpec(memory_space=pltpu.VMEM), pl.BlockSpec(memory_space=pltpu.SMEM)
+    vm, sm, hbm = [pl.BlockSpec(memory_space=m) for m in (pltpu.VMEM, pltpu.SMEM, pltpu.HBM)]
 
     def exchange(v, axes):
         return lax.all_to_all(v, axes, 0, 0)
 
     group, segs = "zl", ("y", "zh")
-    packed = call(pack_x_kernel, "pack_x", (BLK, X_ROWS, T), [vm] * 3 + [sm] * PARAMS)(
-        ssm_input, b_proj, dt_raw.T, a_log, dt_bias, d_skip, probe_a, probe_dt, probe_skip
+
+    def shift(v, d):
+        return lax.ppermute(v, group, [(i, (i + d) % BLK) for i in range(BLK)])
+
+    zl = lax.axis_index(group).reshape(1)
+    packed = call(pack_x_kernel, "pack_x", (BLK, X_ROWS, T))(ssm_input, b_proj, dt_raw.T)
+    r = exchange(packed, group)
+    parts = call(pack_g_kernel, "pack_g", [(G_ROWS, T)] * BLK, [sm] + [vm] * 5 + [hbm])(
+        zl, gate_input, cotangent, c_proj, norm_gain.reshape(8, 128), probe_gain.reshape(8, 128), norm_gain
     )
-    r = exchange(packed, group)
-    packed_g = call(pack_g_kernel, "pack_g", (BLK, G_ROWS, T))(
-        gate_input, cotangent, c_proj, norm_gain.reshape(8, 128), probe_gain.reshape(8, 128)
-    )
-    g = exchange(packed_g, group)
+    parts = [shift(v, d) if d else v for d, v in enumerate(parts)]
     table, cols, s, msg = call(
         state_kernel,
         "state",
         [(TABLE, ROWS, T), (T, T), (BLK, 2, CPD, N), (SEGS, M_ROWS, N)],
-    )(r)
-    before = call(functools.partial(scan_kernel, False), "scan_up", (SEGS, 2 * CPS, N))(exchange(msg, segs))
+        [sm] * (1 + PARAMS) + [vm] + [hbm] * len(FIRST),
+    )(zl, a_log, dt_bias, d_skip, probe_a, probe_dt, probe_skip, r, *[parts[d] for d in FIRST])
+    decay = exchange(msg, segs)
+    early = [parts[d] for d in EARLY]
+    before = call(scan_up_kernel, "scan_up", (SEGS, 2 * CPS, N), [vm] + [hbm] * len(early))(decay, *early)
     h_in = exchange(before, segs)
-    y, h_blocks, norms = call(
-        out_kernel, "mix", [(2, BLK, CPD, T), (BLK, 2, CPD, N), (BLK, 4 * BLK, T)]
-    )(r, g, h_in, table, cols, s)
+    g, y, h_blocks, norms = call(
+        out_kernel,
+        "mix",
+        [(BLK, G_ROWS, T), (2, BLK, CPD, T), (BLK, 2, CPD, N), (BLK, 4 * BLK, T)],
+        [sm, vm] + [hbm] * BLK + [vm] * 4,
+        [pltpu.SemaphoreType.DMA((BLK,))],
+    )(zl, r, *parts, h_in, table, cols, s)
     norms = exchange(norms, group)
     y_bar, seeds, d_gain, msg = call(
         seed_kernel,
         "seeds",
-        [(2, BLK, CPD, T), (BLK, 2, CPD, N), (2, 128), (SEGS, M_ROWS, N)],
+        [(2, BLK, CPD, T), (BLK, 2, CPD, N), (2, 128), (SEGS, 2 * CPS, N)],
     )(r, g, norms, table, y)
-    after = call(functools.partial(scan_kernel, True), "scan_down", (SEGS, 2 * CPS, N))(exchange(msg, segs))
+    after = call(functools.partial(scan_kernel, True), "scan_down", (SEGS, 2 * CPS, N))(
+        decay, exchange(msg, segs)
+    )
     adj = exchange(after, segs)
-    c_all = g[:, 2 * CPD : 2 * CPD + T, :]
-    out, part = call(input_kernel, "input_grad", [(BLK, CPD, 128), (4 * HPD, T)])(
-        r, c_all, adj, table, cols, y, y_bar, h_blocks, seeds, d_gain
-    )
-    out = exchange(out, group).reshape(CH // 128, T, 128)
-    hvp_input = jnp.transpose(out, (1, 0, 2)).reshape(T, CH)
-
-    devices = lax.axis_size("dp")
-    part = jnp.sum(exchange(jnp.broadcast_to(part[None], (devices,) + part.shape), "dp"), axis=0)
-    whole = SEGS * BLK
-    part = exchange(jnp.broadcast_to(part[None], (whole,) + part.shape), ("y", "zh", "zl"))
-    part = jnp.sum(part.reshape(SEGS, BLK, 4 * HPD, T), axis=0)
-    factor = 1.0 / math.sqrt(T * devices * whole)
-    heads = jnp.sum(part[:, : 3 * HPD, :], axis=2).reshape(BLK, 3, HPD) * factor
-    hvp_gain = part[:, 3 * HPD : 3 * HPD + 2, :].reshape(CH) * factor
+    *outs, part = call(
+        input_kernel,
+        "input_grad",
+        [(CPD, 128)] * BLK + [(NEAR, 4 * HPD, T)],
+        [sm] + [vm] * 10,
+        [pltpu.VMEM((BLK, CPD, 128), F32), pltpu.SemaphoreType.DMA((BLK,))],
+        [hbm] * BLK + [vm],
+    )(zl, r, g, adj, table, cols, y, y_bar, h_blocks, seeds, d_gain)
+    outs = [shift(v, d) if d else v for d, v in enumerate(outs)]
+    part = call(sum_kernel, "near_sum", (FAR, 4 * HPD, T))(exchange(part, ("x", "core", "y")))
+    hvp_input = call(
+        place_kernel,
+        "place",
+        (T, CH),
+        [sm] + [hbm] * BLK,
+        [pltpu.SemaphoreType.DMA((CH // 128,))],
+        hbm,
+    )(zl, *outs)
+    factor = 1.0 / math.sqrt(T * NEAR * FAR)
+    hvp_a, hvp_dt, hvp_skip, hvp_gain = call(
+        functools.partial(finish_kernel, factor), "finish", [(1, HEADS)] * 3 + [(8, 128)]
+    )(exchange(part, ("zhi", "zh", "zl")))
     return (
         hvp_input,
-        heads[:, 0].reshape(HEADS),
-        heads[:, 1].reshape(HEADS),
-        heads[:, 2].reshape(HEADS),
-        hvp_gain,
+        hvp_a.reshape(HEADS),
+        hvp_dt.reshape(HEADS),
+        hvp_skip.reshape(HEADS),
+        hvp_gain.reshape(CH),
     )
 
 
 def solution(mesh):
-    fine = Mesh(mesh.devices.reshape(mesh.devices.shape[0], 4, 2, 4), ("dp", "y", "zh", "zl"))
-    tokens = P(("dp", "y", "zh", "zl"), None)
+    axes = ("zhi", "x", "core", "y", "zh", "zl")
+    fine = Mesh(mesh.devices.reshape(2, 4, 2, 4, 2, 4), axes)
+    tokens = P(axes, None)
     return jax.shard_map(
         per_device,
         mesh=fine,

time: 257 us -> 201 us (0.78)
  blocking collectives: 125 us -> 89.3 us
  waiting for transfers between devices: 77.1 us -> 48.1 us
  starting transfers between devices: 22.6 us -> 44.6 us
  local copies, waits for them, and re-layouts: 18.1 us -> 3.18 us
    all_to_all x4 -> x3, waiting for transfers between devices: 77.1 us -> 5.43 us  [exchange(): return lax.all_to_all(v, axes, 0, 0)]
    ppermute x0 -> x6, waiting for transfers between devices: none -> 42.7 us  [shift(): return lax.ppermute(v, group, [(i, (i + d) % BLK) for i in range(BLK)])]
    all_to_all x6 -> x5, blocking collectives: 125 us -> 89.3 us  [exchange(): return lax.all_to_all(v, axes, 0, 0)]
    ppermute x0 -> x6, starting transfers between devices: none -> 17.6 us  [shift(): return lax.ppermute(v, group, [(i, (i + d) % BLK) for i in range(BLK)])]
    unnamed x46 -> x34, local copies, waits for them, and re-layouts: 14.6 us -> 3.18 us
    all_to_all x4 -> x3, starting transfers between devices: 22.6 us -> 27 us  [exchange(): return lax.all_to_all(v, axes, 0, 0)]
    pallas_call x8 -> x11, Pallas kernels: 11.3 us -> 13.3 us  [run(): pl.pallas_call(kernel, name=name, out_shape=[shape(o) for o in outs] if m...]
  transfers between devices with their start and end apart: 4 -> 9, of which waited for: 4 -> 5; matrix products, arithmetic and copies ran while one was open for 1% -> 0% of each run, Pallas kernels for 1% -> 1%
where the time goes in v2:
time: 201 us; the launch traced here: 199 us
  blocking collectives  89.3 us (44%)
  waiting for transfers between devices  48.1 us (24%)
  starting transfers between devices  44.6 us (22%)
  Pallas kernels  13.3 us (7%)
  local copies, waits for them, and re-layouts  3.18 us (2%)
    all_to_all x5, blocking collectives, exchange(): return lax.all_to_all(v, axes, 0, 0)  89.3 us
    ppermute x6, waiting for transfers between devices, shift(): return lax.ppermute(v, group, [(i, (i + d) % BLK) for i in range(BLK)])  42.7 us
    all_to_all x3, starting transfers between devices, exchange(): return lax.all_to_all(v, axes, 0, 0)  27 us
    ppermute x6, starting transfers between devices, shift(): return lax.ppermute(v, group, [(i, (i + d) % BLK) for i in range(BLK)])  17.6 us
    pallas_call x11, Pallas kernels, run(): pl.pallas_call(kernel, name=name, out_shape=[shape(o) for o in outs] if m...  13.3 us
    all_to_all x3, waiting for transfers between devices, exchange(): return lax.all_to_all(v, axes, 0, 0)  5.43 us
  transfers between devices with their start and end apart: 9, of which 5 were waited for; matrix products, arithmetic and copies ran while one was open for 0% of the time, Pallas kernels for 1%

profile of v2, /device:TPU:1, one launch (start us, length us, event | category | flops | bytes accessed | tf_op | source)
XLA Modules:
  0.0 199.3 jit_solution(7631560966554382333)
XLA Ops:
  3.1 1.0 pack_x.1
  4.1 6.6 %all-to-all-start = ((f32[4,392,128]{2,1,0:T(8,128)}), f32[4,392,128]{2,1,0:T(8,128)S(1)}, u32[]{:S(2)}, u32[]{:S(2)}) async-start(f32[4,392,128]{2,1,0:T(8,128)} %pack_x.1), calls=%async_computation | async-start | bytes 1605632 | tf_op jit(solution)/shard_map/all_to_all | solution.py:474
  12.4 3.4 %collective-permute-start = (f32[648,128]{1,0:T(8,128)S(1)}, f32[648,128]{1,0:T(8,128)S(1)}, u32[]{:S(2)}, u32[]{:S(2)}) collective-permute-start(f32[648,128]{1,0:T(8,128)S(1)} %get-tuple-element.31), channel_id=1, source_target_pairs={{0,1},{1,2},{2,3},{3,0},{4,5},{5,6},{6,7},{7,4},{8,9},{9,10},{10,1... | collective-permute-start | bytes 995336 | tf_op jit(solution)/shard_map/ppermute | solution.py:479
  15.8 15.1 %collective-permute-done.rest_7_.g1 = f32[648,128]{1,0:T(8,128)S(1)} collective-permute-done((f32[648,128]{1,0:T(8,128)S(1)}, f32[648,128]{1,0:T(8,128)S(1)}, u32[]{:S(2)}, u32[]{:S(2)}) %collective-permute-start) | collective-permute-done | bytes 331808 | tf_op jit(solution)/shard_map/ppermute | solution.py:479
  30.9 5.4 %all-to-all-done.rest_6_.r_ref = f32[4,392,128]{2,1,0:T(8,128)S(1)} async-done(((f32[4,392,128]{2,1,0:T(8,128)}), f32[4,392,128]{2,1,0:T(8,128)S(1)}, u32[]{:S(2)}, u32[]{:S(2)}) %all-to-all-start) | async-done | bytes 802848 | tf_op jit(solution)/shard_map/all_to_all | solution.py:474
  36.3 2.1 %state.1 = (f32[17,16,128]{2,1,0:T(8,128)S(1)}, f32[128,128]{1,0:T(8,128)S(1)}, f32[4,2,256,128]{3,2,1,0:T(8,128)S(1)}, f32[8,72,128]{2,1,0:T(8,128)}) custom-call(s32[1]{0:T(128)} %bitcast.zl_ref, f32[16]{0:T(128)S(1)} %copy-done.10, f32[16]{0:T(128)S(1)} %copy-done.11, f32[16]{0:T(128)S(1)} %copy-done.12, f32[16]{0:T(128)S(1)} %copy-done.13, ...), custom_call_target="tpu_custom_call" | custom-call | tf_op jit(solution)/shard_map/state/pallas_call | solution.py:442
  38.4 12.3 %all-to-all-start.1 = ((f32[8,72,128]{2,1,0:T(8,128)}), f32[8,72,128]{2,1,0:T(8,128)S(1)}, u32[]{:S(2)}, u32[]{:S(2)}) async-start(f32[8,72,128]{2,1,0:T(8,128)} %get-tuple-element.34), calls=%async_computation.1 | async-start | bytes 589824 | tf_op jit(solution)/shard_map/all_to_all | solution.py:474
  50.8 1.9 collective-permute-start.1
  52.7 2.0 collective-permute-start.2
  54.6 19.5 %collective-permute-done.1.rest_0_.g2 = f32[648,128]{1,0:T(8,128)S(1)} collective-permute-done((f32[648,128]{1,0:T(8,128)}, f32[648,128]{1,0:T(8,128)S(1)}, u32[]{:S(2)}, u32[]{:S(2)}) %collective-permute-start.1) | collective-permute-done | bytes 331808 | tf_op jit(solution)/shard_map/ppermute | solution.py:479
  74.2 14.9 %all_to_all.40.h_ref = f32[8,64,128]{2,1,0:T(8,128)S(1)} all-to-all(f32[8,64,128]{2,1,0:T(8,128)S(1)} %scan_up.1), channel_id=1, replica_groups=mesh['zhi'=2,'x'=4,'core'=2,'y'=4,'zh'=2,'zl'=4] {'y','zh'}, dimensions={0} | all-to-all | bytes 524288 | tf_op jit(solution)/shard_map/all_to_all | solution.py:474
  89.2 2.5 %mix.1 = (f32[4,648,128]{2,1,0:T(8,128)S(1)}, f32[2,4,256,128]{3,2,1,0:T(8,128)S(1)}, f32[4,2,256,128]{3,2,1,0:T(8,128)S(1)}, f32[4,16,128]{2,1,0:T(8,128)S(1)}) custom-call(s32[1]{0:T(128)} %bitcast.zl_ref, f32[4,392,128]{2,1,0:T(8,128)S(1)} %all-to-all-done.rest_6_.r_ref, f32[648,128]{1,0:T(8,128)S(1)} %copy-done.1, ...), custom_call_target="tpu_custom_call" | custom-call | tf_op jit(solution)/shard_map/mix/pallas_call | solution.py:442
  91.7 17.5 %all_to_all.41.n_ref = f32[4,16,128]{2,1,0:T(8,128)S(1)} all-to-all(f32[4,16,128]{2,1,0:T(8,128)S(1)} %get-tuple-element.39), channel_id=1, replica_groups=mesh['zhi'=2,'x'=4,'core'=2,'y'=4,'zh'=2,'zl'=4] {'zl'}, dimensions={0} | all-to-all | bytes 65536 | tf_op jit(solution)/shard_map/all_to_all | solution.py:474
  109.2 1.1 seeds.1
  110.3 24.4 %all_to_all.42.m_ref = f32[8,64,128]{2,1,0:T(8,128)S(1)} all-to-all(f32[8,64,128]{2,1,0:T(8,128)S(1)} %get-tuple-element.41), channel_id=1, replica_groups=mesh['zhi'=2,'x'=4,'core'=2,'y'=4,'zh'=2,'zl'=4] {'y','zh'}, dimensions={0} | all-to-all | bytes 524288 | tf_op jit(solution)/shard_map/all_to_all | solution.py:474
  134.7 18.6 %all_to_all.43.l_ref = f32[8,64,128]{2,1,0:T(8,128)S(1)} all-to-all(f32[8,64,128]{2,1,0:T(8,128)S(1)} %scan_down.1), channel_id=1, replica_groups=mesh['zhi'=2,'x'=4,'core'=2,'y'=4,'zh'=2,'zl'=4] {'y','zh'}, dimensions={0} | all-to-all | bytes 524288 | tf_op jit(solution)/shard_map/all_to_all | solution.py:474
  153.3 3.4 %input_grad.1 = (f32[256,128]{1,0:T(8,128)S(1)}, f32[256,128]{1,0:T(8,128)S(1)}, f32[256,128]{1,0:T(8,128)S(1)}, f32[256,128]{1,0:T(8,128)S(1)}, f32[32,16,128]{2,1,0:T(8,128)S(1)}) custom-call(s32[1]{0:T(128)} %bitcast.zl_ref, f32[4,392,128]{2,1,0:T(8,128)S(1)} %all-to-all-done.rest_6_.r_ref, f32[4,648,128]{2,1,0:T(8,128)S(1)} %get-tuple-element.38.g_ref, ...), custom_call_target="tpu_custom_call" | custom-call | tf_op jit(solution)/shard_map/input_grad/pallas_call | solution.py:442
  156.7 13.8 %all_to_all.44.m_ref = f32[32,16,128]{2,1,0:T(8,128)S(1)} all-to-all(f32[32,16,128]{2,1,0:T(8,128)S(1)} %get-tuple-element.50), channel_id=1, replica_groups=mesh['zhi'=2,'x'=4,'core'=2,'y'=4,'zh'=2,'zl'=4] {'x','core','y'}, dimensions={0} | all-to-all | bytes 524288 | tf_op jit(solution)/shard_map/all_to_all | solution.py:474
  171.2 8.1 %all-to-all-start.7 = ((f32[16,16,128]{2,1,0:T(8,128)}), f32[16,16,128]{2,1,0:T(8,128)S(1)}, u32[]{:S(2)}, u32[]{:S(2)}) async-start(f32[16,16,128]{2,1,0:T(8,128)} %near_sum.1), calls=%async_computation.7 | async-start | bytes 262144 | tf_op jit(solution)/shard_map/all_to_all | solution.py:474
  179.4 3.3 %collective-permute-start.3 = (f32[256,128]{1,0:T(8,128)S(1)}, f32[256,128]{1,0:T(8,128)S(1)}, u32[]{:S(2)}, u32[]{:S(2)}) collective-permute-start(f32[256,128]{1,0:T(8,128)S(1)} %get-tuple-element.47), channel_id=1, source_target_pairs={{0,1},{1,2},{2,3},{3,0},{4,5},{5,6},{6,7},{7,4},{8,9},{9,10},{10,1... | collective-permute-start | bytes 393224 | tf_op jit(solution)/shard_map/ppermute | solution.py:479
  182.6 4.0 %collective-permute-start.4 = (f32[256,128]{1,0:T(8,128)S(1)}, f32[256,128]{1,0:T(8,128)S(1)}, u32[]{:S(2)}, u32[]{:S(2)}) collective-permute-start(f32[256,128]{1,0:T(8,128)S(1)} %get-tuple-element.48), channel_id=1, source_target_pairs={{0,2},{1,3},{2,0},{3,1},{4,6},{5,7},{6,4},{7,5},{8,10},{9,11},{10,... | collective-permute-start | bytes 393224 | tf_op jit(solution)/shard_map/ppermute | solution.py:479
  186.6 3.1 %collective-permute-start.5 = (f32[256,128]{1,0:T(8,128)S(1)}, f32[256,128]{1,0:T(8,128)S(1)}, u32[]{:S(2)}, u32[]{:S(2)}) collective-permute-start(f32[256,128]{1,0:T(8,128)S(1)} %get-tuple-element.49), channel_id=1, source_target_pairs={{0,3},{1,0},{2,1},{3,2},{4,7},{5,4},{6,5},{7,6},{8,11},{9,8},{10,9... | collective-permute-start | bytes 393224 | tf_op jit(solution)/shard_map/ppermute | solution.py:479
  189.7 2.3 %collective-permute-done.3.i1 = f32[256,128]{1,0:T(8,128)S(1)} collective-permute-done((f32[256,128]{1,0:T(8,128)S(1)}, f32[256,128]{1,0:T(8,128)S(1)}, u32[]{:S(2)}, u32[]{:S(2)}) %collective-permute-start.3) | collective-permute-done | bytes 131104 | tf_op jit(solution)/shard_map/ppermute | solution.py:479
  192.0 5.8 %collective-permute-done.4.i2 = f32[256,128]{1,0:T(8,128)S(1)} collective-permute-done((f32[256,128]{1,0:T(8,128)S(1)}, f32[256,128]{1,0:T(8,128)S(1)}, u32[]{:S(2)}, u32[]{:S(2)}) %collective-permute-start.4) | collective-permute-done | bytes 131104 | tf_op jit(solution)/shard_map/ppermute | solution.py:479
  (44 shorter events, 6.4 us)
Async XLA Ops:
  0.6 1.0 copy-start.4
  1.6 0.8 copy-start.5
  3.0 7.7 %copy-start.2 = (bf16[128,1024]{1,0:T(8,128)(2,1)S(1)}, bf16[128,1024]{1,0:T(8,128)(2,1)}, u32[]{:S(2)}) copy-start(bf16[128,1024]{1,0:T(8,128)(2,1)} %z_ref.1) | copy-start | bytes 786436
  3.0 7.7 %copy-start.3 = (bf16[128,1024]{1,0:T(8,128)(2,1)S(1)}, bf16[128,1024]{1,0:T(8,128)(2,1)}, u32[]{:S(2)}) copy-start(bf16[128,1024]{1,0:T(8,128)(2,1)} %cot_ref.1) | copy-start | bytes 786436
  3.0 7.7 %copy-start.6 = (bf16[128,128]{1,0:T(8,128)(2,1)S(1)}, bf16[128,128]{1,0:T(8,128)(2,1)}, u32[]{:S(2)}) copy-start(bf16[128,128]{1,0:T(8,128)(2,1)} %c_ref.1) | copy-start | bytes 98308
  3.0 7.7 %copy-start.7 = (f32[1024]{0:T(1024)S(1)}, f32[1024]{0:T(1024)}, u32[]{:S(2)}) copy-start(f32[1024]{0:T(1024)} %after_ref.1) | copy-start | bytes 12292
  3.1 7.7 %copy-start.9 = (f32[1024]{0:T(1024)S(1)}, f32[1024]{0:T(1024)}, u32[]{:S(2)}) copy-start(f32[1024]{0:T(1024)} %param.27) | copy-start | bytes 12292
  4.1 32.2 %copy-start.10 = (f32[16]{0:T(128)S(1)}, f32[16]{0:T(128)}, u32[]{:S(2)}) copy-start(f32[16]{0:T(128)} %rest_0_.1) | copy-start | bytes 196
  4.1 32.2 %copy-start.11 = (f32[16]{0:T(128)S(1)}, f32[16]{0:T(128)}, u32[]{:S(2)}) copy-start(f32[16]{0:T(128)} %rest_1_.1) | copy-start | bytes 196
  4.1 32.2 %copy-start.12 = (f32[16]{0:T(128)S(1)}, f32[16]{0:T(128)}, u32[]{:S(2)}) copy-start(f32[16]{0:T(128)} %rest_2_.1) | copy-start | bytes 196
  4.1 32.2 %copy-start.13 = (f32[16]{0:T(128)S(1)}, f32[16]{0:T(128)}, u32[]{:S(2)}) copy-start(f32[16]{0:T(128)} %rest_3_.1) | copy-start | bytes 196
  4.1 32.2 %copy-start.14 = (f32[16]{0:T(128)S(1)}, f32[16]{0:T(128)}, u32[]{:S(2)}) copy-start(f32[16]{0:T(128)} %rest_4_.1) | copy-start | bytes 196
  4.1 32.2 %copy-start.15 = (f32[16]{0:T(128)S(1)}, f32[16]{0:T(128)}, u32[]{:S(2)}) copy-start(f32[16]{0:T(128)} %rest_5_.1) | copy-start | bytes 196
  4.1 32.1 %all-to-all-start = ((f32[4,392,128]{2,1,0:T(8,128)}), f32[4,392,128]{2,1,0:T(8,128)S(1)}, u32[]{:S(2)}, u32[]{:S(2)}) async-start(f32[4,392,128]{2,1,0:T(8,128)} %pack_x.1), calls=%async_computation | async-start | bytes 1605632 | tf_op jit(solution)/shard_map/all_to_all | solution.py:474
  12.4 3.4 %copy-start.16 = (f32[648,128]{1,0:T(8,128)}, f32[648,128]{1,0:T(8,128)S(1)}, u32[]{:S(2)}) copy-start(f32[648,128]{1,0:T(8,128)S(1)} %get-tuple-element.33) | copy-start | bytes 995332
  12.4 18.5 %collective-permute-start = (f32[648,128]{1,0:T(8,128)S(1)}, f32[648,128]{1,0:T(8,128)S(1)}, u32[]{:S(2)}, u32[]{:S(2)}) collective-permute-start(f32[648,128]{1,0:T(8,128)S(1)} %get-tuple-element.31), channel_id=1, source_target_pairs={{0,1},{1,2},{2,3},{3,0},{4,5},{5,6},{6,7},{7,4},{8,9},{9,10},{10,1... | collective-permute-start | bytes 995336 | tf_op jit(solution)/shard_map/ppermute | solution.py:479
  38.4 35.8 %all-to-all-start.1 = ((f32[8,72,128]{2,1,0:T(8,128)}), f32[8,72,128]{2,1,0:T(8,128)S(1)}, u32[]{:S(2)}, u32[]{:S(2)}) async-start(f32[8,72,128]{2,1,0:T(8,128)} %get-tuple-element.34), calls=%async_computation.1 | async-start | bytes 589824 | tf_op jit(solution)/shard_map/all_to_all | solution.py:474
  50.8 23.4 %collective-permute-start.1 = (f32[648,128]{1,0:T(8,128)}, f32[648,128]{1,0:T(8,128)S(1)}, u32[]{:S(2)}, u32[]{:S(2)}) collective-permute-start(f32[648,128]{1,0:T(8,128)} %get-tuple-element.32), channel_id=1, source_target_pairs={{0,2},{1,3},{2,0},{3,1},{4,6},{5,7},{6,4},{7,5},{8,10},{9,11},{10,... | collective-permute-start | bytes 995336 | tf_op jit(solution)/shard_map/ppermute | solution.py:479
  52.7 21.5 %collective-permute-start.2 = (f32[648,128]{1,0:T(8,128)}, f32[648,128]{1,0:T(8,128)S(1)}, u32[]{:S(2)}, u32[]{:S(2)}) collective-permute-start(f32[648,128]{1,0:T(8,128)} %copy-done.16), channel_id=1, source_target_pairs={{0,3},{1,0},{2,1},{3,2},{4,7},{5,4},{6,5},{7,6},{8,11},{9,8},{10,9... | collective-permute-start | bytes 995336 | tf_op jit(solution)/shard_map/ppermute | solution.py:479
  74.2 15.0 %copy-start.1 = (f32[648,128]{1,0:T(8,128)S(1)}, f32[648,128]{1,0:T(8,128)}, u32[]{:S(2)}) copy-start(f32[648,128]{1,0:T(8,128)} %copy-done) | copy-start | bytes 995332
  171.2 27.4 %all-to-all-start.7 = ((f32[16,16,128]{2,1,0:T(8,128)}), f32[16,16,128]{2,1,0:T(8,128)S(1)}, u32[]{:S(2)}, u32[]{:S(2)}) async-start(f32[16,16,128]{2,1,0:T(8,128)} %near_sum.1), calls=%async_computation.7 | async-start | bytes 262144 | tf_op jit(solution)/shard_map/all_to_all | solution.py:474
  179.4 12.6 %collective-permute-start.3 = (f32[256,128]{1,0:T(8,128)S(1)}, f32[256,128]{1,0:T(8,128)S(1)}, u32[]{:S(2)}, u32[]{:S(2)}) collective-permute-start(f32[256,128]{1,0:T(8,128)S(1)} %get-tuple-element.47), channel_id=1, source_target_pairs={{0,1},{1,2},{2,3},{3,0},{4,5},{5,6},{6,7},{7,4},{8,9},{9,10},{10,1... | collective-permute-start | bytes 393224 | tf_op jit(solution)/shard_map/ppermute | solution.py:479
  182.6 15.1 %collective-permute-start.4 = (f32[256,128]{1,0:T(8,128)S(1)}, f32[256,128]{1,0:T(8,128)S(1)}, u32[]{:S(2)}, u32[]{:S(2)}) collective-permute-start(f32[256,128]{1,0:T(8,128)S(1)} %get-tuple-element.48), channel_id=1, source_target_pairs={{0,2},{1,3},{2,0},{3,1},{4,6},{5,7},{6,4},{7,5},{8,10},{9,11},{10,... | collective-permute-start | bytes 393224 | tf_op jit(solution)/shard_map/ppermute | solution.py:479
  186.6 11.1 %collective-permute-start.5 = (f32[256,128]{1,0:T(8,128)S(1)}, f32[256,128]{1,0:T(8,128)S(1)}, u32[]{:S(2)}, u32[]{:S(2)}) collective-permute-start(f32[256,128]{1,0:T(8,128)S(1)} %get-tuple-element.49), channel_id=1, source_target_pairs={{0,3},{1,0},{2,1},{3,2},{4,7},{5,4},{6,5},{7,6},{8,11},{9,8},{10,9... | collective-permute-start | bytes 393224 | tf_op jit(solution)/shard_map/ppermute | solution.py:479
  (2 other events, 1.4 us)

commit v3 on v2

--- a/solution.py
+++ b/solution.py
@@ -25,9 +25,10 @@
 NEAR = 32
 FAR = 16
 FIRST = (1,)
-EARLY = (2, 3)
+EARLY = (2,)
+BACK = (2,)
 X_ROWS = CPD + N + HPD + 4
-G_ROWS = 2 * CPD + T + 8
+G_ROWS = 2 * CPD + T
 M_ROWS = 2 * CPS + 8
 VMEM = 16 * 1024 * 1024
 
@@ -54,7 +55,13 @@
     )
 
 
-def pack_x_kernel(x_ref, b_ref, dt_ref, o_ref):
+def pack_x_kernel(x_hbm, b_hbm, dt_hbm, o_ref, x_ref, b_ref, dt_ref, sems):
+    pairs = ((x_hbm, x_ref), (b_hbm, b_ref), (dt_hbm, dt_ref))
+    copies = [pltpu.make_async_copy(src, dst, sems.at[n]) for n, (src, dst) in enumerate(pairs)]
+    for copy in copies:
+        copy.start()
+    for copy in copies:
+        copy.wait()
     for j in range(BLK):
         for i in range(CPD // 128):
             lo = j * CPD + i * 128
@@ -66,22 +73,21 @@
         o_ref[j, at:X_ROWS, :] = jnp.zeros((X_ROWS - at, T), F32)
 
 
-def pack_g_kernel(zl_ref, z_ref, cot_ref, c_ref, gain_ref, dgain_ref, after_ref, *o_refs):
-    del after_ref
-    halves = CPD // 128
-    for d, o_ref in enumerate(o_refs):
+def pack_g_kernel(zl_ref, z_ref, cot_ref, c_ref, *rest):
+    o_refs, made, sems = rest[:BLK], rest[BLK : 2 * BLK], rest[2 * BLK]
+    copies = [pltpu.make_async_copy(made[d], o_refs[d], sems.at[d]) for d in range(BLK)]
+    for d in (*range(1, BLK), 0):
+        o_ref = made[d]
         j = lax.rem(zl_ref[0] + d, BLK)
         for n, ref in enumerate((z_ref, cot_ref)):
-            for i in range(halves):
+            for i in range(CPD // 128):
                 lo = pl.multiple_of(j * CPD + i * 128, 128)
                 at = n * CPD + i * 128
                 o_ref[at : at + 128, :] = ref[:, pl.ds(lo, 128)].astype(F32).T
         o_ref[2 * CPD : 2 * CPD + T, :] = c_ref[...].astype(F32)
-        at = 2 * CPD + T
-        for i in range(halves):
-            o_ref[at + i : at + i + 1, :] = gain_ref[pl.ds(j * halves + i, 1), :]
-            o_ref[at + halves + i : at + halves + i + 1, :] = dgain_ref[pl.ds(j * halves + i, 1), :]
-        o_ref[at + 2 * halves : at + 8, :] = jnp.zeros((8 - 2 * halves, 128), F32)
+        copies[d].start()
+    for copy in copies:
+        copy.wait()
 
 
 def write_message(msg_ref, total, d_total):
@@ -103,16 +109,14 @@
         msg_ref[j, 2 * CPS + 2 : M_ROWS, :] = jnp.zeros((M_ROWS - 2 * CPS - 2, T), F32)
 
 
-def state_kernel(zl_ref, *rest):
-    prm, r_ref = rest[:PARAMS], rest[PARAMS]
-    table_ref, cols_ref, s_ref, msg_ref = rest[-4:]
+def state_kernel(prm_ref, r_ref, *rest):
+    table_ref, s_ref, msg_ref = rest[-3:]
     at = CPD + N
     raw = jnp.concatenate([r_ref[b, at : at + HPD, :] for b in range(BLK)], axis=0)
 
-    def head_values(ref):
-        return jnp.concatenate([jnp.full((1, T), ref[zl_ref[0] * HPD + h], F32) for h in range(HPD)] * BLK, axis=0)
-
-    a_log, dt_bias, d_skip, p_a, p_dt, p_skip = [head_values(ref) for ref in prm]
+    a_log, dt_bias, d_skip, p_a, p_dt, p_skip = [
+        jnp.concatenate([prm_ref[k * HPD : (k + 1) * HPD, :]] * BLK, axis=0) for k in range(PARAMS)
+    ]
     pre = raw + dt_bias
     dt = jnp.maximum(pre, 0.0) + jnp.log1p(jnp.exp(-jnp.abs(pre)))
     sg = 1.0 / (1.0 + jnp.exp(-pre))
@@ -147,9 +151,6 @@
         (K_D, d_skip), (K_DD, p_skip),
     ):
         table_ref[k] = v
-    cols_ref[...] = jnp.concatenate(
-        [c, dc, dt, ddt, jnp.zeros((T - 4 * ROWS, T), F32)], axis=0
-    ).T
     total = jnp.zeros((CPD, N), F32)
     d_total = jnp.zeros((CPD, N), F32)
     for b in range(BLK):
@@ -184,12 +185,11 @@
     scan_kernel(False, m_ref, m_ref, rest[-1])
 
 
-def gains(g_ref):
-    at = 2 * CPD + T
+def gains(zl_ref, *refs):
     halves = CPD // 128
     out = []
-    for n in range(2):
-        rows = [g_ref[0, at + n * halves + i : at + n * halves + i + 1, :] for i in range(halves)]
+    for ref in refs:
+        rows = [ref[pl.ds(zl_ref[0] * halves + i, 1), :] for i in range(halves)]
         out.append(jnp.concatenate([jnp.broadcast_to(v, (T, 128)).T for v in rows], axis=0))
     return out
 
@@ -204,12 +204,18 @@
     return jnp.where(causal, scores * jnp.exp(jnp.where(causal, gap, 0.0)), 0.0), d_gap
 
 
+def columns(table):
+    rows = [table[k] for k in (K_C, K_DC, K_DT, K_DDT)]
+    return jnp.concatenate(rows + [jnp.zeros((T - 4 * ROWS, T), F32)], axis=0).T
+
+
 def causal_mask():
     return lax.broadcasted_iota(jnp.int32, (T, T), 0) <= lax.broadcasted_iota(jnp.int32, (T, T), 1)
 
 
 def out_kernel(
-    zl_ref, r_ref, g0, g1, g2, g3, h_ref, table_ref, cols_ref, s_ref, g_ref, y_ref, hb_ref, msg_ref, sems
+    zl_ref, gain_in, dgain_in, r_ref, g0, g1, g2, g3, h_ref, table_ref, s_ref,
+    g_ref, y_ref, hb_ref, msg_ref, sems,
 ):
     copies = []
     for d, src in enumerate((g0, g1, g2, g3)):
@@ -219,7 +225,8 @@
     for copy in copies:
         copy.wait()
     causal = causal_mask()
-    gain, dgain = gains(g_ref)
+    cols = columns(table_ref)
+    gain, dgain = gains(zl_ref, gain_in, dgain_in)
     h = h_ref[:, 0:CPS, :].reshape(CPD, N)
     dh = h_ref[:, CPS : 2 * CPS, :].reshape(CPD, N)
     for b in range(BLK):
@@ -236,9 +243,9 @@
         y_parts, dy_parts = [], []
         for i in range(HPD):
             r = b * HPD + i
-            mat, d_gap = decays(table_ref, cols_ref, r, scores, causal)
-            dt = cols_ref[:, 2 * ROWS + r : 2 * ROWS + r + 1]
-            ddt = cols_ref[:, 3 * ROWS + r : 3 * ROWS + r + 1]
+            mat, d_gap = decays(table_ref, cols, r, scores, causal)
+            dt = cols[:, 2 * ROWS + r : 2 * ROWS + r + 1]
+            ddt = cols[:, 3 * ROWS + r : 3 * ROWS + r + 1]
             w = mat * dt
             dw = mat * (d_gap * dt + ddt)
             w_hi, w_lo = split(jnp.concatenate([w, dw], axis=1))
@@ -267,8 +274,10 @@
         h = eg * h + s_ref[b, 0]
 
 
-def seed_kernel(r_ref, g_ref, n_ref, table_ref, y_ref, yb_ref, seed_ref, gain_ref, msg_ref):
-    gain, dgain = gains(g_ref)
+def seed_kernel(
+    zl_ref, gain_in, dgain_in, r_ref, g_ref, n_ref, table_ref, y_ref, yb_ref, seed_ref, gain_ref, msg_ref
+):
+    gain, dgain = gains(zl_ref, gain_in, dgain_in)
     sums = n_ref[0] + n_ref[1] + n_ref[2] + n_ref[3]
     acc = jnp.zeros((CPD, T), F32)
     adj = jnp.zeros((CPD, N), F32)
@@ -315,10 +324,11 @@
 
 
 def input_kernel(
-    zl_ref, r_ref, g_ref, l_ref, table_ref, cols_ref, y_ref, yb_ref, hb_ref, seed_ref, gain_ref, *rest
+    zl_ref, r_ref, g_ref, l_ref, table_ref, y_ref, yb_ref, hb_ref, seed_ref, gain_ref, *rest
 ):
     o_refs, part_ref, o_ref, sems = rest[:BLK], rest[BLK], rest[BLK + 1], rest[BLK + 2]
     causal = causal_mask()
+    cols = columns(table_ref)
     adj = l_ref[:, 0:CPS, :].reshape(CPD, N)
     d_adj = l_ref[:, CPS : 2 * CPS, :].reshape(CPD, N)
     acc_a = [jnp.zeros((1, T), F32) for _ in range(HPD)]
@@ -339,7 +349,7 @@
             def row(k):
                 return table_ref[k, r : r + 1, :]
 
-            mat, d_gap = decays(table_ref, cols_ref, r, scores, causal)
+            mat, d_gap = decays(table_ref, cols, r, scores, causal)
             l_hi, l_lo = split(mat)
             n_hi, n_lo = split(mat * d_gap)
             yb, dyb = yb_ref[0, b, rows, :], yb_ref[1, b, rows, :]
@@ -408,7 +418,8 @@
         copy.wait()
 
 
-def sum_kernel(m_ref, o_ref):
+def sum_kernel(m_ref, *rest):
+    o_ref = rest[-1]
     total = m_ref[0]
     for i in range(1, NEAR):
         total = total + m_ref[i]
@@ -470,6 +481,9 @@
 ):
     vm, sm, hbm = [pl.BlockSpec(memory_space=m) for m in (pltpu.VMEM, pltpu.SMEM, pltpu.HBM)]
 
+    def in_hbm(v):
+        return pltpu.with_memory_space_constraint(v, pltpu.HBM)
+
     def exchange(v, axes):
         return lax.all_to_all(v, axes, 0, 0)
 
@@ -479,18 +493,25 @@
         return lax.ppermute(v, group, [(i, (i + d) % BLK) for i in range(BLK)])
 
     zl = lax.axis_index(group).reshape(1)
-    packed = call(pack_x_kernel, "pack_x", (BLK, X_ROWS, T))(ssm_input, b_proj, dt_raw.T)
+    params = jnp.stack([a_log, dt_bias, d_skip, probe_a, probe_dt, probe_skip])
+    params = lax.dynamic_slice_in_dim(params, lax.axis_index(group) * HPD, HPD, 1)
+    params = jnp.broadcast_to(params.reshape(PARAMS * HPD, 1), (PARAMS * HPD, T))
+    gain = (norm_gain.reshape(8, 128), probe_gain.reshape(8, 128))
+    packed = call(pack_x_kernel, "pack_x", (BLK, X_ROWS, T), [hbm] * 3,
+        [pltpu.VMEM((T, CH), BF16), pltpu.VMEM((T, N), BF16), pltpu.VMEM((HEADS, T), F32)]
+        + [pltpu.SemaphoreType.DMA((3,))],
+    )(*[in_hbm(v) for v in (ssm_input, b_proj, dt_raw.T)])
     r = exchange(packed, group)
-    parts = call(pack_g_kernel, "pack_g", [(G_ROWS, T)] * BLK, [sm] + [vm] * 5 + [hbm])(
-        zl, gate_input, cotangent, c_proj, norm_gain.reshape(8, 128), probe_gain.reshape(8, 128), norm_gain
-    )
+    parts = call(pack_g_kernel, "pack_g", [(G_ROWS, T)] * BLK, [sm] + [vm] * 3,
+        [pltpu.VMEM((G_ROWS, T), F32)] * BLK + [pltpu.SemaphoreType.DMA((BLK,))], [hbm] * BLK,
+    )(zl, gate_input, cotangent, c_proj)
     parts = [shift(v, d) if d else v for d, v in enumerate(parts)]
-    table, cols, s, msg = call(
+    table, s, msg = call(
         state_kernel,
         "state",
-        [(TABLE, ROWS, T), (T, T), (BLK, 2, CPD, N), (SEGS, M_ROWS, N)],
-        [sm] * (1 + PARAMS) + [vm] + [hbm] * len(FIRST),
-    )(zl, a_log, dt_bias, d_skip, probe_a, probe_dt, probe_skip, r, *[parts[d] for d in FIRST])
+        [(TABLE, ROWS, T), (BLK, 2, CPD, N), (SEGS, M_ROWS, N)],
+        [vm, vm] + [hbm] * len(FIRST),
+    )(params, r, *[parts[d] for d in FIRST])
     decay = exchange(msg, segs)
     early = [parts[d] for d in EARLY]
     before = call(scan_up_kernel, "scan_up", (SEGS, 2 * CPS, N), [vm] + [hbm] * len(early))(decay, *early)
@@ -499,15 +520,16 @@
         out_kernel,
         "mix",
         [(BLK, G_ROWS, T), (2, BLK, CPD, T), (BLK, 2, CPD, N), (BLK, 4 * BLK, T)],
-        [sm, vm] + [hbm] * BLK + [vm] * 4,
+        [sm] + [vm] * 3 + [hbm] * BLK + [vm] * 3,
         [pltpu.SemaphoreType.DMA((BLK,))],
-    )(zl, r, *parts, h_in, table, cols, s)
+    )(zl, *gain, r, *[in_hbm(v) for v in parts], h_in, table, s)
     norms = exchange(norms, group)
     y_bar, seeds, d_gain, msg = call(
         seed_kernel,
         "seeds",
         [(2, BLK, CPD, T), (BLK, 2, CPD, N), (2, 128), (SEGS, 2 * CPS, N)],
-    )(r, g, norms, table, y)
+        [sm] + [vm] * 7,
+    )(zl, *gain, r, g, norms, table, y)
     after = call(functools.partial(scan_kernel, True), "scan_down", (SEGS, 2 * CPS, N))(
         decay, exchange(msg, segs)
     )
@@ -516,12 +538,14 @@
         input_kernel,
         "input_grad",
         [(CPD, 128)] * BLK + [(NEAR, 4 * HPD, T)],
-        [sm] + [vm] * 10,
+        [sm] + [vm] * 9,
         [pltpu.VMEM((BLK, CPD, 128), F32), pltpu.SemaphoreType.DMA((BLK,))],
         [hbm] * BLK + [vm],
-    )(zl, r, g, adj, table, cols, y, y_bar, h_blocks, seeds, d_gain)
+    )(zl, r, g, adj, table, y, y_bar, h_blocks, seeds, d_gain)
     outs = [shift(v, d) if d else v for d, v in enumerate(outs)]
-    part = call(sum_kernel, "near_sum", (FAR, 4 * HPD, T))(exchange(part, ("x", "core", "y")))
+    part = exchange(part, ("x", "core", "y"))
+    early = [outs[d] for d in BACK]
+    part = call(sum_kernel, "near_sum", (FAR, 4 * HPD, T), [vm] + [hbm] * len(early))(part, *early)
     hvp_input = call(
         place_kernel,
         "place",

time: 201 us -> 194 us (0.965)
  blocking collectives: 89.3 us -> 51.8 us
  waiting for transfers between devices: 48.1 us -> 69.6 us
  starting transfers between devices: 44.6 us -> 53.6 us
  Pallas kernels: 13.3 us -> 15.5 us
    all_to_all x5 -> x3, blocking collectives: 89.3 us -> 51.8 us  [exchange(): return lax.all_to_all(v, axes, 0, 0)]
    ppermute x6, waiting for transfers between devices: 42.7 us -> 54.2 us  [shift(): return lax.ppermute(v, group, [(i, (i + d) % BLK) for i in range(BLK)])]
    all_to_all x3 -> x5, waiting for transfers between devices: 5.43 us -> 15.3 us  [exchange(): return lax.all_to_all(v, axes, 0, 0)]
    all_to_all x3 -> x5, starting transfers between devices: 27 us -> 36 us  [exchange(): return lax.all_to_all(v, axes, 0, 0)]
    pallas_call x11, Pallas kernels: 13.3 us -> 15.5 us  [run(): pl.pallas_call(kernel, name=name, out_shape=[shape(o) for o in outs] if m...]
  transfers between devices with their start and end apart: 9 -> 11, of which waited for: 5 -> 9; matrix products, arithmetic and copies ran while one was open for 0% -> 0% of each run, Pallas kernels for 1% -> 1%
where the time goes in v3:
time: 194 us; the launch traced here: 193 us
  waiting for transfers between devices  69.6 us (36%)
  starting transfers between devices  53.6 us (28%)
  blocking collectives  51.8 us (27%)
  Pallas kernels  15.5 us (8%)
    ppermute x6, waiting for transfers between devices, shift(): return lax.ppermute(v, group, [(i, (i + d) % BLK) for i in range(BLK)])  54.2 us
    all_to_all x3, blocking collectives, exchange(): return lax.all_to_all(v, axes, 0, 0)  51.8 us
    all_to_all x5, starting transfers between devices, exchange(): return lax.all_to_all(v, axes, 0, 0)  36 us
    ppermute x6, starting transfers between devices, shift(): return lax.ppermute(v, group, [(i, (i + d) % BLK) for i in range(BLK)])  17.6 us
    pallas_call x11, Pallas kernels, run(): pl.pallas_call(kernel, name=name, out_shape=[shape(o) for o in outs] if m...  15.5 us
    all_to_all x5, waiting for transfers between devices, exchange(): return lax.all_to_all(v, axes, 0, 0)  15.3 us
  transfers between devices with their start and end apart: 11, of which 9 were waited for; matrix products, arithmetic and copies ran while one was open for 0% of the time, Pallas kernels for 1%

profile of v3, /device:TPU:1, one launch (start us, length us, event | category | flops | bytes accessed | tf_op | source)
XLA Modules:
  0.0 193.2 jit_solution(11676225522932286918)
XLA Ops:
  0.7 2.1 %pack_x.1 = f32[4,392,128]{2,1,0:T(8,128)} custom-call(bf16[128,1024]{1,0:T(8,128)(2,1)} %x_hbm.1, bf16[128,128]{1,0:T(8,128)(2,1)} %b_hbm.1, f32[16,128]{1,0:T(8,128)} %bitcast.18), custom_call_target="tpu_custom_call" | custom-call | tf_op jit(solution)/shard_map/pack_x/pallas_call | solution.py:453
  2.8 6.6 %all-to-all-start = ((f32[4,392,128]{2,1,0:T(8,128)}), f32[4,392,128]{2,1,0:T(8,128)S(1)}, u32[]{:S(2)}, u32[]{:S(2)}) async-start(f32[4,392,128]{2,1,0:T(8,128)} %pack_x.1), calls=%async_computation | async-start | bytes 1605632 | tf_op jit(solution)/shard_map/all_to_all | solution.py:488
  11.8 3.4 %collective-permute-start = (f32[640,128]{1,0:T(8,128)S(1)}, f32[640,128]{1,0:T(8,128)S(1)}, u32[]{:S(2)}, u32[]{:S(2)}) collective-permute-start(f32[640,128]{1,0:T(8,128)S(1)} %get-tuple-element.30), channel_id=1, source_target_pairs={{0,1},{1,2},{2,3},{3,0},{4,5},{5,6},{6,7},{7,4},{8,9},{9,10},{10,1... | collective-permute-start | bytes 983048 | tf_op jit(solution)/shard_map/ppermute | solution.py:493
  15.4 14.0 %collective-permute-done.rest_0_.g1 = f32[640,128]{1,0:T(8,128)S(1)} collective-permute-done((f32[640,128]{1,0:T(8,128)S(1)}, f32[640,128]{1,0:T(8,128)S(1)}, u32[]{:S(2)}, u32[]{:S(2)}) %collective-permute-start) | collective-permute-done | bytes 327712 | tf_op jit(solution)/shard_map/ppermute | solution.py:493
  29.4 5.4 %all-to-all-done.r_ref = f32[4,392,128]{2,1,0:T(8,128)S(1)} async-done(((f32[4,392,128]{2,1,0:T(8,128)}), f32[4,392,128]{2,1,0:T(8,128)S(1)}, u32[]{:S(2)}, u32[]{:S(2)}) %all-to-all-start) | async-done | bytes 802848 | tf_op jit(solution)/shard_map/all_to_all | solution.py:488
  36.4 12.3 %all-to-all-start.1 = ((f32[8,72,128]{2,1,0:T(8,128)}), f32[8,72,128]{2,1,0:T(8,128)S(1)}, u32[]{:S(2)}, u32[]{:S(2)}) async-start(f32[8,72,128]{2,1,0:T(8,128)} %get-tuple-element.33), calls=%async_computation.1 | async-start | bytes 589824 | tf_op jit(solution)/shard_map/all_to_all | solution.py:488
  48.8 1.9 collective-permute-start.1
  50.7 21.3 %collective-permute-done.1.rest_0_.g2 = f32[640,128]{1,0:T(8,128)S(1)} collective-permute-done((f32[640,128]{1,0:T(8,128)}, f32[640,128]{1,0:T(8,128)S(1)}, u32[]{:S(2)}, u32[]{:S(2)}) %collective-permute-start.1) | collective-permute-done | bytes 327712 | tf_op jit(solution)/shard_map/ppermute | solution.py:493
  72.7 3.7 %all-to-all-start.2 = ((f32[8,64,128]{2,1,0:T(8,128)}), f32[8,64,128]{2,1,0:T(8,128)S(1)}, u32[]{:S(2)}, u32[]{:S(2)}) async-start(f32[8,64,128]{2,1,0:T(8,128)} %scan_up.1), calls=%async_computation.2 | async-start | bytes 524288 | tf_op jit(solution)/shard_map/all_to_all | solution.py:488
  76.4 3.4 %collective-permute-start.2 = (f32[640,128]{1,0:T(8,128)S(1)}, f32[640,128]{1,0:T(8,128)}, u32[]{:S(2)}, u32[]{:S(2)}) collective-permute-start(f32[640,128]{1,0:T(8,128)S(1)} %get-tuple-element.32), channel_id=1, source_target_pairs={{0,3},{1,0},{2,1},{3,2},{4,7},{5,4},{6,5},{7,6},{8,11},{9,8},{10,9... | collective-permute-start | bytes 983048 | tf_op jit(solution)/shard_map/ppermute | solution.py:493
  79.8 5.8 %collective-permute-done.2.g3 = f32[640,128]{1,0:T(8,128)} collective-permute-done((f32[640,128]{1,0:T(8,128)S(1)}, f32[640,128]{1,0:T(8,128)}, u32[]{:S(2)}, u32[]{:S(2)}) %collective-permute-start.2) | collective-permute-done | bytes 327712 | tf_op jit(solution)/shard_map/ppermute | solution.py:493
  85.6 9.4 %all-to-all-done.2.h_ref = f32[8,64,128]{2,1,0:T(8,128)S(1)} async-done(((f32[8,64,128]{2,1,0:T(8,128)}), f32[8,64,128]{2,1,0:T(8,128)S(1)}, u32[]{:S(2)}, u32[]{:S(2)}) %all-to-all-start.2) | async-done | bytes 262176 | tf_op jit(solution)/shard_map/all_to_all | solution.py:488
  95.0 3.2 %mix.1 = (f32[4,640,128]{2,1,0:T(8,128)S(1)}, f32[2,4,256,128]{3,2,1,0:T(8,128)S(1)}, f32[4,2,256,128]{3,2,1,0:T(8,128)S(1)}, f32[4,16,128]{2,1,0:T(8,128)S(1)}) custom-call(s32[1]{0:T(128)} %bitcast.zl_ref, f32[8,128]{1,0:T(8,128)S(1)} %bitcast.14, f32[8,128]{1,0:T(8,128)S(1)} %bitcast.16, f32[4,392,128]{2,1,0:T(8,128)S(1)} %all-to-all-done.r_ref, ...), custom_call_target="tpu_custom_call" | custom-call | tf_op jit(solution)/shard_map/mix/pallas_call | solution.py:453
  98.3 6.9 %all_to_all.40.n_ref = f32[4,16,128]{2,1,0:T(8,128)S(1)} all-to-all(f32[4,16,128]{2,1,0:T(8,128)S(1)} %get-tuple-element.37), channel_id=1, replica_groups=mesh['zhi'=2,'x'=4,'core'=2,'y'=4,'zh'=2,'zl'=4] {'zl'}, dimensions={0} | all-to-all | bytes 65536 | tf_op jit(solution)/shard_map/all_to_all | solution.py:488
  106.1 27.1 %all_to_all.41.m_ref = f32[8,64,128]{2,1,0:T(8,128)S(1)} all-to-all(f32[8,64,128]{2,1,0:T(8,128)S(1)} %get-tuple-element.39), channel_id=1, replica_groups=mesh['zhi'=2,'x'=4,'core'=2,'y'=4,'zh'=2,'zl'=4] {'y','zh'}, dimensions={0} | all-to-all | bytes 524288 | tf_op jit(solution)/shard_map/all_to_all | solution.py:488
  133.3 17.9 %all_to_all.42.l_ref = f32[8,64,128]{2,1,0:T(8,128)S(1)} all-to-all(f32[8,64,128]{2,1,0:T(8,128)S(1)} %scan_down.1), channel_id=1, replica_groups=mesh['zhi'=2,'x'=4,'core'=2,'y'=4,'zh'=2,'zl'=4] {'y','zh'}, dimensions={0} | all-to-all | bytes 524288 | tf_op jit(solution)/shard_map/all_to_all | solution.py:488
  151.2 3.8 %input_grad.1 = (f32[256,128]{1,0:T(8,128)S(1)}, f32[256,128]{1,0:T(8,128)S(1)}, f32[256,128]{1,0:T(8,128)S(1)}, f32[256,128]{1,0:T(8,128)S(1)}, f32[32,16,128]{2,1,0:T(8,128)}) custom-call(s32[1]{0:T(128)} %bitcast.zl_ref, f32[4,392,128]{2,1,0:T(8,128)S(1)} %all-to-all-done.r_ref, f32[4,640,128]{2,1,0:T(8,128)S(1)} %get-tuple-element.36.g_ref, ...), custom_call_target="tpu_custom_call" | custom-call | tf_op jit(solution)/shard_map/input_grad/pallas_call | solution.py:453
  155.0 5.2 %all-to-all-start.6 = ((f32[32,16,128]{2,1,0:T(8,128)}), f32[32,16,128]{2,1,0:T(8,128)S(1)}, u32[]{:S(2)}, u32[]{:S(2)}) async-start(f32[32,16,128]{2,1,0:T(8,128)} %get-tuple-element.48), calls=%async_computation.6 | async-start | bytes 524288 | tf_op jit(solution)/shard_map/all_to_all | solution.py:488
  160.3 1.9 collective-permute-start.4
  162.2 6.4 %collective-permute-done.4.i2.rest_0_ = f32[256,128]{1,0:T(8,128)S(1)} collective-permute-done((f32[256,128]{1,0:T(8,128)S(1)}, f32[256,128]{1,0:T(8,128)S(1)}, u32[]{:S(2)}, u32[]{:S(2)}) %collective-permute-start.4) | collective-permute-done | bytes 131104 | tf_op jit(solution)/shard_map/ppermute | solution.py:493
  169.7 8.1 %all-to-all-start.7 = ((f32[16,16,128]{2,1,0:T(8,128)}), f32[16,16,128]{2,1,0:T(8,128)S(1)}, u32[]{:S(2)}, u32[]{:S(2)}) async-start(f32[16,16,128]{2,1,0:T(8,128)} %near_sum.1), calls=%async_computation.7 | async-start | bytes 262144 | tf_op jit(solution)/shard_map/all_to_all | solution.py:488
  177.9 3.3 %collective-permute-start.3 = (f32[256,128]{1,0:T(8,128)S(1)}, f32[256,128]{1,0:T(8,128)S(1)}, u32[]{:S(2)}, u32[]{:S(2)}) collective-permute-start(f32[256,128]{1,0:T(8,128)S(1)} %get-tuple-element.45), channel_id=1, source_target_pairs={{0,1},{1,2},{2,3},{3,0},{4,5},{5,6},{6,7},{7,4},{8,9},{9,10},{10,1... | collective-permute-start | bytes 393224 | tf_op jit(solution)/shard_map/ppermute | solution.py:493
  181.1 3.8 %collective-permute-start.5 = (f32[256,128]{1,0:T(8,128)S(1)}, f32[256,128]{1,0:T(8,128)S(1)}, u32[]{:S(2)}, u32[]{:S(2)}) collective-permute-start(f32[256,128]{1,0:T(8,128)S(1)} %get-tuple-element.47), channel_id=1, source_target_pairs={{0,3},{1,0},{2,1},{3,2},{4,7},{5,4},{6,5},{7,6},{8,11},{9,8},{10,9... | collective-permute-start | bytes 393224 | tf_op jit(solution)/shard_map/ppermute | solution.py:493
  184.9 5.5 %collective-permute-done.3.i1 = f32[256,128]{1,0:T(8,128)S(1)} collective-permute-done((f32[256,128]{1,0:T(8,128)S(1)}, f32[256,128]{1,0:T(8,128)S(1)}, u32[]{:S(2)}, u32[]{:S(2)}) %collective-permute-start.3) | collective-permute-done | bytes 131104 | tf_op jit(solution)/shard_map/ppermute | solution.py:493
  (46 shorter events, 9.9 us)
Async XLA Ops:
  0.6 8.8 %copy-start.3 = (bf16[128,1024]{1,0:T(8,128)(2,1)S(1)}, bf16[128,1024]{1,0:T(8,128)(2,1)}, u32[]{:S(2)}) copy-start(bf16[128,1024]{1,0:T(8,128)(2,1)} %z_ref.1) | copy-start | bytes 786436
  0.6 8.7 %copy-start.4 = (bf16[128,1024]{1,0:T(8,128)(2,1)S(1)}, bf16[128,1024]{1,0:T(8,128)(2,1)}, u32[]{:S(2)}) copy-start(bf16[128,1024]{1,0:T(8,128)(2,1)} %cot_ref.1) | copy-start | bytes 786436
  0.7 8.7 %copy-start.5 = (bf16[128,128]{1,0:T(8,128)(2,1)S(1)}, bf16[128,128]{1,0:T(8,128)(2,1)}, u32[]{:S(2)}) copy-start(bf16[128,128]{1,0:T(8,128)(2,1)} %c_ref.1) | copy-start | bytes 98308
  2.7 12.4 %copy-start.9 = (f32[16]{0:T(128)S(1)}, f32[16]{0:T(128)}, u32[]{:S(2)}) copy-start(f32[16]{0:T(128)} %param.20) | copy-start | bytes 196
  2.7 12.4 %copy-start.10 = (f32[16]{0:T(128)S(1)}, f32[16]{0:T(128)}, u32[]{:S(2)}) copy-start(f32[16]{0:T(128)} %param.21) | copy-start | bytes 196
  2.8 12.4 %copy-start.11 = (f32[16]{0:T(128)S(1)}, f32[16]{0:T(128)}, u32[]{:S(2)}) copy-start(f32[16]{0:T(128)} %param.22) | copy-start | bytes 196
  2.8 12.4 %copy-start.12 = (f32[16]{0:T(128)S(1)}, f32[16]{0:T(128)}, u32[]{:S(2)}) copy-start(f32[16]{0:T(128)} %param.24) | copy-start | bytes 196
  2.8 12.4 %copy-start.13 = (f32[16]{0:T(128)S(1)}, f32[16]{0:T(128)}, u32[]{:S(2)}) copy-start(f32[16]{0:T(128)} %param.25) | copy-start | bytes 196
  2.8 12.4 %copy-start.14 = (f32[16]{0:T(128)S(1)}, f32[16]{0:T(128)}, u32[]{:S(2)}) copy-start(f32[16]{0:T(128)} %param.26) | copy-start | bytes 196
  2.8 32.1 %all-to-all-start = ((f32[4,392,128]{2,1,0:T(8,128)}), f32[4,392,128]{2,1,0:T(8,128)S(1)}, u32[]{:S(2)}, u32[]{:S(2)}) async-start(f32[4,392,128]{2,1,0:T(8,128)} %pack_x.1), calls=%async_computation | async-start | bytes 1605632 | tf_op jit(solution)/shard_map/all_to_all | solution.py:488
  11.8 17.7 %collective-permute-start = (f32[640,128]{1,0:T(8,128)S(1)}, f32[640,128]{1,0:T(8,128)S(1)}, u32[]{:S(2)}, u32[]{:S(2)}) collective-permute-start(f32[640,128]{1,0:T(8,128)S(1)} %get-tuple-element.30), channel_id=1, source_target_pairs={{0,1},{1,2},{2,3},{3,0},{4,5},{5,6},{6,7},{7,4},{8,9},{9,10},{10,1... | collective-permute-start | bytes 983048 | tf_op jit(solution)/shard_map/ppermute | solution.py:493
  29.4 43.3 %copy-start.1 = (f32[640,128]{1,0:T(8,128)}, f32[640,128]{1,0:T(8,128)S(1)}, u32[]{:S(2)}) copy-start(f32[640,128]{1,0:T(8,128)S(1)} %collective-permute-done.rest_0_.g1) | copy-start | bytes 983044
  34.9 60.1 %copy-start.6 = (f32[1024]{0:T(1024)S(1)}, f32[1024]{0:T(1024)}, u32[]{:S(2)}) copy-start(f32[1024]{0:T(1024)} %param.23) | copy-start | bytes 12292
  34.9 60.1 %copy-start.7 = (f32[1024]{0:T(1024)S(1)}, f32[1024]{0:T(1024)}, u32[]{:S(2)}) copy-start(f32[1024]{0:T(1024)} %param.27) | copy-start | bytes 12292
  36.4 35.5 %all-to-all-start.1 = ((f32[8,72,128]{2,1,0:T(8,128)}), f32[8,72,128]{2,1,0:T(8,128)S(1)}, u32[]{:S(2)}, u32[]{:S(2)}) async-start(f32[8,72,128]{2,1,0:T(8,128)} %get-tuple-element.33), calls=%async_computation.1 | async-start | bytes 589824 | tf_op jit(solution)/shard_map/all_to_all | solution.py:488
  48.8 23.2 %collective-permute-start.1 = (f32[640,128]{1,0:T(8,128)}, f32[640,128]{1,0:T(8,128)S(1)}, u32[]{:S(2)}, u32[]{:S(2)}) collective-permute-start(f32[640,128]{1,0:T(8,128)} %copy-done.8), channel_id=1, source_target_pairs={{0,2},{1,3},{2,0},{3,1},{4,6},{5,7},{6,4},{7,5},{8,10},{9,11},{10,... | collective-permute-start | bytes 983048 | tf_op jit(solution)/shard_map/ppermute | solution.py:493
  71.9 23.1 %copy-start = (f32[640,128]{1,0:T(8,128)}, f32[640,128]{1,0:T(8,128)S(1)}, u32[]{:S(2)}) copy-start(f32[640,128]{1,0:T(8,128)S(1)} %collective-permute-done.1.rest_0_.g2) | copy-start | bytes 983044
  72.7 22.3 %all-to-all-start.2 = ((f32[8,64,128]{2,1,0:T(8,128)}), f32[8,64,128]{2,1,0:T(8,128)S(1)}, u32[]{:S(2)}, u32[]{:S(2)}) async-start(f32[8,64,128]{2,1,0:T(8,128)} %scan_up.1), calls=%async_computation.2 | async-start | bytes 524288 | tf_op jit(solution)/shard_map/all_to_all | solution.py:488
  76.4 9.2 %collective-permute-start.2 = (f32[640,128]{1,0:T(8,128)S(1)}, f32[640,128]{1,0:T(8,128)}, u32[]{:S(2)}, u32[]{:S(2)}) collective-permute-start(f32[640,128]{1,0:T(8,128)S(1)} %get-tuple-element.32), channel_id=1, source_target_pairs={{0,3},{1,0},{2,1},{3,2},{4,7},{5,4},{6,5},{7,6},{8,11},{9,8},{10,9... | collective-permute-start | bytes 983048 | tf_op jit(solution)/shard_map/ppermute | solution.py:493
  155.0 14.1 %all-to-all-start.6 = ((f32[32,16,128]{2,1,0:T(8,128)}), f32[32,16,128]{2,1,0:T(8,128)S(1)}, u32[]{:S(2)}, u32[]{:S(2)}) async-start(f32[32,16,128]{2,1,0:T(8,128)} %get-tuple-element.48), calls=%async_computation.6 | async-start | bytes 524288 | tf_op jit(solution)/shard_map/all_to_all | solution.py:488
  160.3 8.3 %collective-permute-start.4 = (f32[256,128]{1,0:T(8,128)S(1)}, f32[256,128]{1,0:T(8,128)S(1)}, u32[]{:S(2)}, u32[]{:S(2)}) collective-permute-start(f32[256,128]{1,0:T(8,128)S(1)} %get-tuple-element.46), channel_id=1, source_target_pairs={{0,2},{1,3},{2,0},{3,1},{4,6},{5,7},{6,4},{7,5},{8,10},{9,11},{10,... | collective-permute-start | bytes 393224 | tf_op jit(solution)/shard_map/ppermute | solution.py:493
  169.7 22.8 %all-to-all-start.7 = ((f32[16,16,128]{2,1,0:T(8,128)}), f32[16,16,128]{2,1,0:T(8,128)S(1)}, u32[]{:S(2)}, u32[]{:S(2)}) async-start(f32[16,16,128]{2,1,0:T(8,128)} %near_sum.1), calls=%async_computation.7 | async-start | bytes 262144 | tf_op jit(solution)/shard_map/all_to_all | solution.py:488
  177.9 12.6 %collective-permute-start.3 = (f32[256,128]{1,0:T(8,128)S(1)}, f32[256,128]{1,0:T(8,128)S(1)}, u32[]{:S(2)}, u32[]{:S(2)}) collective-permute-start(f32[256,128]{1,0:T(8,128)S(1)} %get-tuple-element.45), channel_id=1, source_target_pairs={{0,1},{1,2},{2,3},{3,0},{4,5},{5,6},{6,7},{7,4},{8,9},{9,10},{10,1... | collective-permute-start | bytes 393224 | tf_op jit(solution)/shard_map/ppermute | solution.py:493
  181.1 10.6 %collective-permute-start.5 = (f32[256,128]{1,0:T(8,128)S(1)}, f32[256,128]{1,0:T(8,128)S(1)}, u32[]{:S(2)}, u32[]{:S(2)}) collective-permute-start(f32[256,128]{1,0:T(8,128)S(1)} %get-tuple-element.47), channel_id=1, source_target_pairs={{0,3},{1,0},{2,1},{3,2},{4,7},{5,4},{6,5},{7,6},{8,11},{9,8},{10,9... | collective-permute-start | bytes 393224 | tf_op jit(solution)/shard_map/ppermute | solution.py:493
  (2 other events, 1.5 us)

commit v4 on v3

--- a/solution.py
+++ b/solution.py
@@ -22,6 +22,7 @@
 SEGS = 8
 CPS = CPD // SEGS
 PARAMS = 6
+PART = 8
 NEAR = 32
 FAR = 16
 FIRST = (1,)
@@ -172,7 +173,8 @@
 def scan_kernel(reverse, decay_ref, m_ref, o_ref):
     total = jnp.zeros((CPS, N), F32)
     d_total = jnp.zeros((CPS, N), F32)
-    for i in range(SEGS - 1, -1, -1) if reverse else range(SEGS):
+    for n in range(SEGS - 1, -1, -1) if reverse else range(SEGS):
+        i = n % 2 * (SEGS // 2) + n // 2
         o_ref[i, 0:CPS, :] = total
         o_ref[i, CPS : 2 * CPS, :] = d_total
         eg = jnp.exp(decay_ref[i, 2 * CPS : 2 * CPS + 1, :])
@@ -391,7 +393,9 @@
             eg = jnp.exp(heads_rows(table_ref, K_G, b))
             d_adj = eg * (d_adj + heads_rows(table_ref, K_DG, b) * adj) + seed_ref[b, 1]
             adj = eg * adj + seed_ref[b, 0]
-    part = jnp.concatenate(acc_a + acc_dt + acc_skip + [gain_ref[...], jnp.zeros((2, T), F32)], axis=0)
+    sums = jnp.concatenate(acc_a + acc_dt + acc_skip + [jnp.zeros((T - 3 * HPD, T), F32)], axis=0)
+    sums = jnp.sum(sums.T, axis=0, keepdims=True)
+    part = jnp.concatenate([gain_ref[...], sums, jnp.zeros((PART - 3, T), F32)], axis=0)
     copies = []
     for d in range(BLK):
         copies.append(pltpu.make_async_copy(o_ref.at[lax.rem(zl_ref[0] + d, BLK)], o_refs[d], sems.at[d]))
@@ -427,19 +431,17 @@
         o_ref[i] = total
 
 
-def finish_kernel(factor, m_ref, a_ref, dt_ref, skip_ref, gain_ref):
-    outs = (a_ref, dt_ref, skip_ref)
-    rows = [[] for _ in outs]
+def finish_kernel(factor, m_ref, gain_ref, *head_refs):
+    heads = []
     for j in range(BLK):
         total = m_ref[j]
         for i in range(1, FAR // BLK):
             total = total + m_ref[i * BLK + j]
         total = total * factor
-        for n in range(len(outs)):
-            rows[n].append(total[n * HPD : (n + 1) * HPD, :])
-        gain_ref[2 * j : 2 * j + 2, :] = total[3 * HPD : 3 * HPD + 2, :]
-    for n, ref in enumerate(outs):
-        ref[...] = jnp.sum(jnp.concatenate(rows[n], axis=0).T, axis=0, keepdims=True)
+        gain_ref[2 * j : 2 * j + 2, :] = total[0:2, :]
+        heads.append(total[2:3, :])
+    for n, ref in enumerate(head_refs):
+        ref[...] = jnp.concatenate([v[:, n * HPD : (n + 1) * HPD] for v in heads], axis=1)
 
 
 def call(kernel, name, outs, in_specs=None, scratch=(), out_specs=None):
@@ -487,7 +489,7 @@
     def exchange(v, axes):
         return lax.all_to_all(v, axes, 0, 0)
 
-    group, segs = "zl", ("y", "zh")
+    group, segs = "zl", ("zh", "y")
 
     def shift(v, d):
         return lax.ppermute(v, group, [(i, (i + d) % BLK) for i in range(BLK)])
@@ -537,7 +539,7 @@
     *outs, part = call(
         input_kernel,
         "input_grad",
-        [(CPD, 128)] * BLK + [(NEAR, 4 * HPD, T)],
+        [(CPD, 128)] * BLK + [(NEAR, PART, T)],
         [sm] + [vm] * 9,
         [pltpu.VMEM((BLK, CPD, 128), F32), pltpu.SemaphoreType.DMA((BLK,))],
         [hbm] * BLK + [vm],
@@ -545,7 +547,7 @@
     outs = [shift(v, d) if d else v for d, v in enumerate(outs)]
     part = exchange(part, ("x", "core", "y"))
     early = [outs[d] for d in BACK]
-    part = call(sum_kernel, "near_sum", (FAR, 4 * HPD, T), [vm] + [hbm] * len(early))(part, *early)
+    part = call(sum_kernel, "near_sum", (FAR, PART, T), [vm] + [hbm] * len(early))(part, *early)
     hvp_input = call(
         place_kernel,
         "place",
@@ -555,14 +557,12 @@
         hbm,
     )(zl, *outs)
     factor = 1.0 / math.sqrt(T * NEAR * FAR)
-    hvp_a, hvp_dt, hvp_skip, hvp_gain = call(
-        functools.partial(finish_kernel, factor), "finish", [(1, HEADS)] * 3 + [(8, 128)]
-    )(exchange(part, ("zhi", "zh", "zl")))
+    hvp_gain, *heads = call(functools.partial(finish_kernel, factor), "finish", [(8, 128)] + [(1, HEADS)] * 3)(
+        exchange(part, ("zhi", "zh", "zl"))
+    )
     return (
         hvp_input,
-        hvp_a.reshape(HEADS),
-        hvp_dt.reshape(HEADS),
-        hvp_skip.reshape(HEADS),
+        *[v.reshape(HEADS) for v in heads],
         hvp_gain.reshape(CH),
     )
 

time: 194 us -> 193 us (level)
  blocking collectives: 51.8 us -> 64.9 us
  waiting for transfers between devices: 69.6 us -> 60.8 us
  starting transfers between devices: 53.6 us -> 49 us
    all_to_all x3 -> x4, blocking collectives: 51.8 us -> 64.9 us  [exchange(): return lax.all_to_all(v, axes, 0, 0)]
    ppermute x6, waiting for transfers between devices: 54.2 us -> 46.7 us  [shift(): return lax.ppermute(v, group, [(i, (i + d) % BLK) for i in range(BLK)])]
    all_to_all x5 -> x4, starting transfers between devices: 36 us -> 31.3 us  [exchange(): return lax.all_to_all(v, axes, 0, 0)]
    all_to_all x5 -> x4, waiting for transfers between devices: 15.3 us -> 14.2 us  [exchange(): return lax.all_to_all(v, axes, 0, 0)]
  transfers between devices with their start and end apart: 11 -> 10, of which waited for: 9 -> 7; matrix products, arithmetic and copies ran while one was open for 0% -> 0% of each run, Pallas kernels for 1% -> 1%
where the time goes in v4:
time: 193 us; the launch traced here: 192 us
  blocking collectives  64.9 us (34%)
  waiting for transfers between devices  60.8 us (32%)
  starting transfers between devices  49 us (25%)
  Pallas kernels  14.8 us (8%)
    all_to_all x4, blocking collectives, exchange(): return lax.all_to_all(v, axes, 0, 0)  64.9 us
    ppermute x6, waiting for transfers between devices, shift(): return lax.ppermute(v, group, [(i, (i + d) % BLK) for i in range(BLK)])  46.7 us
    all_to_all x4, starting transfers between devices, exchange(): return lax.all_to_all(v, axes, 0, 0)  31.3 us
    ppermute x6, starting transfers between devices, shift(): return lax.ppermute(v, group, [(i, (i + d) % BLK) for i in range(BLK)])  17.6 us
    pallas_call x11, Pallas kernels, run(): pl.pallas_call(kernel, name=name, out_shape=[shape(o) for o in outs] if m...  14.8 us
    all_to_all x4, waiting for transfers between devices, exchange(): return lax.all_to_all(v, axes, 0, 0)  14.2 us
  transfers between devices with their start and end apart: 10, of which 7 were waited for; matrix products, arithmetic and copies ran while one was open for 0% of the time, Pallas kernels for 1%

profile of v4, /device:TPU:1, one launch (start us, length us, event | category | flops | bytes accessed | tf_op | source)
XLA Modules:
  0.0 192.2 jit_solution(18251649781473994564)
XLA Ops:
  0.7 2.1 %pack_x.1 = f32[4,392,128]{2,1,0:T(8,128)} custom-call(bf16[128,1024]{1,0:T(8,128)(2,1)} %x_hbm.1, bf16[128,128]{1,0:T(8,128)(2,1)} %b_hbm.1, f32[16,128]{1,0:T(8,128)} %bitcast.18), custom_call_target="tpu_custom_call" | custom-call | tf_op jit(solution)/shard_map/pack_x/pallas_call | solution.py:455
  2.8 6.6 %all-to-all-start = ((f32[4,392,128]{2,1,0:T(8,128)}), f32[4,392,128]{2,1,0:T(8,128)S(1)}, u32[]{:S(2)}, u32[]{:S(2)}) async-start(f32[4,392,128]{2,1,0:T(8,128)} %pack_x.1), calls=%async_computation | async-start | bytes 1605632 | tf_op jit(solution)/shard_map/all_to_all | solution.py:490
  11.8 3.4 %collective-permute-start = (f32[640,128]{1,0:T(8,128)S(1)}, f32[640,128]{1,0:T(8,128)S(1)}, u32[]{:S(2)}, u32[]{:S(2)}) collective-permute-start(f32[640,128]{1,0:T(8,128)S(1)} %get-tuple-element.30), channel_id=1, source_target_pairs={{0,1},{1,2},{2,3},{3,0},{4,5},{5,6},{6,7},{7,4},{8,9},{9,10},{10,1... | collective-permute-start | bytes 983048 | tf_op jit(solution)/shard_map/ppermute | solution.py:495
  15.4 14.1 %collective-permute-done.rest_0_.g1 = f32[640,128]{1,0:T(8,128)S(1)} collective-permute-done((f32[640,128]{1,0:T(8,128)S(1)}, f32[640,128]{1,0:T(8,128)S(1)}, u32[]{:S(2)}, u32[]{:S(2)}) %collective-permute-start) | collective-permute-done | bytes 327712 | tf_op jit(solution)/shard_map/ppermute | solution.py:495
  29.5 5.4 %all-to-all-done.r_ref = f32[4,392,128]{2,1,0:T(8,128)S(1)} async-done(((f32[4,392,128]{2,1,0:T(8,128)}), f32[4,392,128]{2,1,0:T(8,128)S(1)}, u32[]{:S(2)}, u32[]{:S(2)}) %all-to-all-start) | async-done | bytes 802848 | tf_op jit(solution)/shard_map/all_to_all | solution.py:490
  36.5 12.3 %all-to-all-start.1 = ((f32[8,72,128]{2,1,0:T(8,128)}), f32[8,72,128]{2,1,0:T(8,128)S(1)}, u32[]{:S(2)}, u32[]{:S(2)}) async-start(f32[8,72,128]{2,1,0:T(8,128)} %get-tuple-element.33), calls=%async_computation.1 | async-start | bytes 589824 | tf_op jit(solution)/shard_map/all_to_all | solution.py:490
  48.8 1.9 collective-permute-start.1
  50.7 21.2 %collective-permute-done.1.rest_0_.g2 = f32[640,128]{1,0:T(8,128)S(1)} collective-permute-done((f32[640,128]{1,0:T(8,128)}, f32[640,128]{1,0:T(8,128)S(1)}, u32[]{:S(2)}, u32[]{:S(2)}) %collective-permute-start.1) | collective-permute-done | bytes 327712 | tf_op jit(solution)/shard_map/ppermute | solution.py:495
  72.7 3.8 %all-to-all-start.2 = ((f32[8,64,128]{2,1,0:T(8,128)}), f32[8,64,128]{2,1,0:T(8,128)S(1)}, u32[]{:S(2)}, u32[]{:S(2)}) async-start(f32[8,64,128]{2,1,0:T(8,128)} %scan_up.1), calls=%async_computation.2 | async-start | bytes 524288 | tf_op jit(solution)/shard_map/all_to_all | solution.py:490
  76.5 3.4 %collective-permute-start.2 = (f32[640,128]{1,0:T(8,128)S(1)}, f32[640,128]{1,0:T(8,128)}, u32[]{:S(2)}, u32[]{:S(2)}) collective-permute-start(f32[640,128]{1,0:T(8,128)S(1)} %get-tuple-element.32), channel_id=1, source_target_pairs={{0,3},{1,0},{2,1},{3,2},{4,7},{5,4},{6,5},{7,6},{8,11},{9,8},{10,9... | collective-permute-start | bytes 983048 | tf_op jit(solution)/shard_map/ppermute | solution.py:495
  79.8 5.8 %collective-permute-done.2.g3 = f32[640,128]{1,0:T(8,128)} collective-permute-done((f32[640,128]{1,0:T(8,128)S(1)}, f32[640,128]{1,0:T(8,128)}, u32[]{:S(2)}, u32[]{:S(2)}) %collective-permute-start.2) | collective-permute-done | bytes 327712 | tf_op jit(solution)/shard_map/ppermute | solution.py:495
  85.6 8.7 %all-to-all-done.2.h_ref = f32[8,64,128]{2,1,0:T(8,128)S(1)} async-done(((f32[8,64,128]{2,1,0:T(8,128)}), f32[8,64,128]{2,1,0:T(8,128)S(1)}, u32[]{:S(2)}, u32[]{:S(2)}) %all-to-all-start.2) | async-done | bytes 262176 | tf_op jit(solution)/shard_map/all_to_all | solution.py:490
  94.4 3.2 %mix.1 = (f32[4,640,128]{2,1,0:T(8,128)S(1)}, f32[2,4,256,128]{3,2,1,0:T(8,128)S(1)}, f32[4,2,256,128]{3,2,1,0:T(8,128)S(1)}, f32[4,16,128]{2,1,0:T(8,128)S(1)}) custom-call(s32[1]{0:T(128)} %bitcast.zl_ref, f32[8,128]{1,0:T(8,128)S(1)} %bitcast.14, f32[8,128]{1,0:T(8,128)S(1)} %bitcast.16, f32[4,392,128]{2,1,0:T(8,128)S(1)} %all-to-all-done.r_ref, ...), custom_call_target="tpu_custom_call" | custom-call | tf_op jit(solution)/shard_map/mix/pallas_call | solution.py:455
  97.6 7.3 %all_to_all.40.n_ref = f32[4,16,128]{2,1,0:T(8,128)S(1)} all-to-all(f32[4,16,128]{2,1,0:T(8,128)S(1)} %get-tuple-element.37), channel_id=1, replica_groups=mesh['zhi'=2,'x'=4,'core'=2,'y'=4,'zh'=2,'zl'=4] {'zl'}, dimensions={0} | all-to-all | bytes 65536 | tf_op jit(solution)/shard_map/all_to_all | solution.py:490
  105.9 26.7 %all_to_all.41.m_ref = f32[8,64,128]{2,1,0:T(8,128)S(1)} all-to-all(f32[8,64,128]{2,1,0:T(8,128)S(1)} %get-tuple-element.39), channel_id=1, replica_groups=mesh['zhi'=2,'x'=4,'core'=2,'y'=4,'zh'=2,'zl'=4] {'zh','y'}, dimensions={0} | all-to-all | bytes 524288 | tf_op jit(solution)/shard_map/all_to_all | solution.py:490
  132.6 17.6 %all_to_all.42.l_ref = f32[8,64,128]{2,1,0:T(8,128)S(1)} all-to-all(f32[8,64,128]{2,1,0:T(8,128)S(1)} %scan_down.1), channel_id=1, replica_groups=mesh['zhi'=2,'x'=4,'core'=2,'y'=4,'zh'=2,'zl'=4] {'zh','y'}, dimensions={0} | all-to-all | bytes 524288 | tf_op jit(solution)/shard_map/all_to_all | solution.py:490
  150.2 3.2 %input_grad.1 = (f32[256,128]{1,0:T(8,128)S(1)}, f32[256,128]{1,0:T(8,128)S(1)}, f32[256,128]{1,0:T(8,128)S(1)}, f32[256,128]{1,0:T(8,128)S(1)}, f32[32,8,128]{2,1,0:T(8,128)S(1)}) custom-call(s32[1]{0:T(128)} %bitcast.zl_ref, f32[4,392,128]{2,1,0:T(8,128)S(1)} %all-to-all-done.r_ref, f32[4,640,128]{2,1,0:T(8,128)S(1)} %get-tuple-element.36.g_ref, ...), custom_call_target="tpu_custom_call" | custom-call | tf_op jit(solution)/shard_map/input_grad/pallas_call | solution.py:455
  153.4 1.9 collective-permute-start.4
  155.3 13.3 %all_to_all.43.m_ref = f32[32,8,128]{2,1,0:T(8,128)S(1)} all-to-all(f32[32,8,128]{2,1,0:T(8,128)S(1)} %get-tuple-element.48), channel_id=1, replica_groups=mesh['zhi'=2,'x'=4,'core'=2,'y'=4,'zh'=2,'zl'=4] {'x','core','y'}, dimensions={0} | all-to-all | bytes 262144 | tf_op jit(solution)/shard_map/all_to_all | solution.py:490
  169.3 8.7 %all-to-all-start.7 = ((f32[16,8,128]{2,1,0:T(8,128)}), f32[16,8,128]{2,1,0:T(8,128)S(1)}, u32[]{:S(2)}, u32[]{:S(2)}) async-start(f32[16,8,128]{2,1,0:T(8,128)} %near_sum.1), calls=%async_computation.7 | async-start | bytes 131072 | tf_op jit(solution)/shard_map/all_to_all | solution.py:490
  178.0 3.3 %collective-permute-start.3 = (f32[256,128]{1,0:T(8,128)S(1)}, f32[256,128]{1,0:T(8,128)S(1)}, u32[]{:S(2)}, u32[]{:S(2)}) collective-permute-start(f32[256,128]{1,0:T(8,128)S(1)} %get-tuple-element.45), channel_id=1, source_target_pairs={{0,1},{1,2},{2,3},{3,0},{4,5},{5,6},{6,7},{7,4},{8,9},{9,10},{10,1... | collective-permute-start | bytes 393224 | tf_op jit(solution)/shard_map/ppermute | solution.py:495
  181.2 3.8 %collective-permute-start.5 = (f32[256,128]{1,0:T(8,128)S(1)}, f32[256,128]{1,0:T(8,128)S(1)}, u32[]{:S(2)}, u32[]{:S(2)}) collective-permute-start(f32[256,128]{1,0:T(8,128)S(1)} %get-tuple-element.47), channel_id=1, source_target_pairs={{0,3},{1,0},{2,1},{3,2},{4,7},{5,4},{6,5},{7,6},{8,11},{9,8},{10,9... | collective-permute-start | bytes 393224 | tf_op jit(solution)/shard_map/ppermute | solution.py:495
  185.1 2.4 %collective-permute-done.3.i1 = f32[256,128]{1,0:T(8,128)S(1)} collective-permute-done((f32[256,128]{1,0:T(8,128)S(1)}, f32[256,128]{1,0:T(8,128)S(1)}, u32[]{:S(2)}, u32[]{:S(2)}) %collective-permute-start.3) | collective-permute-done | bytes 131104 | tf_op jit(solution)/shard_map/ppermute | solution.py:495
  187.5 3.2 %collective-permute-done.5.i3 = f32[256,128]{1,0:T(8,128)S(1)} collective-permute-done((f32[256,128]{1,0:T(8,128)S(1)}, f32[256,128]{1,0:T(8,128)S(1)}, u32[]{:S(2)}, u32[]{:S(2)}) %collective-permute-start.5) | collective-permute-done | bytes 131104 | tf_op jit(solution)/shard_map/ppermute | solution.py:495
  (45 shorter events, 8.1 us)
Async XLA Ops:
  0.6 8.8 %copy-start.3 = (bf16[128,1024]{1,0:T(8,128)(2,1)S(1)}, bf16[128,1024]{1,0:T(8,128)(2,1)}, u32[]{:S(2)}) copy-start(bf16[128,1024]{1,0:T(8,128)(2,1)} %z_ref.1) | copy-start | bytes 786436
  0.6 8.8 %copy-start.4 = (bf16[128,1024]{1,0:T(8,128)(2,1)S(1)}, bf16[128,1024]{1,0:T(8,128)(2,1)}, u32[]{:S(2)}) copy-start(bf16[128,1024]{1,0:T(8,128)(2,1)} %cot_ref.1) | copy-start | bytes 786436
  0.7 8.8 %copy-start.5 = (bf16[128,128]{1,0:T(8,128)(2,1)S(1)}, bf16[128,128]{1,0:T(8,128)(2,1)}, u32[]{:S(2)}) copy-start(bf16[128,128]{1,0:T(8,128)(2,1)} %c_ref.1) | copy-start | bytes 98308
  2.7 12.4 %copy-start.9 = (f32[16]{0:T(128)S(1)}, f32[16]{0:T(128)}, u32[]{:S(2)}) copy-start(f32[16]{0:T(128)} %param.20) | copy-start | bytes 196
  2.8 12.4 %copy-start.10 = (f32[16]{0:T(128)S(1)}, f32[16]{0:T(128)}, u32[]{:S(2)}) copy-start(f32[16]{0:T(128)} %param.21) | copy-start | bytes 196
  2.8 12.4 %copy-start.11 = (f32[16]{0:T(128)S(1)}, f32[16]{0:T(128)}, u32[]{:S(2)}) copy-start(f32[16]{0:T(128)} %param.22) | copy-start | bytes 196
  2.8 12.4 %copy-start.12 = (f32[16]{0:T(128)S(1)}, f32[16]{0:T(128)}, u32[]{:S(2)}) copy-start(f32[16]{0:T(128)} %param.24) | copy-start | bytes 196
  2.8 12.4 %copy-start.13 = (f32[16]{0:T(128)S(1)}, f32[16]{0:T(128)}, u32[]{:S(2)}) copy-start(f32[16]{0:T(128)} %param.25) | copy-start | bytes 196
  2.8 12.4 %copy-start.14 = (f32[16]{0:T(128)S(1)}, f32[16]{0:T(128)}, u32[]{:S(2)}) copy-start(f32[16]{0:T(128)} %param.26) | copy-start | bytes 196
  2.8 32.1 %all-to-all-start = ((f32[4,392,128]{2,1,0:T(8,128)}), f32[4,392,128]{2,1,0:T(8,128)S(1)}, u32[]{:S(2)}, u32[]{:S(2)}) async-start(f32[4,392,128]{2,1,0:T(8,128)} %pack_x.1), calls=%async_computation | async-start | bytes 1605632 | tf_op jit(solution)/shard_map/all_to_all | solution.py:490
  10.3 0.7 copy-start.2
  11.8 17.7 %collective-permute-start = (f32[640,128]{1,0:T(8,128)S(1)}, f32[640,128]{1,0:T(8,128)S(1)}, u32[]{:S(2)}, u32[]{:S(2)}) collective-permute-start(f32[640,128]{1,0:T(8,128)S(1)} %get-tuple-element.30), channel_id=1, source_target_pairs={{0,1},{1,2},{2,3},{3,0},{4,5},{5,6},{6,7},{7,4},{8,9},{9,10},{10,1... | collective-permute-start | bytes 983048 | tf_op jit(solution)/shard_map/ppermute | solution.py:495
  29.4 43.2 %copy-start.1 = (f32[640,128]{1,0:T(8,128)}, f32[640,128]{1,0:T(8,128)S(1)}, u32[]{:S(2)}) copy-start(f32[640,128]{1,0:T(8,128)S(1)} %collective-permute-done.rest_0_.g1) | copy-start | bytes 983044
  34.9 59.4 %copy-start.6 = (f32[1024]{0:T(1024)S(1)}, f32[1024]{0:T(1024)}, u32[]{:S(2)}) copy-start(f32[1024]{0:T(1024)} %param.23) | copy-start | bytes 12292
  34.9 59.4 %copy-start.7 = (f32[1024]{0:T(1024)S(1)}, f32[1024]{0:T(1024)}, u32[]{:S(2)}) copy-start(f32[1024]{0:T(1024)} %param.27) | copy-start | bytes 12292
  36.5 35.5 %all-to-all-start.1 = ((f32[8,72,128]{2,1,0:T(8,128)}), f32[8,72,128]{2,1,0:T(8,128)S(1)}, u32[]{:S(2)}, u32[]{:S(2)}) async-start(f32[8,72,128]{2,1,0:T(8,128)} %get-tuple-element.33), calls=%async_computation.1 | async-start | bytes 589824 | tf_op jit(solution)/shard_map/all_to_all | solution.py:490
  48.8 23.1 %collective-permute-start.1 = (f32[640,128]{1,0:T(8,128)}, f32[640,128]{1,0:T(8,128)S(1)}, u32[]{:S(2)}, u32[]{:S(2)}) collective-permute-start(f32[640,128]{1,0:T(8,128)} %copy-done.8), channel_id=1, source_target_pairs={{0,2},{1,3},{2,0},{3,1},{4,6},{5,7},{6,4},{7,5},{8,10},{9,11},{10,... | collective-permute-start | bytes 983048 | tf_op jit(solution)/shard_map/ppermute | solution.py:495
  71.9 22.4 %copy-start = (f32[640,128]{1,0:T(8,128)}, f32[640,128]{1,0:T(8,128)S(1)}, u32[]{:S(2)}) copy-start(f32[640,128]{1,0:T(8,128)S(1)} %collective-permute-done.1.rest_0_.g2) | copy-start | bytes 983044
  72.7 21.7 %all-to-all-start.2 = ((f32[8,64,128]{2,1,0:T(8,128)}), f32[8,64,128]{2,1,0:T(8,128)S(1)}, u32[]{:S(2)}, u32[]{:S(2)}) async-start(f32[8,64,128]{2,1,0:T(8,128)} %scan_up.1), calls=%async_computation.2 | async-start | bytes 524288 | tf_op jit(solution)/shard_map/all_to_all | solution.py:490
  76.5 9.2 %collective-permute-start.2 = (f32[640,128]{1,0:T(8,128)S(1)}, f32[640,128]{1,0:T(8,128)}, u32[]{:S(2)}, u32[]{:S(2)}) collective-permute-start(f32[640,128]{1,0:T(8,128)S(1)} %get-tuple-element.32), channel_id=1, source_target_pairs={{0,3},{1,0},{2,1},{3,2},{4,7},{5,4},{6,5},{7,6},{8,11},{9,8},{10,9... | collective-permute-start | bytes 983048 | tf_op jit(solution)/shard_map/ppermute | solution.py:495
  153.4 15.2 %collective-permute-start.4 = (f32[256,128]{1,0:T(8,128)S(1)}, f32[256,128]{1,0:T(8,128)S(1)}, u32[]{:S(2)}, u32[]{:S(2)}) collective-permute-start(f32[256,128]{1,0:T(8,128)S(1)} %get-tuple-element.46), channel_id=1, source_target_pairs={{0,2},{1,3},{2,0},{3,1},{4,6},{5,7},{6,4},{7,5},{8,10},{9,11},{10,... | collective-permute-start | bytes 393224 | tf_op jit(solution)/shard_map/ppermute | solution.py:495
  169.3 22.3 %all-to-all-start.7 = ((f32[16,8,128]{2,1,0:T(8,128)}), f32[16,8,128]{2,1,0:T(8,128)S(1)}, u32[]{:S(2)}, u32[]{:S(2)}) async-start(f32[16,8,128]{2,1,0:T(8,128)} %near_sum.1), calls=%async_computation.7 | async-start | bytes 131072 | tf_op jit(solution)/shard_map/all_to_all | solution.py:490
  178.0 9.5 %collective-permute-start.3 = (f32[256,128]{1,0:T(8,128)S(1)}, f32[256,128]{1,0:T(8,128)S(1)}, u32[]{:S(2)}, u32[]{:S(2)}) collective-permute-start(f32[256,128]{1,0:T(8,128)S(1)} %get-tuple-element.45), channel_id=1, source_target_pairs={{0,1},{1,2},{2,3},{3,0},{4,5},{5,6},{6,7},{7,4},{8,9},{9,10},{10,1... | collective-permute-start | bytes 393224 | tf_op jit(solution)/shard_map/ppermute | solution.py:495
  181.2 9.5 %collective-permute-start.5 = (f32[256,128]{1,0:T(8,128)S(1)}, f32[256,128]{1,0:T(8,128)S(1)}, u32[]{:S(2)}, u32[]{:S(2)}) collective-permute-start(f32[256,128]{1,0:T(8,128)S(1)} %get-tuple-element.47), channel_id=1, source_target_pairs={{0,3},{1,0},{2,1},{3,2},{4,7},{5,4},{6,5},{7,6},{8,11},{9,8},{10,9... | collective-permute-start | bytes 393224 | tf_op jit(solution)/shard_map/ppermute | solution.py:495
  (1 other events, 0.7 us)

commit v5 on v4

--- a/solution.py
+++ b/solution.py
@@ -28,8 +28,8 @@
 FIRST = (1,)
 EARLY = (2,)
 BACK = (2,)
-X_ROWS = CPD + N + HPD + 4
-G_ROWS = 2 * CPD + T
+X_ROWS = CPD + N + T + HPD + 4
+G_ROWS = 2 * CPD
 M_ROWS = 2 * CPS + 8
 VMEM = 16 * 1024 * 1024
 
@@ -56,8 +56,8 @@
     )
 
 
-def pack_x_kernel(x_hbm, b_hbm, dt_hbm, o_ref, x_ref, b_ref, dt_ref, sems):
-    pairs = ((x_hbm, x_ref), (b_hbm, b_ref), (dt_hbm, dt_ref))
+def pack_x_kernel(x_hbm, b_hbm, dt_hbm, c_hbm, o_ref, x_ref, b_ref, dt_ref, c_ref, sems):
+    pairs = ((x_hbm, x_ref), (b_hbm, b_ref), (dt_hbm, dt_ref), (c_hbm, c_ref))
     copies = [pltpu.make_async_copy(src, dst, sems.at[n]) for n, (src, dst) in enumerate(pairs)]
     for copy in copies:
         copy.start()
@@ -68,13 +68,14 @@
             lo = j * CPD + i * 128
             o_ref[j, i * 128 : (i + 1) * 128, :] = x_ref[:, lo : lo + 128].astype(F32).T
         o_ref[j, CPD : CPD + N, :] = b_ref[...].astype(F32)
-        at = CPD + N
+        o_ref[j, CPD + N : CPD + N + T, :] = c_ref[...].astype(F32)
+        at = CPD + N + T
         o_ref[j, at : at + HPD, :] = dt_ref[j * HPD : (j + 1) * HPD, :]
         at += HPD
         o_ref[j, at:X_ROWS, :] = jnp.zeros((X_ROWS - at, T), F32)
 
 
-def pack_g_kernel(zl_ref, z_ref, cot_ref, c_ref, *rest):
+def pack_g_kernel(zl_ref, z_ref, cot_ref, *rest):
     o_refs, made, sems = rest[:BLK], rest[BLK : 2 * BLK], rest[2 * BLK]
     copies = [pltpu.make_async_copy(made[d], o_refs[d], sems.at[d]) for d in range(BLK)]
     for d in (*range(1, BLK), 0):
@@ -85,7 +86,6 @@
                 lo = pl.multiple_of(j * CPD + i * 128, 128)
                 at = n * CPD + i * 128
                 o_ref[at : at + 128, :] = ref[:, pl.ds(lo, 128)].astype(F32).T
-        o_ref[2 * CPD : 2 * CPD + T, :] = c_ref[...].astype(F32)
         copies[d].start()
     for copy in copies:
         copy.wait()
@@ -112,7 +112,7 @@
 
 def state_kernel(prm_ref, r_ref, *rest):
     table_ref, s_ref, msg_ref = rest[-3:]
-    at = CPD + N
+    at = CPD + N + T
     raw = jnp.concatenate([r_ref[b, at : at + HPD, :] for b in range(BLK)], axis=0)
 
     a_log, dt_bias, d_skip, p_a, p_dt, p_skip = [
@@ -235,7 +235,7 @@
         xt = r_ref[b, 0:CPD, :]
         xb = xt.astype(BF16)
         bmat = r_ref[b, CPD : CPD + N, :].astype(BF16)
-        cmat = g_ref[b, 2 * CPD : 2 * CPD + T, :].astype(BF16)
+        cmat = r_ref[b, CPD + N : CPD + N + T, :].astype(BF16)
         hb_ref[b, 0] = h
         hb_ref[b, 1] = dh
         got = mmt(jnp.concatenate(split(h) + split(dh), axis=0), cmat)
@@ -286,7 +286,7 @@
     d_adj = jnp.zeros((CPD, N), F32)
     for b in range(BLK - 1, -1, -1):
         xt = r_ref[b, 0:CPD, :]
-        cmat = g_ref[b, 2 * CPD : 2 * CPD + T, :].astype(BF16)
+        cmat = r_ref[b, CPD + N : CPD + N + T, :].astype(BF16)
         s = silu(g_ref[b, 0:CPD, :])
         cot = g_ref[b, CPD : 2 * CPD, :]
         u = (y_ref[0, b] + heads_rows(table_ref, K_D, b) * xt) * s
@@ -338,7 +338,7 @@
     acc_skip = [jnp.zeros((1, T), F32) for _ in range(HPD)]
     for b in range(BLK - 1, -1, -1):
         bmat = r_ref[b, CPD : CPD + N, :].astype(BF16)
-        cmat = g_ref[b, 2 * CPD : 2 * CPD + T, :].astype(BF16)
+        cmat = r_ref[b, CPD + N : CPD + N + T, :].astype(BF16)
         got = mmt(jnp.concatenate(split(adj) + split(d_adj), axis=0), bmat)
         bl = got[0:CPD] + got[CPD : 2 * CPD]
         dbl = got[2 * CPD : 3 * CPD] + got[3 * CPD :]
@@ -499,14 +499,14 @@
     params = lax.dynamic_slice_in_dim(params, lax.axis_index(group) * HPD, HPD, 1)
     params = jnp.broadcast_to(params.reshape(PARAMS * HPD, 1), (PARAMS * HPD, T))
     gain = (norm_gain.reshape(8, 128), probe_gain.reshape(8, 128))
-    packed = call(pack_x_kernel, "pack_x", (BLK, X_ROWS, T), [hbm] * 3,
-        [pltpu.VMEM((T, CH), BF16), pltpu.VMEM((T, N), BF16), pltpu.VMEM((HEADS, T), F32)]
-        + [pltpu.SemaphoreType.DMA((3,))],
-    )(*[in_hbm(v) for v in (ssm_input, b_proj, dt_raw.T)])
+    packed = call(pack_x_kernel, "pack_x", (BLK, X_ROWS, T), [hbm] * 4,
+        [pltpu.VMEM((T, CH), BF16), pltpu.VMEM((T, N), BF16), pltpu.VMEM((HEADS, T), F32), pltpu.VMEM((T, N), BF16)]
+        + [pltpu.SemaphoreType.DMA((4,))],
+    )(*[in_hbm(v) for v in (ssm_input, b_proj, dt_raw.T, c_proj)])
     r = exchange(packed, group)
-    parts = call(pack_g_kernel, "pack_g", [(G_ROWS, T)] * BLK, [sm] + [vm] * 3,
+    parts = call(pack_g_kernel, "pack_g", [(G_ROWS, T)] * BLK, [sm] + [vm] * 2,
         [pltpu.VMEM((G_ROWS, T), F32)] * BLK + [pltpu.SemaphoreType.DMA((BLK,))], [hbm] * BLK,
-    )(zl, gate_input, cotangent, c_proj)
+    )(zl, gate_input, cotangent)
     parts = [shift(v, d) if d else v for d, v in enumerate(parts)]
     table, s, msg = call(
         state_kernel,

time: 193 us -> 191 us (0.990)
  starting transfers between devices: 49 us -> 45.4 us
  waiting for transfers between devices: 60.8 us -> 63.7 us
    all_to_all x4, starting transfers between devices: 31.3 us -> 27.9 us  [exchange(): return lax.all_to_all(v, axes, 0, 0)]
    all_to_all x4, waiting for transfers between devices: 14.2 us -> 17.5 us  [exchange(): return lax.all_to_all(v, axes, 0, 0)]
where the time goes in v5:
time: 191 us; the launch traced here: 190 us
  blocking collectives  63.9 us (33%)
  waiting for transfers between devices  63.7 us (33%)
  starting transfers between devices  45.4 us (24%)
  Pallas kernels  14.4 us (8%)
    all_to_all x4, blocking collectives, exchange(): return lax.all_to_all(v, axes, 0, 0)  63.9 us
    ppermute x6, waiting for transfers between devices, shift(): return lax.ppermute(v, group, [(i, (i + d) % BLK) for i in range(BLK)])  46.1 us
    all_to_all x4, starting transfers between devices, exchange(): return lax.all_to_all(v, axes, 0, 0)  27.9 us
    ppermute x6, starting transfers between devices, shift(): return lax.ppermute(v, group, [(i, (i + d) % BLK) for i in range(BLK)])  17.6 us
    all_to_all x4, waiting for transfers between devices, exchange(): return lax.all_to_all(v, axes, 0, 0)  17.5 us
    pallas_call x11, Pallas kernels, run(): pl.pallas_call(kernel, name=name, out_shape=[shape(o) for o in outs] if m...  14.4 us
  transfers between devices with their start and end apart: 10, of which 7 were waited for; matrix products, arithmetic and copies ran while one was open for 0% of the time, Pallas kernels for 1%

profile of v5, /device:TPU:1, one launch (start us, length us, event | category | flops | bytes accessed | tf_op | source)
XLA Modules:
  0.0 190.0 jit_solution(12561597051128540874)
XLA Ops:
  0.6 2.1 %pack_x.1 = f32[4,520,128]{2,1,0:T(8,128)} custom-call(bf16[128,1024]{1,0:T(8,128)(2,1)} %x_hbm.1, bf16[128,128]{1,0:T(8,128)(2,1)} %b_hbm.1, f32[16,128]{1,0:T(8,128)} %bitcast.18, bf16[128,128]{1,0:T(8,128)(2,1)} %c_hbm.1), custom_call_target="tpu_custom_call" | custom-call | tf_op jit(solution)/shard_map/pack_x/pallas_call | solution.py:455
  2.9 6.6 %all-to-all-start = ((f32[4,520,128]{2,1,0:T(8,128)}), f32[4,520,128]{2,1,0:T(8,128)S(1)}, u32[]{:S(2)}, u32[]{:S(2)}) async-start(f32[4,520,128]{2,1,0:T(8,128)} %pack_x.1), calls=%async_computation | async-start | bytes 2129920 | tf_op jit(solution)/shard_map/all_to_all | solution.py:490
  11.4 3.4 %collective-permute-start = (f32[512,128]{1,0:T(8,128)S(1)}, f32[512,128]{1,0:T(8,128)S(1)}, u32[]{:S(2)}, u32[]{:S(2)}) collective-permute-start(f32[512,128]{1,0:T(8,128)S(1)} %get-tuple-element.30), channel_id=1, source_target_pairs={{0,1},{1,2},{2,3},{3,0},{4,5},{5,6},{6,7},{7,4},{8,9},{9,10},{10,1... | collective-permute-start | bytes 786440 | tf_op jit(solution)/shard_map/ppermute | solution.py:495
  15.0 17.2 %collective-permute-done.rest_0_.g1 = f32[512,128]{1,0:T(8,128)S(1)} collective-permute-done((f32[512,128]{1,0:T(8,128)S(1)}, f32[512,128]{1,0:T(8,128)S(1)}, u32[]{:S(2)}, u32[]{:S(2)}) %collective-permute-start) | collective-permute-done | bytes 262176 | tf_op jit(solution)/shard_map/ppermute | solution.py:495
  32.3 7.8 %all-to-all-done.r_ref = f32[4,520,128]{2,1,0:T(8,128)S(1)} async-done(((f32[4,520,128]{2,1,0:T(8,128)}), f32[4,520,128]{2,1,0:T(8,128)S(1)}, u32[]{:S(2)}, u32[]{:S(2)}) %all-to-all-start) | async-done | bytes 1064992 | tf_op jit(solution)/shard_map/all_to_all | solution.py:490
  41.7 11.5 %all-to-all-start.1 = ((f32[8,72,128]{2,1,0:T(8,128)}), f32[8,72,128]{2,1,0:T(8,128)S(1)}, u32[]{:S(2)}, u32[]{:S(2)}) async-start(f32[8,72,128]{2,1,0:T(8,128)} %get-tuple-element.33), calls=%async_computation.1 | async-start | bytes 589824 | tf_op jit(solution)/shard_map/all_to_all | solution.py:490
  53.2 1.9 %collective-permute-start.1 = (f32[512,128]{1,0:T(8,128)}, f32[512,128]{1,0:T(8,128)S(1)}, u32[]{:S(2)}, u32[]{:S(2)}) collective-permute-start(f32[512,128]{1,0:T(8,128)} %copy-done.7), channel_id=1, source_target_pairs={{0,2},{1,3},{2,0},{3,1},{4,6},{5,7},{6,4},{7,5},{8,10},{9,11},{10,... | collective-permute-start | bytes 786440 | tf_op jit(solution)/shard_map/ppermute | solution.py:495
  55.1 18.6 %collective-permute-done.1.rest_0_.g2 = f32[512,128]{1,0:T(8,128)S(1)} collective-permute-done((f32[512,128]{1,0:T(8,128)}, f32[512,128]{1,0:T(8,128)S(1)}, u32[]{:S(2)}, u32[]{:S(2)}) %collective-permute-start.1) | collective-permute-done | bytes 262176 | tf_op jit(solution)/shard_map/ppermute | solution.py:495
  74.5 4.0 %all-to-all-start.2 = ((f32[8,64,128]{2,1,0:T(8,128)}), f32[8,64,128]{2,1,0:T(8,128)S(1)}, u32[]{:S(2)}, u32[]{:S(2)}) async-start(f32[8,64,128]{2,1,0:T(8,128)} %scan_up.1), calls=%async_computation.2 | async-start | bytes 524288 | tf_op jit(solution)/shard_map/all_to_all | solution.py:490
  78.5 3.3 %collective-permute-start.2 = (f32[512,128]{1,0:T(8,128)S(1)}, f32[512,128]{1,0:T(8,128)}, u32[]{:S(2)}, u32[]{:S(2)}) collective-permute-start(f32[512,128]{1,0:T(8,128)S(1)} %get-tuple-element.32), channel_id=1, source_target_pairs={{0,3},{1,0},{2,1},{3,2},{4,7},{5,4},{6,5},{7,6},{8,11},{9,8},{10,9... | collective-permute-start | bytes 786440 | tf_op jit(solution)/shard_map/ppermute | solution.py:495
  81.8 4.7 %collective-permute-done.2.g3 = f32[512,128]{1,0:T(8,128)} collective-permute-done((f32[512,128]{1,0:T(8,128)S(1)}, f32[512,128]{1,0:T(8,128)}, u32[]{:S(2)}, u32[]{:S(2)}) %collective-permute-start.2) | collective-permute-done | bytes 262176 | tf_op jit(solution)/shard_map/ppermute | solution.py:495
  86.4 9.7 %all-to-all-done.2.h_ref = f32[8,64,128]{2,1,0:T(8,128)S(1)} async-done(((f32[8,64,128]{2,1,0:T(8,128)}), f32[8,64,128]{2,1,0:T(8,128)S(1)}, u32[]{:S(2)}, u32[]{:S(2)}) %all-to-all-start.2) | async-done | bytes 262176 | tf_op jit(solution)/shard_map/all_to_all | solution.py:490
  96.1 3.1 %mix.1 = (f32[4,512,128]{2,1,0:T(8,128)S(1)}, f32[2,4,256,128]{3,2,1,0:T(8,128)S(1)}, f32[4,2,256,128]{3,2,1,0:T(8,128)S(1)}, f32[4,16,128]{2,1,0:T(8,128)S(1)}) custom-call(s32[1]{0:T(128)} %bitcast.zl_ref, f32[8,128]{1,0:T(8,128)S(1)} %bitcast.14, f32[8,128]{1,0:T(8,128)S(1)} %bitcast.16, f32[4,520,128]{2,1,0:T(8,128)S(1)} %all-to-all-done.r_ref, ...), custom_call_target="tpu_custom_call" | custom-call | tf_op jit(solution)/shard_map/mix/pallas_call | solution.py:455
  99.3 6.9 %all_to_all.40.n_ref = f32[4,16,128]{2,1,0:T(8,128)S(1)} all-to-all(f32[4,16,128]{2,1,0:T(8,128)S(1)} %get-tuple-element.37), channel_id=1, replica_groups=mesh['zhi'=2,'x'=4,'core'=2,'y'=4,'zh'=2,'zl'=4] {'zl'}, dimensions={0} | all-to-all | bytes 65536 | tf_op jit(solution)/shard_map/all_to_all | solution.py:490
  107.1 26.1 %all_to_all.41.m_ref = f32[8,64,128]{2,1,0:T(8,128)S(1)} all-to-all(f32[8,64,128]{2,1,0:T(8,128)S(1)} %get-tuple-element.39), channel_id=1, replica_groups=mesh['zhi'=2,'x'=4,'core'=2,'y'=4,'zh'=2,'zl'=4] {'zh','y'}, dimensions={0} | all-to-all | bytes 524288 | tf_op jit(solution)/shard_map/all_to_all | solution.py:490
  133.3 17.6 %all_to_all.42.l_ref = f32[8,64,128]{2,1,0:T(8,128)S(1)} all-to-all(f32[8,64,128]{2,1,0:T(8,128)S(1)} %scan_down.1), channel_id=1, replica_groups=mesh['zhi'=2,'x'=4,'core'=2,'y'=4,'zh'=2,'zl'=4] {'zh','y'}, dimensions={0} | all-to-all | bytes 524288 | tf_op jit(solution)/shard_map/all_to_all | solution.py:490
  150.9 3.2 %input_grad.1 = (f32[256,128]{1,0:T(8,128)S(1)}, f32[256,128]{1,0:T(8,128)S(1)}, f32[256,128]{1,0:T(8,128)S(1)}, f32[256,128]{1,0:T(8,128)S(1)}, f32[32,8,128]{2,1,0:T(8,128)S(1)}) custom-call(s32[1]{0:T(128)} %bitcast.zl_ref, f32[4,520,128]{2,1,0:T(8,128)S(1)} %all-to-all-done.r_ref, f32[4,512,128]{2,1,0:T(8,128)S(1)} %get-tuple-element.36.g_ref, ...), custom_call_target="tpu_custom_call" | custom-call | tf_op jit(solution)/shard_map/input_grad/pallas_call | solution.py:455
  154.1 1.9 %collective-permute-start.4 = (f32[256,128]{1,0:T(8,128)S(1)}, f32[256,128]{1,0:T(8,128)S(1)}, u32[]{:S(2)}, u32[]{:S(2)}) collective-permute-start(f32[256,128]{1,0:T(8,128)S(1)} %get-tuple-element.46), channel_id=1, source_target_pairs={{0,2},{1,3},{2,0},{3,1},{4,6},{5,7},{6,4},{7,5},{8,10},{9,11},{10,... | collective-permute-start | bytes 393224 | tf_op jit(solution)/shard_map/ppermute | solution.py:495
  156.0 13.3 %all_to_all.43.m_ref = f32[32,8,128]{2,1,0:T(8,128)S(1)} all-to-all(f32[32,8,128]{2,1,0:T(8,128)S(1)} %get-tuple-element.48), channel_id=1, replica_groups=mesh['zhi'=2,'x'=4,'core'=2,'y'=4,'zh'=2,'zl'=4] {'x','core','y'}, dimensions={0} | all-to-all | bytes 262144 | tf_op jit(solution)/shard_map/all_to_all | solution.py:490
  170.0 5.8 %all-to-all-start.7 = ((f32[16,8,128]{2,1,0:T(8,128)}), f32[16,8,128]{2,1,0:T(8,128)S(1)}, u32[]{:S(2)}, u32[]{:S(2)}) async-start(f32[16,8,128]{2,1,0:T(8,128)} %near_sum.1), calls=%async_computation.7 | async-start | bytes 131072 | tf_op jit(solution)/shard_map/all_to_all | solution.py:490
  175.8 3.3 %collective-permute-start.3 = (f32[256,128]{1,0:T(8,128)S(1)}, f32[256,128]{1,0:T(8,128)S(1)}, u32[]{:S(2)}, u32[]{:S(2)}) collective-permute-start(f32[256,128]{1,0:T(8,128)S(1)} %get-tuple-element.45), channel_id=1, source_target_pairs={{0,1},{1,2},{2,3},{3,0},{4,5},{5,6},{6,7},{7,4},{8,9},{9,10},{10,1... | collective-permute-start | bytes 393224 | tf_op jit(solution)/shard_map/ppermute | solution.py:495
  179.1 3.8 %collective-permute-start.5 = (f32[256,128]{1,0:T(8,128)S(1)}, f32[256,128]{1,0:T(8,128)S(1)}, u32[]{:S(2)}, u32[]{:S(2)}) collective-permute-start(f32[256,128]{1,0:T(8,128)S(1)} %get-tuple-element.47), channel_id=1, source_target_pairs={{0,3},{1,0},{2,1},{3,2},{4,7},{5,4},{6,5},{7,6},{8,11},{9,8},{10,9... | collective-permute-start | bytes 393224 | tf_op jit(solution)/shard_map/ppermute | solution.py:495
  182.9 2.4 %collective-permute-done.3.i1 = f32[256,128]{1,0:T(8,128)S(1)} collective-permute-done((f32[256,128]{1,0:T(8,128)S(1)}, f32[256,128]{1,0:T(8,128)S(1)}, u32[]{:S(2)}, u32[]{:S(2)}) %collective-permute-start.3) | collective-permute-done | bytes 131104 | tf_op jit(solution)/shard_map/ppermute | solution.py:495
  185.4 3.2 %collective-permute-done.5.i3 = f32[256,128]{1,0:T(8,128)S(1)} collective-permute-done((f32[256,128]{1,0:T(8,128)S(1)}, f32[256,128]{1,0:T(8,128)S(1)}, u32[]{:S(2)}, u32[]{:S(2)}) %collective-permute-start.5) | collective-permute-done | bytes 131104 | tf_op jit(solution)/shard_map/ppermute | solution.py:495
  (43 shorter events, 7.7 us)
Async XLA Ops:
  2.8 6.7 %copy-start.2 = (bf16[128,1024]{1,0:T(8,128)(2,1)S(1)}, bf16[128,1024]{1,0:T(8,128)(2,1)}, u32[]{:S(2)}) copy-start(bf16[128,1024]{1,0:T(8,128)(2,1)} %z_ref.1) | copy-start | bytes 786436
  2.8 6.7 %copy-start.3 = (bf16[128,1024]{1,0:T(8,128)(2,1)S(1)}, bf16[128,1024]{1,0:T(8,128)(2,1)}, u32[]{:S(2)}) copy-start(bf16[128,1024]{1,0:T(8,128)(2,1)} %cot_ref.1) | copy-start | bytes 786436
  2.8 12.0 %copy-start.8 = (f32[16]{0:T(128)S(1)}, f32[16]{0:T(128)}, u32[]{:S(2)}) copy-start(f32[16]{0:T(128)} %param.20) | copy-start | bytes 196
  2.8 12.0 %copy-start.9 = (f32[16]{0:T(128)S(1)}, f32[16]{0:T(128)}, u32[]{:S(2)}) copy-start(f32[16]{0:T(128)} %param.21) | copy-start | bytes 196
  2.8 12.0 %copy-start.10 = (f32[16]{0:T(128)S(1)}, f32[16]{0:T(128)}, u32[]{:S(2)}) copy-start(f32[16]{0:T(128)} %param.22) | copy-start | bytes 196
  2.8 12.0 %copy-start.11 = (f32[16]{0:T(128)S(1)}, f32[16]{0:T(128)}, u32[]{:S(2)}) copy-start(f32[16]{0:T(128)} %param.24) | copy-start | bytes 196
  2.8 12.0 %copy-start.12 = (f32[16]{0:T(128)S(1)}, f32[16]{0:T(128)}, u32[]{:S(2)}) copy-start(f32[16]{0:T(128)} %param.25) | copy-start | bytes 196
  2.8 12.0 %copy-start.13 = (f32[16]{0:T(128)S(1)}, f32[16]{0:T(128)}, u32[]{:S(2)}) copy-start(f32[16]{0:T(128)} %param.26) | copy-start | bytes 196
  2.9 37.2 %all-to-all-start = ((f32[4,520,128]{2,1,0:T(8,128)}), f32[4,520,128]{2,1,0:T(8,128)S(1)}, u32[]{:S(2)}, u32[]{:S(2)}) async-start(f32[4,520,128]{2,1,0:T(8,128)} %pack_x.1), calls=%async_computation | async-start | bytes 2129920 | tf_op jit(solution)/shard_map/all_to_all | solution.py:490
  10.0 0.7 copy-start.4
  10.7 0.7 copy-start.7
  11.4 20.8 %collective-permute-start = (f32[512,128]{1,0:T(8,128)S(1)}, f32[512,128]{1,0:T(8,128)S(1)}, u32[]{:S(2)}, u32[]{:S(2)}) collective-permute-start(f32[512,128]{1,0:T(8,128)S(1)} %get-tuple-element.30), channel_id=1, source_target_pairs={{0,1},{1,2},{2,3},{3,0},{4,5},{5,6},{6,7},{7,4},{8,9},{9,10},{10,1... | collective-permute-start | bytes 786440 | tf_op jit(solution)/shard_map/ppermute | solution.py:495
  32.3 42.2 %copy-start.1 = (f32[512,128]{1,0:T(8,128)}, f32[512,128]{1,0:T(8,128)S(1)}, u32[]{:S(2)}) copy-start(f32[512,128]{1,0:T(8,128)S(1)} %collective-permute-done.rest_0_.g1) | copy-start | bytes 786436
  41.7 54.4 %copy-start.5 = (f32[1024]{0:T(1024)S(1)}, f32[1024]{0:T(1024)}, u32[]{:S(2)}) copy-start(f32[1024]{0:T(1024)} %param.23) | copy-start | bytes 12292
  41.7 54.5 %copy-start.6 = (f32[1024]{0:T(1024)S(1)}, f32[1024]{0:T(1024)}, u32[]{:S(2)}) copy-start(f32[1024]{0:T(1024)} %param.27) | copy-start | bytes 12292
  41.7 32.0 %all-to-all-start.1 = ((f32[8,72,128]{2,1,0:T(8,128)}), f32[8,72,128]{2,1,0:T(8,128)S(1)}, u32[]{:S(2)}, u32[]{:S(2)}) async-start(f32[8,72,128]{2,1,0:T(8,128)} %get-tuple-element.33), calls=%async_computation.1 | async-start | bytes 589824 | tf_op jit(solution)/shard_map/all_to_all | solution.py:490
  53.2 20.5 %collective-permute-start.1 = (f32[512,128]{1,0:T(8,128)}, f32[512,128]{1,0:T(8,128)S(1)}, u32[]{:S(2)}, u32[]{:S(2)}) collective-permute-start(f32[512,128]{1,0:T(8,128)} %copy-done.7), channel_id=1, source_target_pairs={{0,2},{1,3},{2,0},{3,1},{4,6},{5,7},{6,4},{7,5},{8,10},{9,11},{10,... | collective-permute-start | bytes 786440 | tf_op jit(solution)/shard_map/ppermute | solution.py:495
  73.7 22.4 %copy-start = (f32[512,128]{1,0:T(8,128)}, f32[512,128]{1,0:T(8,128)S(1)}, u32[]{:S(2)}) copy-start(f32[512,128]{1,0:T(8,128)S(1)} %collective-permute-done.1.rest_0_.g2) | copy-start | bytes 786436
  74.5 21.6 %all-to-all-start.2 = ((f32[8,64,128]{2,1,0:T(8,128)}), f32[8,64,128]{2,1,0:T(8,128)S(1)}, u32[]{:S(2)}, u32[]{:S(2)}) async-start(f32[8,64,128]{2,1,0:T(8,128)} %scan_up.1), calls=%async_computation.2 | async-start | bytes 524288 | tf_op jit(solution)/shard_map/all_to_all | solution.py:490
  78.5 7.9 %collective-permute-start.2 = (f32[512,128]{1,0:T(8,128)S(1)}, f32[512,128]{1,0:T(8,128)}, u32[]{:S(2)}, u32[]{:S(2)}) collective-permute-start(f32[512,128]{1,0:T(8,128)S(1)} %get-tuple-element.32), channel_id=1, source_target_pairs={{0,3},{1,0},{2,1},{3,2},{4,7},{5,4},{6,5},{7,6},{8,11},{9,8},{10,9... | collective-permute-start | bytes 786440 | tf_op jit(solution)/shard_map/ppermute | solution.py:495
  154.1 15.2 %collective-permute-start.4 = (f32[256,128]{1,0:T(8,128)S(1)}, f32[256,128]{1,0:T(8,128)S(1)}, u32[]{:S(2)}, u32[]{:S(2)}) collective-permute-start(f32[256,128]{1,0:T(8,128)S(1)} %get-tuple-element.46), channel_id=1, source_target_pairs={{0,2},{1,3},{2,0},{3,1},{4,6},{5,7},{6,4},{7,5},{8,10},{9,11},{10,... | collective-permute-start | bytes 393224 | tf_op jit(solution)/shard_map/ppermute | solution.py:495
  170.0 19.4 %all-to-all-start.7 = ((f32[16,8,128]{2,1,0:T(8,128)}), f32[16,8,128]{2,1,0:T(8,128)S(1)}, u32[]{:S(2)}, u32[]{:S(2)}) async-start(f32[16,8,128]{2,1,0:T(8,128)} %near_sum.1), calls=%async_computation.7 | async-start | bytes 131072 | tf_op jit(solution)/shard_map/all_to_all | solution.py:490
  175.8 9.5 %collective-permute-start.3 = (f32[256,128]{1,0:T(8,128)S(1)}, f32[256,128]{1,0:T(8,128)S(1)}, u32[]{:S(2)}, u32[]{:S(2)}) collective-permute-start(f32[256,128]{1,0:T(8,128)S(1)} %get-tuple-element.45), channel_id=1, source_target_pairs={{0,1},{1,2},{2,3},{3,0},{4,5},{5,6},{6,7},{7,4},{8,9},{9,10},{10,1... | collective-permute-start | bytes 393224 | tf_op jit(solution)/shard_map/ppermute | solution.py:495
  179.1 9.5 %collective-permute-start.5 = (f32[256,128]{1,0:T(8,128)S(1)}, f32[256,128]{1,0:T(8,128)S(1)}, u32[]{:S(2)}, u32[]{:S(2)}) collective-permute-start(f32[256,128]{1,0:T(8,128)S(1)} %get-tuple-element.47), channel_id=1, source_target_pairs={{0,3},{1,0},{2,1},{3,2},{4,7},{5,4},{6,5},{7,6},{8,11},{9,8},{10,9... | collective-permute-start | bytes 393224 | tf_op jit(solution)/shard_map/ppermute | solution.py:495

commit v6 on v5

--- a/solution.py
+++ b/solution.py
@@ -26,7 +26,7 @@
 NEAR = 32
 FAR = 16
 FIRST = (1,)
-EARLY = (2,)
+EARLY = (2, 3)
 BACK = (2,)
 X_ROWS = CPD + N + T + HPD + 4
 G_ROWS = 2 * CPD

time: 191 us -> 194 us (1.016)
  blocking collectives: 63.9 us -> 86.4 us
  waiting for transfers between devices: 63.7 us -> 47 us
  starting transfers between devices: 45.4 us -> 42.6 us
    all_to_all x4 -> x5, blocking collectives: 63.9 us -> 86.4 us  [exchange(): return lax.all_to_all(v, axes, 0, 0)]
    all_to_all x4 -> x3, waiting for transfers between devices: 17.5 us -> 7.82 us  [exchange(): return lax.all_to_all(v, axes, 0, 0)]
    ppermute x6, waiting for transfers between devices: 46.1 us -> 39.1 us  [shift(): return lax.ppermute(v, group, [(i, (i + d) % BLK) for i in range(BLK)])]
    all_to_all x4 -> x3, starting transfers between devices: 27.9 us -> 26.4 us  [exchange(): return lax.all_to_all(v, axes, 0, 0)]
  transfers between devices with their start and end apart: 10 -> 9, of which waited for: 7 -> 5; matrix products, arithmetic and copies ran while one was open for 0% -> 0% of each run, Pallas kernels for 1% -> 1%
where the time goes in v6:
time: 194 us; the launch traced here: 193 us
  blocking collectives  86.4 us (45%)
  waiting for transfers between devices  47 us (24%)
  starting transfers between devices  42.6 us (22%)
  Pallas kernels  14.1 us (7%)
    all_to_all x5, blocking collectives, exchange(): return lax.all_to_all(v, axes, 0, 0)  86.4 us
    ppermute x6, waiting for transfers between devices, shift(): return lax.ppermute(v, group, [(i, (i + d) % BLK) for i in range(BLK)])  39.1 us
    all_to_all x3, starting transfers between devices, exchange(): return lax.all_to_all(v, axes, 0, 0)  26.4 us
    ppermute x6, starting transfers between devices, shift(): return lax.ppermute(v, group, [(i, (i + d) % BLK) for i in range(BLK)])  16.2 us
    pallas_call x11, Pallas kernels, run(): pl.pallas_call(kernel, name=name, out_shape=[shape(o) for o in outs] if m...  14.1 us
    all_to_all x3, waiting for transfers between devices, exchange(): return lax.all_to_all(v, axes, 0, 0)  7.82 us
  transfers between devices with their start and end apart: 9, of which 5 were waited for; matrix products, arithmetic and copies ran while one was open for 0% of the time, Pallas kernels for 1%

profile of v6, /device:TPU:1, one launch (start us, length us, event | category | flops | bytes accessed | tf_op | source)
XLA Modules:
  0.0 192.8 jit_solution(18205879290449284872)
XLA Ops:
  0.6 2.1 %pack_x.1 = f32[4,520,128]{2,1,0:T(8,128)} custom-call(bf16[128,1024]{1,0:T(8,128)(2,1)} %x_hbm.1, bf16[128,128]{1,0:T(8,128)(2,1)} %b_hbm.1, f32[16,128]{1,0:T(8,128)} %bitcast.18, bf16[128,128]{1,0:T(8,128)(2,1)} %c_hbm.1), custom_call_target="tpu_custom_call" | custom-call | tf_op jit(solution)/shard_map/pack_x/pallas_call | solution.py:455
  2.9 6.6 %all-to-all-start = ((f32[4,520,128]{2,1,0:T(8,128)}), f32[4,520,128]{2,1,0:T(8,128)S(1)}, u32[]{:S(2)}, u32[]{:S(2)}) async-start(f32[4,520,128]{2,1,0:T(8,128)} %pack_x.1), calls=%async_computation | async-start | bytes 2129920 | tf_op jit(solution)/shard_map/all_to_all | solution.py:490
  11.9 3.4 %collective-permute-start = (f32[512,128]{1,0:T(8,128)S(1)}, f32[512,128]{1,0:T(8,128)S(1)}, u32[]{:S(2)}, u32[]{:S(2)}) collective-permute-start(f32[512,128]{1,0:T(8,128)S(1)} %get-tuple-element.30), channel_id=1, source_target_pairs={{0,1},{1,2},{2,3},{3,0},{4,5},{5,6},{6,7},{7,4},{8,9},{9,10},{10,1... | collective-permute-start | bytes 786440 | tf_op jit(solution)/shard_map/ppermute | solution.py:495
  15.5 16.8 %collective-permute-done.rest_0_.g1 = f32[512,128]{1,0:T(8,128)S(1)} collective-permute-done((f32[512,128]{1,0:T(8,128)S(1)}, f32[512,128]{1,0:T(8,128)S(1)}, u32[]{:S(2)}, u32[]{:S(2)}) %collective-permute-start) | collective-permute-done | bytes 262176 | tf_op jit(solution)/shard_map/ppermute | solution.py:495
  32.3 7.8 %all-to-all-done.r_ref = f32[4,520,128]{2,1,0:T(8,128)S(1)} async-done(((f32[4,520,128]{2,1,0:T(8,128)}), f32[4,520,128]{2,1,0:T(8,128)S(1)}, u32[]{:S(2)}, u32[]{:S(2)}) %all-to-all-start) | async-done | bytes 1064992 | tf_op jit(solution)/shard_map/all_to_all | solution.py:490
  40.2 1.5 state.1
  41.7 11.5 %all-to-all-start.1 = ((f32[8,72,128]{2,1,0:T(8,128)}), f32[8,72,128]{2,1,0:T(8,128)S(1)}, u32[]{:S(2)}, u32[]{:S(2)}) async-start(f32[8,72,128]{2,1,0:T(8,128)} %get-tuple-element.33), calls=%async_computation.1 | async-start | bytes 589824 | tf_op jit(solution)/shard_map/all_to_all | solution.py:490
  53.2 1.9 collective-permute-start.1
  55.1 1.9 %collective-permute-start.2 = (f32[512,128]{1,0:T(8,128)}, f32[512,128]{1,0:T(8,128)S(1)}, u32[]{:S(2)}, u32[]{:S(2)}) collective-permute-start(f32[512,128]{1,0:T(8,128)} %copy-done.8), channel_id=1, source_target_pairs={{0,3},{1,0},{2,1},{3,2},{4,7},{5,4},{6,5},{7,6},{8,11},{9,8},{10,9... | collective-permute-start | bytes 786440 | tf_op jit(solution)/shard_map/ppermute | solution.py:495
  57.0 16.7 %collective-permute-done.1.rest_0_.g2 = f32[512,128]{1,0:T(8,128)S(1)} collective-permute-done((f32[512,128]{1,0:T(8,128)}, f32[512,128]{1,0:T(8,128)S(1)}, u32[]{:S(2)}, u32[]{:S(2)}) %collective-permute-start.1) | collective-permute-done | bytes 262176 | tf_op jit(solution)/shard_map/ppermute | solution.py:495
  73.8 15.1 %all_to_all.40.h_ref = f32[8,64,128]{2,1,0:T(8,128)S(1)} all-to-all(f32[8,64,128]{2,1,0:T(8,128)S(1)} %scan_up.1), channel_id=1, replica_groups=mesh['zhi'=2,'x'=4,'core'=2,'y'=4,'zh'=2,'zl'=4] {'zh','y'}, dimensions={0} | all-to-all | bytes 524288 | tf_op jit(solution)/shard_map/all_to_all | solution.py:490
  88.9 3.1 %mix.1 = (f32[4,512,128]{2,1,0:T(8,128)S(1)}, f32[2,4,256,128]{3,2,1,0:T(8,128)S(1)}, f32[4,2,256,128]{3,2,1,0:T(8,128)S(1)}, f32[4,16,128]{2,1,0:T(8,128)S(1)}) custom-call(s32[1]{0:T(128)} %bitcast.zl_ref, f32[8,128]{1,0:T(8,128)S(1)} %bitcast.14, f32[8,128]{1,0:T(8,128)S(1)} %bitcast.16, f32[4,520,128]{2,1,0:T(8,128)S(1)} %all-to-all-done.r_ref, ...), custom_call_target="tpu_custom_call" | custom-call | tf_op jit(solution)/shard_map/mix/pallas_call | solution.py:455
  92.1 14.9 %all_to_all.41.n_ref = f32[4,16,128]{2,1,0:T(8,128)S(1)} all-to-all(f32[4,16,128]{2,1,0:T(8,128)S(1)} %get-tuple-element.37), channel_id=1, replica_groups=mesh['zhi'=2,'x'=4,'core'=2,'y'=4,'zh'=2,'zl'=4] {'zl'}, dimensions={0} | all-to-all | bytes 65536 | tf_op jit(solution)/shard_map/all_to_all | solution.py:490
  107.0 1.0 seeds.1
  108.0 24.4 %all_to_all.42.m_ref = f32[8,64,128]{2,1,0:T(8,128)S(1)} all-to-all(f32[8,64,128]{2,1,0:T(8,128)S(1)} %get-tuple-element.39), channel_id=1, replica_groups=mesh['zhi'=2,'x'=4,'core'=2,'y'=4,'zh'=2,'zl'=4] {'zh','y'}, dimensions={0} | all-to-all | bytes 524288 | tf_op jit(solution)/shard_map/all_to_all | solution.py:490
  132.4 18.7 %all_to_all.43.l_ref = f32[8,64,128]{2,1,0:T(8,128)S(1)} all-to-all(f32[8,64,128]{2,1,0:T(8,128)S(1)} %scan_down.1), channel_id=1, replica_groups=mesh['zhi'=2,'x'=4,'core'=2,'y'=4,'zh'=2,'zl'=4] {'zh','y'}, dimensions={0} | all-to-all | bytes 524288 | tf_op jit(solution)/shard_map/all_to_all | solution.py:490
  151.1 3.2 %input_grad.1 = (f32[256,128]{1,0:T(8,128)S(1)}, f32[256,128]{1,0:T(8,128)S(1)}, f32[256,128]{1,0:T(8,128)S(1)}, f32[256,128]{1,0:T(8,128)S(1)}, f32[32,8,128]{2,1,0:T(8,128)S(1)}) custom-call(s32[1]{0:T(128)} %bitcast.zl_ref, f32[4,520,128]{2,1,0:T(8,128)S(1)} %all-to-all-done.r_ref, f32[4,512,128]{2,1,0:T(8,128)S(1)} %get-tuple-element.36.g_ref, ...), custom_call_target="tpu_custom_call" | custom-call | tf_op jit(solution)/shard_map/input_grad/pallas_call | solution.py:455
  154.3 1.9 collective-permute-start.4
  156.2 13.3 %all_to_all.44.m_ref = f32[32,8,128]{2,1,0:T(8,128)S(1)} all-to-all(f32[32,8,128]{2,1,0:T(8,128)S(1)} %get-tuple-element.48), channel_id=1, replica_groups=mesh['zhi'=2,'x'=4,'core'=2,'y'=4,'zh'=2,'zl'=4] {'x','core','y'}, dimensions={0} | all-to-all | bytes 262144 | tf_op jit(solution)/shard_map/all_to_all | solution.py:490
  170.2 8.3 %all-to-all-start.7 = ((f32[16,8,128]{2,1,0:T(8,128)}), f32[16,8,128]{2,1,0:T(8,128)S(1)}, u32[]{:S(2)}, u32[]{:S(2)}) async-start(f32[16,8,128]{2,1,0:T(8,128)} %near_sum.1), calls=%async_computation.7 | async-start | bytes 131072 | tf_op jit(solution)/shard_map/all_to_all | solution.py:490
  178.6 3.3 %collective-permute-start.3 = (f32[256,128]{1,0:T(8,128)S(1)}, f32[256,128]{1,0:T(8,128)S(1)}, u32[]{:S(2)}, u32[]{:S(2)}) collective-permute-start(f32[256,128]{1,0:T(8,128)S(1)} %get-tuple-element.45), channel_id=1, source_target_pairs={{0,1},{1,2},{2,3},{3,0},{4,5},{5,6},{6,7},{7,4},{8,9},{9,10},{10,1... | collective-permute-start | bytes 393224 | tf_op jit(solution)/shard_map/ppermute | solution.py:495
  181.8 3.8 %collective-permute-start.5 = (f32[256,128]{1,0:T(8,128)S(1)}, f32[256,128]{1,0:T(8,128)S(1)}, u32[]{:S(2)}, u32[]{:S(2)}) collective-permute-start(f32[256,128]{1,0:T(8,128)S(1)} %get-tuple-element.47), channel_id=1, source_target_pairs={{0,3},{1,0},{2,1},{3,2},{4,7},{5,4},{6,5},{7,6},{8,11},{9,8},{10,9... | collective-permute-start | bytes 393224 | tf_op jit(solution)/shard_map/ppermute | solution.py:495
  185.6 2.4 %collective-permute-done.3.i1 = f32[256,128]{1,0:T(8,128)S(1)} collective-permute-done((f32[256,128]{1,0:T(8,128)S(1)}, f32[256,128]{1,0:T(8,128)S(1)}, u32[]{:S(2)}, u32[]{:S(2)}) %collective-permute-start.3) | collective-permute-done | bytes 131104 | tf_op jit(solution)/shard_map/ppermute | solution.py:495
  188.1 3.2 %collective-permute-done.5.i3 = f32[256,128]{1,0:T(8,128)S(1)} collective-permute-done((f32[256,128]{1,0:T(8,128)S(1)}, f32[256,128]{1,0:T(8,128)S(1)}, u32[]{:S(2)}, u32[]{:S(2)}) %collective-permute-start.5) | collective-permute-done | bytes 131104 | tf_op jit(solution)/shard_map/ppermute | solution.py:495
  (44 shorter events, 4.9 us)
Async XLA Ops:
  2.8 6.7 %copy-start.3 = (bf16[128,1024]{1,0:T(8,128)(2,1)S(1)}, bf16[128,1024]{1,0:T(8,128)(2,1)}, u32[]{:S(2)}) copy-start(bf16[128,1024]{1,0:T(8,128)(2,1)} %z_ref.1) | copy-start | bytes 786436
  2.8 6.7 %copy-start.4 = (bf16[128,1024]{1,0:T(8,128)(2,1)S(1)}, bf16[128,1024]{1,0:T(8,128)(2,1)}, u32[]{:S(2)}) copy-start(bf16[128,1024]{1,0:T(8,128)(2,1)} %cot_ref.1) | copy-start | bytes 786436
  2.8 12.5 %copy-start.9 = (f32[16]{0:T(128)S(1)}, f32[16]{0:T(128)}, u32[]{:S(2)}) copy-start(f32[16]{0:T(128)} %param.20) | copy-start | bytes 196
  2.8 12.5 %copy-start.10 = (f32[16]{0:T(128)S(1)}, f32[16]{0:T(128)}, u32[]{:S(2)}) copy-start(f32[16]{0:T(128)} %param.21) | copy-start | bytes 196
  2.8 12.5 %copy-start.11 = (f32[16]{0:T(128)S(1)}, f32[16]{0:T(128)}, u32[]{:S(2)}) copy-start(f32[16]{0:T(128)} %param.22) | copy-start | bytes 196
  2.8 12.5 %copy-start.12 = (f32[16]{0:T(128)S(1)}, f32[16]{0:T(128)}, u32[]{:S(2)}) copy-start(f32[16]{0:T(128)} %param.24) | copy-start | bytes 196
  2.8 12.4 %copy-start.13 = (f32[16]{0:T(128)S(1)}, f32[16]{0:T(128)}, u32[]{:S(2)}) copy-start(f32[16]{0:T(128)} %param.25) | copy-start | bytes 196
  2.8 12.4 %copy-start.14 = (f32[16]{0:T(128)S(1)}, f32[16]{0:T(128)}, u32[]{:S(2)}) copy-start(f32[16]{0:T(128)} %param.26) | copy-start | bytes 196
  2.9 37.2 %all-to-all-start = ((f32[4,520,128]{2,1,0:T(8,128)}), f32[4,520,128]{2,1,0:T(8,128)S(1)}, u32[]{:S(2)}, u32[]{:S(2)}) async-start(f32[4,520,128]{2,1,0:T(8,128)} %pack_x.1), calls=%async_computation | async-start | bytes 2129920 | tf_op jit(solution)/shard_map/all_to_all | solution.py:490
  10.5 0.7 copy-start.5
  11.2 0.7 copy-start.8
  11.9 20.4 %collective-permute-start = (f32[512,128]{1,0:T(8,128)S(1)}, f32[512,128]{1,0:T(8,128)S(1)}, u32[]{:S(2)}, u32[]{:S(2)}) collective-permute-start(f32[512,128]{1,0:T(8,128)S(1)} %get-tuple-element.30), channel_id=1, source_target_pairs={{0,1},{1,2},{2,3},{3,0},{4,5},{5,6},{6,7},{7,4},{8,9},{9,10},{10,1... | collective-permute-start | bytes 786440 | tf_op jit(solution)/shard_map/ppermute | solution.py:495
  32.3 41.5 %copy-start = (f32[512,128]{1,0:T(8,128)}, f32[512,128]{1,0:T(8,128)S(1)}, u32[]{:S(2)}) copy-start(f32[512,128]{1,0:T(8,128)S(1)} %collective-permute-done.rest_0_.g1) | copy-start | bytes 786436
  41.7 47.3 %copy-start.6 = (f32[1024]{0:T(1024)S(1)}, f32[1024]{0:T(1024)}, u32[]{:S(2)}) copy-start(f32[1024]{0:T(1024)} %param.23) | copy-start | bytes 12292
  41.7 47.3 %copy-start.7 = (f32[1024]{0:T(1024)S(1)}, f32[1024]{0:T(1024)}, u32[]{:S(2)}) copy-start(f32[1024]{0:T(1024)} %param.27) | copy-start | bytes 12292
  41.7 32.1 %all-to-all-start.1 = ((f32[8,72,128]{2,1,0:T(8,128)}), f32[8,72,128]{2,1,0:T(8,128)S(1)}, u32[]{:S(2)}, u32[]{:S(2)}) async-start(f32[8,72,128]{2,1,0:T(8,128)} %get-tuple-element.33), calls=%async_computation.1 | async-start | bytes 589824 | tf_op jit(solution)/shard_map/all_to_all | solution.py:490
  53.2 20.5 %collective-permute-start.1 = (f32[512,128]{1,0:T(8,128)}, f32[512,128]{1,0:T(8,128)S(1)}, u32[]{:S(2)}, u32[]{:S(2)}) collective-permute-start(f32[512,128]{1,0:T(8,128)} %get-tuple-element.31), channel_id=1, source_target_pairs={{0,2},{1,3},{2,0},{3,1},{4,6},{5,7},{6,4},{7,5},{8,10},{9,11},{10,... | collective-permute-start | bytes 786440 | tf_op jit(solution)/shard_map/ppermute | solution.py:495
  55.1 18.6 %collective-permute-start.2 = (f32[512,128]{1,0:T(8,128)}, f32[512,128]{1,0:T(8,128)S(1)}, u32[]{:S(2)}, u32[]{:S(2)}) collective-permute-start(f32[512,128]{1,0:T(8,128)} %copy-done.8), channel_id=1, source_target_pairs={{0,3},{1,0},{2,1},{3,2},{4,7},{5,4},{6,5},{7,6},{8,11},{9,8},{10,9... | collective-permute-start | bytes 786440 | tf_op jit(solution)/shard_map/ppermute | solution.py:495
  73.7 15.2 %copy-start.1 = (f32[512,128]{1,0:T(8,128)}, f32[512,128]{1,0:T(8,128)S(1)}, u32[]{:S(2)}) copy-start(f32[512,128]{1,0:T(8,128)S(1)} %collective-permute-done.1.rest_0_.g2) | copy-start | bytes 786436
  73.7 15.2 %copy-start.2 = (f32[512,128]{1,0:T(8,128)}, f32[512,128]{1,0:T(8,128)S(1)}, u32[]{:S(2)}) copy-start(f32[512,128]{1,0:T(8,128)S(1)} %collective-permute-done.2.rest_1_.g3) | copy-start | bytes 786436
  154.3 15.3 %collective-permute-start.4 = (f32[256,128]{1,0:T(8,128)S(1)}, f32[256,128]{1,0:T(8,128)S(1)}, u32[]{:S(2)}, u32[]{:S(2)}) collective-permute-start(f32[256,128]{1,0:T(8,128)S(1)} %get-tuple-element.46), channel_id=1, source_target_pairs={{0,2},{1,3},{2,0},{3,1},{4,6},{5,7},{6,4},{7,5},{8,10},{9,11},{10,... | collective-permute-start | bytes 393224 | tf_op jit(solution)/shard_map/ppermute | solution.py:495
  170.2 21.9 %all-to-all-start.7 = ((f32[16,8,128]{2,1,0:T(8,128)}), f32[16,8,128]{2,1,0:T(8,128)S(1)}, u32[]{:S(2)}, u32[]{:S(2)}) async-start(f32[16,8,128]{2,1,0:T(8,128)} %near_sum.1), calls=%async_computation.7 | async-start | bytes 131072 | tf_op jit(solution)/shard_map/all_to_all | solution.py:490
  178.6 9.5 %collective-permute-start.3 = (f32[256,128]{1,0:T(8,128)S(1)}, f32[256,128]{1,0:T(8,128)S(1)}, u32[]{:S(2)}, u32[]{:S(2)}) collective-permute-start(f32[256,128]{1,0:T(8,128)S(1)} %get-tuple-element.45), channel_id=1, source_target_pairs={{0,1},{1,2},{2,3},{3,0},{4,5},{5,6},{6,7},{7,4},{8,9},{9,10},{10,1... | collective-permute-start | bytes 393224 | tf_op jit(solution)/shard_map/ppermute | solution.py:495
  181.8 9.5 %collective-permute-start.5 = (f32[256,128]{1,0:T(8,128)S(1)}, f32[256,128]{1,0:T(8,128)S(1)}, u32[]{:S(2)}, u32[]{:S(2)}) collective-permute-start(f32[256,128]{1,0:T(8,128)S(1)} %get-tuple-element.47), channel_id=1, source_target_pairs={{0,3},{1,0},{2,1},{3,2},{4,7},{5,4},{6,5},{7,6},{8,11},{9,8},{10,9... | collective-permute-start | bytes 393224 | tf_op jit(solution)/shard_map/ppermute | solution.py:495
